TPU v7x, 128 devices: a whole 4x4x4 slice. The times are simulated.
128 devices in a mesh: row: 8 (over z, core), col: 16 (over x, y).
Axes of the slice: x: 4, y: 4, z: 4, core: 2. Of those that a mesh axis runs over, the one named last changes fastest.
Arguments:
- normed: bfloat16 [1024, 8192], P('col', 'row'), may hold values from -16 to 16, as said below
- w_qkv: bfloat16 [3, 8192, 8192], P(None, 'row', 'col'), as said below
- w_out: bfloat16 [8192, 8192], P('col', 'row'), may hold values from -0.0625 to 0.0625
- doc_start: int32 [8], replicated, may hold values from 0 to 896, as said below
- grad_y: bfloat16 [1024, 8192], P('col', 'row'), may hold values from -6 to 6
Outputs:
- layer_out: bfloat16 [1024, 8192], P('col', 'row')
- grad_x: bfloat16 [1024, 8192], P('col', 'row')
- grad_qkv: float32 [3, 8192, 8192], P(None, 'row', 'col')
- grad_out: float32 [8192, 8192], P('col', 'row')
Inputs may be any that keep to these rules, and one draw needn't show every extreme that they name: doc_start[b] is a multiple of 128, at most b * 128, never falling, and equal either to b * 128 (block b opens a document) or to doc_start[b - 1]; doc_start[0] = 0 and the last block opens a document. `normed`: activations of order one. `w_qkv`: entries of standard deviation about 1 / sqrt(8192).
All inputs are finite; a program needn't handle non-finite values.
Results may differ from a plain program's by a relative error of at most 0.034.
Values may be sent and summed in bfloat16 or wider, within the bound.
No kernel may reach another device: no remote copies, remote signals or barrier semaphores. Data moves between devices by JAX's collectives and lax.ppermute only.
A program may use at most 128 MiB of HBM per device.

v0:
```python
import math

import jax
import jax.numpy as jnp
from jax import lax
from jax.experimental import pallas as pl
from jax.experimental.pallas import tpu as pltpu
from jax.sharding import PartitionSpec as P

HD = 128
BLOCK = 128
NEG = -1e30
F32 = jnp.float32
BF16 = jnp.bfloat16
NT = (((1,), (1,)), ((), ()))
TN = (((0,), (0,)), ((), ()))
MIB = 1024 * 1024

RING = 4
CORES = 2
QKV = 3


def to_x(value, step):
    pairs = [(c, (c // RING + step) % RING * RING + c % RING) for c in range(RING * RING)]
    return lax.ppermute(value, "col", pairs)


def to_y(value, step):
    pairs = [(c, c // RING * RING + (c % RING + step) % RING) for c in range(RING * RING)]
    return lax.ppermute(value, "col", pairs)


def to_z(value, step):
    pairs = [(r, (r // CORES + step) % RING * CORES + r % CORES) for r in range(RING * CORES)]
    return lax.ppermute(value, "row", pairs)


def swap_cores(value):
    pairs = [(r, r // CORES * CORES + 1 - r % CORES) for r in range(RING * CORES)]
    return lax.ppermute(value, "row", pairs)


def tied(values, others):
    out = lax.optimization_barrier((tuple(values), tuple(others)))
    return list(out[0])


def mm(a, b):
    return jnp.dot(a, b, preferred_element_type=F32)


def whole(array):
    return pl.BlockSpec(array.shape, lambda i, s: (0,) * array.ndim)


def shape_of(array_shape, dtype):
    return jax.ShapeDtypeStruct(array_shape, dtype)


def call(
    kernel,
    scalar,
    inputs,
    in_specs,
    out_shape,
    out_specs,
    grid=1,
    flops=0,
    moved=0,
    scratch=(),
    limit=16,
):
    return pl.pallas_call(
        kernel,
        grid_spec=pltpu.PrefetchScalarGridSpec(
            num_scalar_prefetch=1,
            grid=(grid,),
            in_specs=in_specs,
            out_specs=out_specs,
            scratch_shapes=list(scratch),
        ),
        out_shape=out_shape,
        compiler_params=pltpu.CompilerParams(vmem_limit_bytes=limit * MIB),
        cost_estimate=pl.CostEstimate(flops=flops, bytes_accessed=moved, transcendentals=0),
    )(scalar, *inputs)


def turn_weights(z_arg, w_qkv):
    count, depth, width = w_qkv.shape

    def kernel(z_ref, w_ref, out_ref):
        for which in range(count):
            out_ref[which * HD : (which + 1) * HD, :] = w_ref[which].T

    return call(
        kernel,
        z_arg,
        [w_qkv],
        [pl.BlockSpec((count, depth, HD), lambda d, z: (0, 0, (z[0] + d) % RING))],
        shape_of((count * width, depth), BF16),
        pl.BlockSpec((count * HD, depth), lambda d, z: (d, 0)),
        grid=RING,
        moved=4 * count * depth * width,
    )


def stack_blocks(core_arg, blocks):
    rows, width = blocks[0].shape
    half = rows // 2

    def kernel(core_ref, *refs):
        out_ref = refs[RING]
        for side in range(2):
            start = pl.multiple_of((core_ref[0] ^ side) * half, half)
            for i in range(RING):
                place = (side * RING + i) * half
                out_ref[place : place + half, :] = refs[i][pl.ds(start, half), :]

    out = shape_of((RING * rows, width), BF16)
    return call(
        kernel, core_arg, blocks, [whole(b) for b in blocks], out, whole(out), moved=8 * rows * width * 2
    )


def ring_gather(block, send):
    half = block.shape[0] // 2
    before, after = send(block, 1), send(block, -1)
    far = (send(before[:half], 1), send(after[half:], -1))
    return [block, after, far, before]


def near_gather(block, send):
    return [block] + [send(block, -step) for step in range(1, RING)]


def halves(parts, side, width=None, column=lambda i: 0):
    arrays, specs = [], []
    for part in parts:
        array, place = (part[side], 0) if isinstance(part, tuple) else (part, side)
        rows = array.shape[0] if isinstance(part, tuple) else array.shape[0] // 2
        arrays.append(array)
        specs.append(
            pl.BlockSpec(
                (rows, width or array.shape[1]), lambda i, s, place=place: (place, column(i))
            )
        )
    return arrays, specs


def flat(parts):
    return [array for part in parts for array in (part if isinstance(part, tuple) else (part,))]


def joined(parts, refs):
    values, refs = [], list(refs)
    for part in parts:
        if isinstance(part, tuple):
            values.append(jnp.concatenate([refs.pop(0)[...] for _ in part], axis=0))
        else:
            values.append(refs.pop(0)[...])
    return values


def by_place(refs, rows):
    return jnp.concatenate(
        [refs[dx][dy * rows : (dy + 1) * rows, :] for dy in range(RING) for dx in range(RING)], axis=0
    )


def head_products(z_arg, x_parts, dy_parts, w_qkv, w_out, side, dtype):
    count, depth, _ = w_qkv.shape
    x_arrays, x_specs = halves(x_parts, side)
    dy_arrays, dy_specs = halves(dy_parts, side)
    part = dy_specs[0].block_shape[0] // RING
    tokens = part * RING * RING
    width = (count + 1) * HD

    def kernel(z_ref, *refs):
        x_refs, dy_refs, (w_ref, wo_ref) = refs[:RING], refs[RING : 2 * RING], refs[2 * RING : 2 * RING + 2]
        out_refs, (x_all, dy_all) = refs[2 * RING + 2 : -2], refs[-2:]
        step = pl.program_id(0)

        @pl.when(step == 0)
        def _():
            x_all[...] = jnp.concatenate([ref[...] for ref in x_refs], axis=0)
            dy_all[...] = by_place(dy_refs, part)

        w = jnp.concatenate([w_ref[which] for which in range(count)], axis=1)
        prod = mm(x_all[...], w).astype(dtype)
        prod_out = lax.dot_general(
            dy_all[...], wo_ref[...], NT, preferred_element_type=F32
        ).astype(dtype)
        for i, out_ref in enumerate(out_refs):

            @pl.when(step == i)
            def _():
                out_ref[:, : count * HD] = prod
                out_ref[:, count * HD :] = prod_out

    outs = [shape_of((tokens, width), dtype) for _ in range(RING)]
    return call(
        kernel,
        z_arg,
        x_arrays + dy_arrays + [w_qkv, w_out],
        x_specs
        + dy_specs
        + [
            pl.BlockSpec((count, depth, HD), lambda i, z: (0, 0, (z[0] + i) % RING)),
            pl.BlockSpec((HD, depth), lambda i, z: ((z[0] + i) % RING, 0)),
        ],
        outs,
        [whole(o) for o in outs],
        grid=RING,
        flops=2 * tokens * depth * width * RING,
        moved=8 * MIB,
        scratch=[pltpu.VMEM((tokens, depth), BF16), pltpu.VMEM((tokens, depth), BF16)],
    )


def small(kernel, scalar, inputs, outs):
    moved = sum(a.size * a.dtype.itemsize for a in list(inputs) + list(outs))
    return call(
        kernel, scalar, inputs, [whole(a) for a in inputs], outs, [whole(o) for o in outs], moved=moved
    )


def first_pieces(scalar, own, got):
    half, width = own.shape[0] // 2, own.shape[1]

    def kernel(s_ref, own_ref, got_ref, top_ref, low_ref):
        total = (own_ref[...] + got_ref[...].astype(F32)).astype(BF16)
        top_ref[...] = total[:half]
        low_ref[...] = total[half:]

    return small(kernel, scalar, [own, got], [shape_of((half, width), BF16)] * 2)


def second_pieces(scalar, one, got_one, top, three, got_three, low):
    half = top.shape[0]

    def kernel(s_ref, one_ref, got_one_ref, top_ref, three_ref, got_three_ref, low_ref, out1, out3):
        first = one_ref[...] + got_one_ref[...].astype(F32)
        out1[:half, :] = (first[:half] + top_ref[...].astype(F32)).astype(BF16)
        out1[half:, :] = first[half:].astype(BF16)
        second = three_ref[...] + got_three_ref[...].astype(F32)
        out3[:half, :] = second[:half].astype(BF16)
        out3[half:, :] = (second[half:] + low_ref[...].astype(F32)).astype(BF16)

    inputs = [one, got_one, top, three, got_three, low]
    return small(kernel, scalar, inputs, [shape_of(one.shape, BF16)] * 2)


def own_piece(scalar, own, got, one, three):
    def kernel(s_ref, own_ref, got_ref, one_ref, three_ref, out_ref, kv_ref):
        total = own_ref[...] + got_ref[...].astype(F32)
        total = total + one_ref[...].astype(F32) + three_ref[...].astype(F32)
        total = total.astype(BF16)
        out_ref[...] = total
        kv_ref[...] = total[:, HD : 3 * HD]

    outs = [shape_of(own.shape, BF16), shape_of((own.shape[0], 2 * HD), BF16)]
    return small(kernel, scalar, [own, got, one, three], outs)


def project(z_arg, x_parts, dy_parts, w_qkv, w_out):
    sent = head_products(z_arg, x_parts, dy_parts, w_qkv, w_out, 1, BF16)
    got = {step: swap_cores(sent[step]) for step in (2, 1, 3, 0)}
    own = head_products(z_arg, x_parts, dy_parts, w_qkv, w_out, 0, F32)
    top, low = first_pieces(z_arg, own[2], got[2])
    top, low = to_z(top, 1), to_z(low, -1)
    one, three = second_pieces(z_arg, own[1], got[1], top, own[3], got[3], low)
    x_late = tied(flat(x_parts) + flat(dy_parts), [one, three])
    one, three = to_z(one, 1), to_z(three, -1)
    both, kv = own_piece(z_arg, own[0], got[0], one, three)
    return both, kv, x_late


def arrange(scalar, x_parts, dy_parts):
    features = x_parts[0].shape[1]
    tokens = 4 * x_parts[0].shape[0]
    tile = 256
    arrays, specs = [], []
    for parts in (x_parts, dy_parts):
        for side in range(2):
            side_arrays, side_specs = halves(parts, side, tile, lambda i: i)
            arrays += side_arrays
            specs += side_specs
    part = specs[0].block_shape[0] // RING

    def kernel(s_ref, *refs):
        x_t_ref, dy_ref = refs[4 * RING :]
        x = jnp.concatenate([ref[...] for ref in refs[: 2 * RING]], axis=0)
        x_t_ref[...] = x.T
        for side in range(2):
            group = refs[(2 + side) * RING : (3 + side) * RING]
            dy_ref[side * tokens // 2 : (side + 1) * tokens // 2, :] = by_place(group, part)

    return call(
        kernel,
        scalar,
        arrays,
        specs,
        [shape_of((features, tokens), BF16), shape_of((tokens, features), BF16)],
        [
            pl.BlockSpec((tile, tokens), lambda i, s: (i, 0)),
            pl.BlockSpec((tokens, tile), lambda i, s: (0, i)),
        ],
        grid=features // tile,
        moved=8 * tokens * features,
    )


def attend(scalar, both, kv_other, tok_col):
    tokens = both.shape[0]
    scale = 1.0 / math.sqrt(HD)
    tile = 128
    part = tok_col // 2

    def kernel(s_ref, both_ref, other_ref, query_out, attn_out, own_out, other_out, probs_all, grads_all):
        def position(index, half):
            dy, dx, token = index // (RING * part), index // part % RING, index % part
            device = (s_ref[0] + dx) % RING * RING + (s_ref[1] + dy) % RING
            return device * tok_col + half * part + token

        side = s_ref[2]
        key_index = lax.broadcasted_iota(jnp.int32, (1, 2 * tokens), 1)
        key_pos = position(key_index % tokens, side ^ (key_index // tokens))
        keys = jnp.concatenate([both_ref[:, HD : 2 * HD], other_ref[:, :HD]], axis=0)
        values = jnp.concatenate([both_ref[:, 2 * HD : 3 * HD], other_ref[:, HD:]], axis=0)
        for start in range(0, tokens, tile):
            rows = slice(start, start + tile)
            queries, grad_rows = both_ref[rows, :HD], both_ref[rows, 3 * HD :]
            query_index = start + lax.broadcasted_iota(jnp.int32, (tile, 1), 0)
            query_pos = position(query_index, side)
            first_pos = jnp.zeros_like(query_pos)
            for block in range(s_ref.shape[0] - 3):
                first_pos = jnp.where(query_pos // BLOCK == block, s_ref[3 + block], first_pos)
            allowed = (key_pos >= first_pos) & (key_pos <= query_pos)
            scores = lax.dot_general(queries, keys, NT, preferred_element_type=F32) * scale
            scores = jnp.where(allowed, scores, NEG)
            row_max = jnp.max(scores, axis=1, keepdims=True)
            weights = jnp.where(allowed, jnp.exp(scores - row_max), 0.0)
            row_sum = jnp.sum(weights, axis=1, keepdims=True)
            attention = (mm(weights.astype(BF16), values) / row_sum).astype(BF16)
            attn_out[rows, :] = attention
            row_delta = jnp.sum(
                grad_rows.astype(F32) * attention.astype(F32), axis=1, keepdims=True
            )
            probs = weights * (1.0 / row_sum)
            grad_probs = lax.dot_general(grad_rows, values, NT, preferred_element_type=F32)
            grad_scores = (probs * (grad_probs - row_delta)).astype(BF16)
            query_out[rows, :] = (mm(grad_scores, keys) * scale).astype(BF16)
            probs_all[rows, :] = probs.astype(BF16)
            grads_all[rows, :] = grad_scores
        grad_keys = (
            lax.dot_general(grads_all[...], both_ref[:, :HD], TN, preferred_element_type=F32) * scale
        )
        grad_values = lax.dot_general(
            probs_all[...], both_ref[:, 3 * HD :], TN, preferred_element_type=F32
        )
        own_out[:, :HD] = grad_keys[:tokens]
        own_out[:, HD:] = grad_values[:tokens]
        other_out[:, :HD] = grad_keys[tokens:].astype(BF16)
        other_out[:, HD:] = grad_values[tokens:].astype(BF16)

    outs = [
        shape_of((tokens, HD), BF16),
        shape_of((tokens, HD), BF16),
        shape_of((tokens, 2 * HD), F32),
        shape_of((tokens, 2 * HD), BF16),
    ]
    return call(
        kernel,
        scalar,
        [both, kv_other],
        [whole(both), whole(kv_other)],
        outs,
        [whole(o) for o in outs],
        flops=14 * tokens * 2 * tokens * HD,
        moved=4 * MIB,
        scratch=[pltpu.VMEM((tokens, 2 * tokens), BF16), pltpu.VMEM((tokens, 2 * tokens), BF16)],
    )


def pack_grads(scalar, grad_query, own, got, attention):
    def kernel(s_ref, query_ref, own_ref, got_ref, attn_ref, out_ref):
        out_ref[:, :HD] = query_ref[...]
        out_ref[:, HD : 3 * HD] = (own_ref[...] + got_ref[...].astype(F32)).astype(BF16)
        out_ref[:, 3 * HD :] = attn_ref[...]

    inputs = [grad_query, own, got, attention]
    (out,) = small(kernel, scalar, inputs, [shape_of((grad_query.shape[0], 4 * HD), BF16)])
    return out


def piece_y(scalar, mine, other, weights, step, received, dtype, cut):
    rows = mine[0].shape[0] // RING
    width = QKV * HD
    depth, features = weights.shape
    arrays, specs = [], []
    for part in mine + other:
        if isinstance(part, tuple):
            count = part[0].shape[0] // rows
            array, place = part[step // count], step % count
        else:
            array, place = part, step
        arrays.append(array)
        specs.append(pl.BlockSpec((rows, width), lambda i, s, place=place: (place, 0)))

    def kernel(s_ref, *refs):
        top = jnp.concatenate([ref[...] for ref in refs[:RING]], axis=1)
        low = jnp.concatenate([ref[...] for ref in refs[RING : 2 * RING]], axis=1)
        prod = mm(jnp.concatenate([top, low], axis=0), refs[2 * RING][...])
        finish_piece(prod, refs[2 * RING + 1 :], step, received, dtype, cut)

    return piece_call(
        kernel,
        scalar,
        arrays + [weights],
        specs + [whole(weights)],
        (2 * rows, features),
        depth,
        received,
        dtype,
        cut,
    )


def finish_piece(prod, refs, step, received, dtype, cut):
    half = prod.shape[0] // 2
    top, low = prod[:half], prod[half:]
    if received:
        if step == 1:
            top = top + refs[0][...].astype(F32)
        else:
            low = low + refs[0][...].astype(F32)
    outs = refs[len(received) :]
    if cut:
        outs[0][...] = top.astype(dtype)
        outs[1][...] = low.astype(dtype)
    else:
        outs[0][:half, :] = top.astype(dtype)
        outs[0][half:, :] = low.astype(dtype)


def piece_call(kernel, scalar, inputs, specs, shape, depth, received, dtype, cut):
    rows, features = shape
    outs = [shape_of((rows // 2, features), dtype)] * 2 if cut else [shape_of(shape, dtype)]
    return call(
        kernel,
        scalar,
        inputs + received,
        specs + [whole(r) for r in received],
        outs,
        [whole(o) for o in outs],
        flops=2 * rows * depth * features,
        moved=2 * depth * (rows + features),
    )


def piece_x(z_arg, mine, other, w_out, step, received, dtype, cut):
    rows = mine[0].shape[0] // (RING * RING)
    depth, features = w_out.shape

    arrays = flat(mine) + flat(other)
    count = len(arrays) // 2

    def kernel(z_ref, *refs):
        def taken(parts, group):
            return jnp.concatenate(
                [
                    jnp.concatenate(
                        [
                            value[(dy * RING + step) * rows : (dy * RING + step + 1) * rows]
                            for dy in range(RING)
                        ],
                        axis=0,
                    )
                    for value in joined(parts, group)
                ],
                axis=1,
            )

        both = jnp.concatenate(
            [taken(mine, refs[:count]), taken(other, refs[count : 2 * count])], axis=0
        )
        w = jnp.concatenate([ref[...] for ref in refs[2 * count : 2 * count + RING]], axis=0)
        finish_piece(mm(both, w), refs[2 * count + RING :], step, received, dtype, cut)

    specs = [pl.BlockSpec((a.shape[0], HD), lambda i, z: (0, QKV)) for a in arrays]
    w_specs = [
        pl.BlockSpec((HD, features), lambda i, z, d=d: ((z[0] + d) % RING, 0)) for d in range(RING)
    ]
    return piece_call(
        kernel,
        z_arg,
        arrays + [w_out] * RING,
        specs + w_specs,
        (2 * rows * RING, features),
        depth,
        received,
        dtype,
        cut,
    )


def split_sum(scalar, own, arrived):
    rows, width = own.shape
    part = rows // (2 * RING)

    def kernel(s_ref, own_ref, *refs):
        outs = refs[len(arrived) :]
        for i, out_ref in enumerate(outs):
            for side in range(2):
                place = pl.ds((side * RING + i) * part, part)
                total = own_ref[place, :]
                for ref in refs[: len(arrived)]:
                    total = total + ref[place, :].astype(F32)
                out_ref[side * part : (side + 1) * part, :] = total.astype(out_ref.dtype)

    outs = [shape_of((2 * part, width), BF16 if i else F32) for i in range(RING)]
    inputs = [own] + arrived
    return call(
        kernel,
        scalar,
        inputs,
        [whole(a) for a in inputs],
        outs,
        [whole(o) for o in outs],
        moved=14 * rows * width,
    )


def last_sum(core_arg, own, arrived):
    rows, width = own.shape
    half = rows // 2

    def kernel(core_ref, own_ref, *refs):
        out_ref = refs[len(arrived)]
        total = own_ref[...]
        for ref in refs[: len(arrived)]:
            total = total + ref[...].astype(F32)
        for side in range(2):
            start = pl.multiple_of((core_ref[0] ^ side) * half, half)
            out_ref[pl.ds(start, half), :] = total[side * half : (side + 1) * half].astype(BF16)

    out = shape_of((rows, width), BF16)
    inputs = [own] + arrived
    return call(
        kernel, core_arg, inputs, [whole(a) for a in inputs], out, whole(out), moved=14 * rows * width
    )


def scatter_sum_col(z_arg, core_arg, mine, other, weights, piece, first, second):
    def product(step, received, dtype, cut=False):
        return piece(z_arg, mine, other, weights, step, received, dtype, cut)

    top, low = product(2, [], BF16, cut=True)
    top, low = first(top, 1), first(low, -1)
    (one,) = product(1, [top], BF16)
    one = first(one, 1)
    (three,) = product(3, [low], BF16)
    three = first(three, -1)
    (own,) = product(0, [], F32)
    own, *parts = split_sum(z_arg, own, [one, three])
    return last_sum(core_arg, own, [second(parts[step - 1], step) for step in (2, 1, 3)])


def grad_qkv_product(z_arg, x_t, g_mine, g_other):
    features, tokens = x_t.shape
    tile = 256
    width = QKV * HD
    g_arrays = flat(g_mine) + flat(g_other)

    def kernel(z_ref, x_ref, *refs):
        g_refs, out_ref = refs[:-1], refs[-1]
        mine = joined(g_mine, g_refs[: len(g_refs) // 2])
        other = joined(g_other, g_refs[len(g_refs) // 2 :])
        for first in range(0, RING, 2):
            g = jnp.concatenate(
                [
                    jnp.concatenate([group[first], group[first + 1]], axis=1)
                    for group in (mine, other)
                ],
                axis=0,
            )
            prod = mm(x_ref[...], g)
            for step in range(2):
                head = lax.rem(z_ref[0] + first + step, RING)
                place = pl.ds(pl.multiple_of(head * HD, HD), HD)
                for which in range(QKV):
                    start = step * width + which * HD
                    out_ref[which, :, place] = prod[:, start : start + HD]

    return call(
        kernel,
        z_arg,
        [x_t] + g_arrays,
        [pl.BlockSpec((tile, tokens), lambda i, z: (i, 0))]
        + [pl.BlockSpec((g.shape[0], width), lambda i, z: (0, 0)) for g in g_arrays],
        shape_of((QKV, features, RING * HD), F32),
        pl.BlockSpec((QKV, tile, RING * HD), lambda i, z: (0, i, 0)),
        grid=features // tile,
        flops=2 * tokens * features * RING * width,
        moved=12 * MIB,
    )


def grad_out_product(z_arg, g_mine, g_other, dy_all):
    tokens, features = dy_all.shape
    tile = 512
    g_arrays = flat(g_mine) + flat(g_other)

    def kernel(z_ref, *refs):
        g_refs, dy_ref, out_ref = refs[:-2], refs[-2], refs[-1]
        attn = jnp.concatenate(
            [
                jnp.concatenate(joined(parts, group), axis=1)
                for parts, group in (
                    (g_mine, g_refs[: len(g_refs) // 2]),
                    (g_other, g_refs[len(g_refs) // 2 :]),
                )
            ],
            axis=0,
        )
        prod = lax.dot_general(attn, dy_ref[...], TN, preferred_element_type=F32)
        for step in range(RING):
            head = lax.rem(z_ref[0] + step, RING)
            out_ref[pl.ds(pl.multiple_of(head * HD, HD), HD), :] = prod[step * HD : (step + 1) * HD]

    return call(
        kernel,
        z_arg,
        g_arrays + [dy_all],
        [pl.BlockSpec((g.shape[0], HD), lambda i, z: (0, QKV)) for g in g_arrays]
        + [pl.BlockSpec((tokens, tile), lambda i, z: (0, i))],
        shape_of((RING * HD, features), F32),
        pl.BlockSpec((RING * HD, tile), lambda i, z: (0, i)),
        grid=features // tile,
        flops=2 * tokens * features * RING * HD,
        moved=5 * MIB,
    )


def on_device(normed, w_qkv, w_out, doc_start, grad_y):
    row_id, col_id = lax.axis_index("row"), lax.axis_index("col")
    z_id, core = row_id // CORES, row_id % CORES
    x_id, y_id = col_id // RING, col_id % RING
    z_arg, core_arg = z_id.reshape(1), core.reshape(1)
    place_arg = jnp.concatenate([jnp.stack([x_id, y_id, core]), doc_start])

    x_blocks, dy_blocks = near_gather(normed, to_x), near_gather(grad_y, to_y)
    blocks = tied(x_blocks + dy_blocks, [])
    x_parts = ring_gather(stack_blocks(core_arg, blocks[:RING]), to_y)
    dy_parts = ring_gather(stack_blocks(core_arg, blocks[RING:]), to_x)
    (w_turn,) = tied([w_qkv], [x_parts[1]])
    w_rel_t = turn_weights(z_arg, w_turn)
    flat_parts = tied(flat(x_parts) + flat(dy_parts), [w_rel_t])

    def parts_of(arrays):
        count = len(arrays) // 2
        return [[a[0], a[1], (a[2], a[3]), a[4]] for a in (arrays[:count], arrays[count:])]

    x_parts, dy_parts = parts_of(flat_parts)
    both, kv_mine, late = project(z_arg, x_parts, dy_parts, w_qkv, w_out)
    x_t, dy_all = arrange(z_arg, *parts_of(late))

    grad_query, attention, grad_kv, grad_kv_other = attend(
        place_arg, both, swap_cores(kv_mine), normed.shape[0]
    )
    grads = pack_grads(z_arg, grad_query, grad_kv, swap_cores(grad_kv_other), attention)
    g_mine = ring_gather(grads, to_z)
    g_other = [
        tuple(swap_cores(p) for p in part) if isinstance(part, tuple) else swap_cores(part)
        for part in g_mine
    ]

    layer_out = scatter_sum_col(z_arg, core_arg, g_mine, g_other, w_out, piece_x, to_x, to_y)
    grad_x = scatter_sum_col(z_arg, core_arg, g_mine, g_other, w_rel_t, piece_y, to_y, to_x)
    grad_qkv = grad_qkv_product(z_arg, x_t, g_mine, g_other)
    grad_out = grad_out_product(z_arg, g_mine, g_other, dy_all)
    return (layer_out, grad_x, grad_qkv, grad_out)


def solution(mesh):
    in_specs = (P("col", "row"), P(None, "row", "col"), P("col", "row"), P(), P("col", "row"))
    out_specs = (P("col", "row"), P("col", "row"), P(None, "row", "col"), P("col", "row"))
    return jax.shard_map(
        on_device, mesh=mesh, in_specs=in_specs, out_specs=out_specs, check_vma=False
    )
```

profile of v0, /device:TPU:24, one launch (start us, length us, event | category | flops | bytes accessed | tf_op | source)
XLA Modules:
  0.0 173.1 jit_solution(7195864846234644947)
XLA Ops:
  0.6 2.8 %collective-permute-start = (bf16[64,1024]{1,0:T(8,128)(2,1)}, bf16[64,1024]{1,0:T(8,128)(2,1)S(1)}, u32[]{:S(2)}, u32[]{:S(2)}) collective-permute-start(bf16[64,1024]{1,0:T(8,128)(2,1)} %refs_0_), channel_id=1, source_target_pairs={{0,12},{1,13},{2,14},{3,15},{4,0},{5,1},{6,2},{7,3},{8,4},{9,5},{1... | collective-permute-start | bytes 393224 | tf_op jit(solution)/shard_map/ppermute | solution.py:26
  6.8 2.5 %collective-permute-done.refs_1_ = bf16[64,1024]{1,0:T(8,128)(2,1)S(1)} collective-permute-done((bf16[64,1024]{1,0:T(8,128)(2,1)}, bf16[64,1024]{1,0:T(8,128)(2,1)S(1)}, u32[]{:S(2)}, u32[]{:S(2)}) %collective-permute-start) | collective-permute-done | bytes 131104 | tf_op jit(solution)/shard_map/ppermute | solution.py:26
  9.6 2.0 %collective-permute-done.1.refs_2_ = bf16[64,1024]{1,0:T(8,128)(2,1)S(1)} collective-permute-done((bf16[64,1024]{1,0:T(8,128)(2,1)}, bf16[64,1024]{1,0:T(8,128)(2,1)S(1)}, u32[]{:S(2)}, u32[]{:S(2)}) %collective-permute-start.1) | collective-permute-done | bytes 131104 | tf_op jit(solution)/shard_map/ppermute | solution.py:26
  16.3 2.5 %collective-permute-start.7 = (bf16[256,1024]{1,0:T(8,128)(2,1)S(1)}, bf16[256,1024]{1,0:T(8,128)(2,1)S(1)}, u32[]{:S(2)}, u32[]{:S(2)}) collective-permute-start(bf16[256,1024]{1,0:T(8,128)(2,1)S(1)} %shard_map.84.refs_0_.refs_4_), channel_id=1, source_target_pairs={{0,1},{1,2},{2,3},{3,0},{4,5},{5,6},{6,7},{7,4},{8,9},{9,10},{10,1... | collective-permute-start | bytes 1572872 | tf_op jit(solution)/shard_map/ppermute | solution.py:31
  21.4 2.0 %collective-permute-start.10 = (bf16[256,1024]{1,0:T(8,128)(2,1)S(1)}, bf16[256,1024]{1,0:T(8,128)(2,1)S(1)}, u32[]{:S(2)}, u32[]{:S(2)}) collective-permute-start(bf16[256,1024]{1,0:T(8,128)(2,1)S(1)} %shard_map.85.refs_4_.refs_8_.refs_12_), channel_id=1, source_target_pairs={{0,12},{1,13},{2,14},{3,15},{4,0},{5,1},{6,2},{7,3},{8,4},{9,5},{1... | collective-permute-start | bytes 1572872 | tf_op jit(solution)/shard_map/ppermute | solution.py:26
  23.4 4.6 %collective-permute-done.7.refs_3_.refs_7_ = bf16[256,1024]{1,0:T(8,128)(2,1)S(1)} collective-permute-done((bf16[256,1024]{1,0:T(8,128)(2,1)S(1)}, bf16[256,1024]{1,0:T(8,128)(2,1)S(1)}, u32[]{:S(2)}, u32[]{:S(2)}) %collective-permute-start.7) | collective-permute-done | bytes 524320 | tf_op jit(solution)/shard_map/ppermute | solution.py:31
  28.8 3.7 %collective-permute-start.8 = (bf16[128,1024]{1,0:T(8,128)(2,1)}, bf16[128,1024]{1,0:T(8,128)(2,1)S(1)}, u32[]{:S(2)}, u32[]{:S(2)}) collective-permute-start(bf16[128,1024]{1,0:T(8,128)(2,1)} %slice.24), channel_id=1, source_target_pairs={{0,1},{1,2},{2,3},{3,0},{4,5},{5,6},{6,7},{7,4},{8,9},{9,10},{10,1... | collective-permute-start | bytes 786440 | tf_op jit(solution)/shard_map/ppermute | solution.py:31
  34.2 1.9 %collective-permute-start.12 = (bf16[128,1024]{1,0:T(8,128)(2,1)}, bf16[128,1024]{1,0:T(8,128)(2,1)}, u32[]{:S(2)}, u32[]{:S(2)}) collective-permute-start(bf16[128,1024]{1,0:T(8,128)(2,1)} %slice.26), channel_id=1, source_target_pairs={{0,4},{1,5},{2,6},{3,7},{4,8},{5,9},{6,10},{7,11},{8,12},{9,13},{1... | collective-permute-start | bytes 786440 | tf_op jit(solution)/shard_map/ppermute | solution.py:26
  44.3 6.0 %shard_map.88 = (bf16[512,512]{1,0:T(8,128)(2,1)S(1)}, bf16[512,512]{1,0:T(8,128)(2,1)S(1)}, bf16[512,512]{1,0:T(8,128)(2,1)S(1)}, bf16[512,512]{1,0:T(8,128)(2,1)S(1)}) custom-call(s32[1]{0:T(128)} %bitcast.1.z_ref.s_ref, bf16[256,1024]{1,0:T(8,128)(2,1)S(1)} %shard_map.84.refs_0_.refs_4_, bf16[256,1024]{1,0:T(8,128)(2,1)S(1)} %collective-permute-done.6.refs_1_.refs_5_, ...), custom_call_target="tpu_custom_call" | custom-call | flops 2147483648 | bytes 8388608 | tf_op jit(solution)/shard_map/pallas_call | solution.py:74
  50.9 5.9 %shard_map.87 = (f32[512,512]{1,0:T(8,128)S(1)}, f32[512,512]{1,0:T(8,128)S(1)}, f32[512,512]{1,0:T(8,128)S(1)}, f32[512,512]{1,0:T(8,128)S(1)}) custom-call(s32[1]{0:T(128)} %bitcast.1.z_ref.s_ref, bf16[256,1024]{1,0:T(8,128)(2,1)S(1)} %shard_map.84.refs_0_.refs_4_, bf16[256,1024]{1,0:T(8,128)(2,1)S(1)} %collective-permute-done.6.refs_1_.refs_5_, ...), custom_call_target="tpu_custom_call" | custom-call | flops 2147483648 | bytes 8388608 | tf_op jit(solution)/shard_map/pallas_call | solution.py:74
  56.9 2.0 %collective-permute-start.17 = (bf16[256,512]{1,0:T(8,128)(2,1)S(1)}, bf16[256,512]{1,0:T(8,128)(2,1)S(1)}, u32[]{:S(2)}, u32[]{:S(2)}) collective-permute-start(bf16[256,512]{1,0:T(8,128)(2,1)S(1)} %get-tuple-element.90), channel_id=1, source_target_pairs={{0,32},{16,48},{32,64},{48,80},{64,96},{80,112},{96,0},{112,16},{1... | collective-permute-start | bytes 786440 | tf_op jit(solution)/shard_map/ppermute | solution.py:36
  58.9 2.2 %collective-permute-start.19 = (bf16[256,512]{1,0:T(8,128)(2,1)S(1)}, bf16[256,512]{1,0:T(8,128)(2,1)S(1)}, u32[]{:S(2)}, u32[]{:S(2)}) collective-permute-start(bf16[256,512]{1,0:T(8,128)(2,1)S(1)} %get-tuple-element.93), channel_id=1, source_target_pairs={{0,96},{16,112},{32,0},{48,16},{64,32},{80,48},{96,64},{112,80},{1... | collective-permute-start | bytes 786440 | tf_op jit(solution)/shard_map/ppermute | solution.py:36
  61.3 6.6 %collective-permute-done.17.top_ref = bf16[256,512]{1,0:T(8,128)(2,1)S(1)} collective-permute-done((bf16[256,512]{1,0:T(8,128)(2,1)S(1)}, bf16[256,512]{1,0:T(8,128)(2,1)S(1)}, u32[]{:S(2)}, u32[]{:S(2)}) %collective-permute-start.17) | collective-permute-done | bytes 262176 | tf_op jit(solution)/shard_map/ppermute | solution.py:36
  69.5 2.0 %collective-permute-start.21 = (bf16[512,512]{1,0:T(8,128)(2,1)S(1)}, bf16[512,512]{1,0:T(8,128)(2,1)S(1)}, u32[]{:S(2)}, u32[]{:S(2)}) collective-permute-start(bf16[512,512]{1,0:T(8,128)(2,1)S(1)} %get-tuple-element.95), channel_id=1, source_target_pairs={{0,96},{16,112},{32,0},{48,16},{64,32},{80,48},{96,64},{112,80},{1... | collective-permute-start | bytes 1572872 | tf_op jit(solution)/shard_map/ppermute | solution.py:36
  71.5 11.6 %collective-permute-done.20.one_ref = bf16[512,512]{1,0:T(8,128)(2,1)S(1)} collective-permute-done((bf16[512,512]{1,0:T(8,128)(2,1)S(1)}, bf16[512,512]{1,0:T(8,128)(2,1)S(1)}, u32[]{:S(2)}, u32[]{:S(2)}) %collective-permute-start.20) | collective-permute-done | bytes 524320 | tf_op jit(solution)/shard_map/ppermute | solution.py:36
  87.7 5.5 %shard_map.92 = (bf16[512,128]{1,0:T(8,128)(2,1)S(1)}, bf16[512,128]{1,0:T(8,128)(2,1)S(1)}, f32[512,256]{1,0:T(8,128)S(1)}, bf16[512,256]{1,0:T(8,128)(2,1)S(1)}) custom-call(s32[11]{0:T(128)S(1)} %pad_add_fusion.s_ref, bf16[512,512]{1,0:T(8,128)(2,1)S(1)} %copy-done.14, bf16[512,256]{1,0:T(8,128)(2,1)} %collective-permute-done.22.other_ref), custom_call_target="tpu_custom_call" | custom-call | flops 939524096 | bytes 4194304 | tf_op jit(solution)/shard_map/pallas_call | solution.py:74
  96.0 2.2 %collective-permute-start.24 = (bf16[512,512]{1,0:T(8,128)(2,1)S(1)}, bf16[512,512]{1,0:T(8,128)(2,1)S(1)}, u32[]{:S(2)}, u32[]{:S(2)}) collective-permute-start(bf16[512,512]{1,0:T(8,128)(2,1)S(1)} %shard_map.93.refs_0_), channel_id=1, source_target_pairs={{0,96},{16,112},{32,0},{48,16},{64,32},{80,48},{96,64},{112,80},{1... | collective-permute-start | bytes 1572872 | tf_op jit(solution)/shard_map/ppermute | solution.py:36
  98.2 11.9 %collective-permute-done.25.refs_4_.refs_3_ = bf16[512,512]{1,0:T(8,128)(2,1)S(1)} collective-permute-done((bf16[512,512]{1,0:T(8,128)(2,1)S(1)}, bf16[512,512]{1,0:T(8,128)(2,1)S(1)}, u32[]{:S(2)}, u32[]{:S(2)}) %collective-permute-start.25) | collective-permute-done | bytes 524320 | tf_op jit(solution)/shard_map/ppermute | solution.py:36
  110.9 3.2 %collective-permute-start.27 = (bf16[256,512]{1,0:T(8,128)(2,1)S(1)}, bf16[256,512]{1,0:T(8,128)(2,1)S(1)}, u32[]{:S(2)}, u32[]{:S(2)}) collective-permute-start(bf16[256,512]{1,0:T(8,128)(2,1)S(1)} %slice.29), channel_id=1, source_target_pairs={{0,96},{16,112},{32,0},{48,16},{64,32},{80,48},{96,64},{112,80},{1... | collective-permute-start | bytes 786440 | tf_op jit(solution)/shard_map/ppermute | solution.py:36
  114.1 4.9 %collective-permute-done.26.refs_2_ = bf16[256,512]{1,0:T(8,128)(2,1)S(1)} collective-permute-done((bf16[256,512]{1,0:T(8,128)(2,1)S(1)}, bf16[256,512]{1,0:T(8,128)(2,1)S(1)}, u32[]{:S(2)}, u32[]{:S(2)}) %collective-permute-start.26) | collective-permute-done | bytes 262176 | tf_op jit(solution)/shard_map/ppermute | solution.py:36
  122.7 2.6 %collective-permute-start.35 = (bf16[128,1024]{1,0:T(8,128)(2,1)S(1)}, bf16[128,1024]{1,0:T(8,128)(2,1)S(1)}, u32[]{:S(2)}, u32[]{:S(2)}) collective-permute-start(bf16[128,1024]{1,0:T(8,128)(2,1)S(1)} %get-tuple-element.103), channel_id=1, source_target_pairs={{0,12},{1,13},{2,14},{3,15},{4,0},{5,1},{6,2},{7,3},{8,4},{9,5},{1... | collective-permute-start | bytes 786440 | tf_op jit(solution)/shard_map/ppermute | solution.py:26
  126.2 3.3 %collective-permute-start.40 = (bf16[128,1024]{1,0:T(8,128)(2,1)S(1)}, bf16[128,1024]{1,0:T(8,128)(2,1)S(1)}, u32[]{:S(2)}, u32[]{:S(2)}) collective-permute-start(bf16[128,1024]{1,0:T(8,128)(2,1)S(1)} %get-tuple-element.108), channel_id=1, source_target_pairs={{0,1},{1,2},{2,3},{3,0},{4,5},{5,6},{6,7},{7,4},{8,9},{9,10},{10,1... | collective-permute-start | bytes 786440 | tf_op jit(solution)/shard_map/ppermute | solution.py:31
  129.6 2.0 %collective-permute-done.33.refs_14_ = bf16[128,1024]{1,0:T(8,128)(2,1)S(1)} collective-permute-done((bf16[128,1024]{1,0:T(8,128)(2,1)S(1)}, bf16[128,1024]{1,0:T(8,128)(2,1)S(1)}, u32[]{:S(2)}, u32[]{:S(2)}) %collective-permute-start.33) | collective-permute-done | bytes 262176 | tf_op jit(solution)/shard_map/ppermute | solution.py:26
  132.6 3.3 %collective-permute-start.36 = (bf16[256,1024]{1,0:T(8,128)(2,1)S(1)}, bf16[256,1024]{1,0:T(8,128)(2,1)S(1)}, u32[]{:S(2)}, u32[]{:S(2)}) collective-permute-start(bf16[256,1024]{1,0:T(8,128)(2,1)S(1)} %shard_map.97), channel_id=1, source_target_pairs={{0,12},{1,13},{2,14},{3,15},{4,0},{5,1},{6,2},{7,3},{8,4},{9,5},{1... | collective-permute-start | bytes 1572872 | tf_op jit(solution)/shard_map/ppermute | solution.py:26
  136.9 3.5 %collective-permute-start.41 = (bf16[256,1024]{1,0:T(8,128)(2,1)S(1)}, bf16[256,1024]{1,0:T(8,128)(2,1)S(1)}, u32[]{:S(2)}, u32[]{:S(2)}) collective-permute-start(bf16[256,1024]{1,0:T(8,128)(2,1)S(1)} %shard_map.102), channel_id=1, source_target_pairs={{0,1},{1,2},{2,3},{3,0},{4,5},{5,6},{6,7},{7,4},{8,9},{9,10},{10,1... | collective-permute-start | bytes 1572872 | tf_op jit(solution)/shard_map/ppermute | solution.py:31
  142.0 4.4 %collective-permute-done.34.refs_0_ = bf16[256,1024]{1,0:T(8,128)(2,1)S(1)} collective-permute-done((bf16[256,1024]{1,0:T(8,128)(2,1)S(1)}, bf16[256,1024]{1,0:T(8,128)(2,1)S(1)}, u32[]{:S(2)}, u32[]{:S(2)}) %collective-permute-start.34) | collective-permute-done | bytes 524320 | tf_op jit(solution)/shard_map/ppermute | solution.py:26
  146.6 2.0 %collective-permute-start.37 = (bf16[64,1024]{1,0:T(8,128)(2,1)S(1)}, bf16[64,1024]{1,0:T(8,128)(2,1)S(1)}, u32[]{:S(2)}, u32[]{:S(2)}) collective-permute-start(bf16[64,1024]{1,0:T(8,128)(2,1)S(1)} %get-tuple-element.105), channel_id=1, source_target_pairs={{0,2},{1,3},{2,0},{3,1},{4,6},{5,7},{6,4},{7,5},{8,10},{9,11},{10,... | collective-permute-start | bytes 393224 | tf_op jit(solution)/shard_map/ppermute | solution.py:31
  148.6 3.1 %shard_map.106 = (bf16[1024,1024]{1,0:T(8,128)(2,1)S(1)}, bf16[1024,1024]{1,0:T(8,128)(2,1)S(1)}) custom-call(s32[1]{0:T(128)} %bitcast.1.z_ref.s_ref, bf16[256,1024]{1,0:T(8,128)(2,1)S(1)} %shard_map.84.refs_0_.refs_4_, bf16[256,1024]{1,0:T(8,128)(2,1)S(1)} %collective-permute-done.6.refs_1_.refs_5_, bf16[128,1024]{1,0:T(8,128)(2,1)S(1)} %collective-permute-done.8.refs_2_, ...), custom_call_target="tpu_custom_call" | custom-call | bytes 8388608 | tf_op jit(solution)/shard_map/pallas_call | solution.py:74
  155.1 4.0 %collective-permute-done.43.refs_1_ = bf16[256,1024]{1,0:T(8,128)(2,1)S(1)} collective-permute-done((bf16[256,1024]{1,0:T(8,128)(2,1)S(1)}, bf16[256,1024]{1,0:T(8,128)(2,1)S(1)}, u32[]{:S(2)}, u32[]{:S(2)}) %collective-permute-start.43) | collective-permute-done | bytes 524320 | tf_op jit(solution)/shard_map/ppermute | solution.py:31
  159.7 3.1 %collective-permute-start.46 = (bf16[64,1024]{1,0:T(8,128)(2,1)S(1)}, bf16[64,1024]{1,0:T(8,128)(2,1)S(1)}, u32[]{:S(2)}, u32[]{:S(2)}) collective-permute-start(bf16[64,1024]{1,0:T(8,128)(2,1)S(1)} %get-tuple-element.113), channel_id=1, source_target_pairs={{0,12},{1,13},{2,14},{3,15},{4,0},{5,1},{6,2},{7,3},{8,4},{9,5},{1... | collective-permute-start | bytes 393224 | tf_op jit(solution)/shard_map/ppermute | solution.py:26
  162.8 6.0 %shard_map.107 = f32[3,1024,512]{2,1,0:T(8,128)} custom-call(s32[1]{0:T(128)} %bitcast.1.z_ref.s_ref, bf16[1024,1024]{1,0:T(8,128)(2,1)S(1)} %get-tuple-element.124.x_ref, bf16[512,512]{1,0:T(8,128)(2,1)S(1)} %shard_map.93.refs_0_, bf16[512,512]{1,0:T(8,128)(2,1)S(1)} %collective-permute-done.24.refs_1_, ...), custom_call_target="tpu_custom_call" | custom-call | flops 3221225472 | bytes 12582912 | tf_op jit(solution)/shard_map/pallas_call | solution.py:74
  168.8 2.8 %shard_map.108 = f32[512,1024]{1,0:T(8,128)} custom-call(s32[1]{0:T(128)} %bitcast.1.z_ref.s_ref, bf16[512,512]{1,0:T(8,128)(2,1)S(1)} %shard_map.93.refs_0_, bf16[512,512]{1,0:T(8,128)(2,1)S(1)} %collective-permute-done.24.refs_1_, bf16[256,512]{1,0:T(8,128)(2,1)S(1)} %collective-permute-done.26.refs_2_, ...), custom_call_target="tpu_custom_call" | custom-call | flops 1073741824 | bytes 5242880 | tf_op jit(solution)/shard_map/pallas_call | solution.py:74
  (126 shorter events, 45.7 us)
Async XLA Ops:
  15.5 17.0 %collective-permute-start.6 = (bf16[256,1024]{1,0:T(8,128)(2,1)S(1)}, bf16[256,1024]{1,0:T(8,128)(2,1)S(1)}, u32[]{:S(2)}, u32[]{:S(2)}) collective-permute-start(bf16[256,1024]{1,0:T(8,128)(2,1)S(1)} %shard_map.84.refs_0_.refs_4_), channel_id=1, source_target_pairs={{0,3},{1,0},{2,1},{3,2},{4,7},{5,4},{6,5},{7,6},{8,11},{9,8},{10,9... | collective-permute-start | bytes 1572872 | tf_op jit(solution)/shard_map/ppermute | solution.py:31
  16.3 11.8 %collective-permute-start.7 = (bf16[256,1024]{1,0:T(8,128)(2,1)S(1)}, bf16[256,1024]{1,0:T(8,128)(2,1)S(1)}, u32[]{:S(2)}, u32[]{:S(2)}) collective-permute-start(bf16[256,1024]{1,0:T(8,128)(2,1)S(1)} %shard_map.84.refs_0_.refs_4_), channel_id=1, source_target_pairs={{0,1},{1,2},{2,3},{3,0},{4,5},{5,6},{6,7},{7,4},{8,9},{9,10},{10,1... | collective-permute-start | bytes 1572872 | tf_op jit(solution)/shard_map/ppermute | solution.py:31
  19.7 13.7 %collective-permute-start.11 = (bf16[256,1024]{1,0:T(8,128)(2,1)S(1)}, bf16[256,1024]{1,0:T(8,128)(2,1)S(1)}, u32[]{:S(2)}, u32[]{:S(2)}) collective-permute-start(bf16[256,1024]{1,0:T(8,128)(2,1)S(1)} %shard_map.85.refs_4_.refs_8_.refs_12_), channel_id=1, source_target_pairs={{0,4},{1,5},{2,6},{3,7},{4,8},{5,9},{6,10},{7,11},{8,12},{9,13},{1... | collective-permute-start | bytes 1572872 | tf_op jit(solution)/shard_map/ppermute | solution.py:26
  21.4 14.8 %collective-permute-start.10 = (bf16[256,1024]{1,0:T(8,128)(2,1)S(1)}, bf16[256,1024]{1,0:T(8,128)(2,1)S(1)}, u32[]{:S(2)}, u32[]{:S(2)}) collective-permute-start(bf16[256,1024]{1,0:T(8,128)(2,1)S(1)} %shard_map.85.refs_4_.refs_8_.refs_12_), channel_id=1, source_target_pairs={{0,12},{1,13},{2,14},{3,15},{4,0},{5,1},{6,2},{7,3},{8,4},{9,5},{1... | collective-permute-start | bytes 1572872 | tf_op jit(solution)/shard_map/ppermute | solution.py:26
  28.8 15.4 %collective-permute-start.8 = (bf16[128,1024]{1,0:T(8,128)(2,1)}, bf16[128,1024]{1,0:T(8,128)(2,1)S(1)}, u32[]{:S(2)}, u32[]{:S(2)}) collective-permute-start(bf16[128,1024]{1,0:T(8,128)(2,1)} %slice.24), channel_id=1, source_target_pairs={{0,1},{1,2},{2,3},{3,0},{4,5},{5,6},{6,7},{7,4},{8,9},{9,10},{10,1... | collective-permute-start | bytes 786440 | tf_op jit(solution)/shard_map/ppermute | solution.py:31
  33.2 11.0 %collective-permute-start.9 = (bf16[128,1024]{1,0:T(8,128)(2,1)}, bf16[128,1024]{1,0:T(8,128)(2,1)}, u32[]{:S(2)}, u32[]{:S(2)}) collective-permute-start(bf16[128,1024]{1,0:T(8,128)(2,1)} %slice.25), channel_id=1, source_target_pairs={{0,3},{1,0},{2,1},{3,2},{4,7},{5,4},{6,5},{7,6},{8,11},{9,8},{10,9... | collective-permute-start | bytes 786440 | tf_op jit(solution)/shard_map/ppermute | solution.py:31
  34.2 10.0 %collective-permute-start.12 = (bf16[128,1024]{1,0:T(8,128)(2,1)}, bf16[128,1024]{1,0:T(8,128)(2,1)}, u32[]{:S(2)}, u32[]{:S(2)}) collective-permute-start(bf16[128,1024]{1,0:T(8,128)(2,1)} %slice.26), channel_id=1, source_target_pairs={{0,4},{1,5},{2,6},{3,7},{4,8},{5,9},{6,10},{7,11},{8,12},{9,13},{1... | collective-permute-start | bytes 786440 | tf_op jit(solution)/shard_map/ppermute | solution.py:26
  50.3 10.9 %collective-permute-start.15 = (bf16[512,512]{1,0:T(8,128)(2,1)S(1)}, bf16[512,512]{1,0:T(8,128)(2,1)S(1)}, u32[]{:S(2)}, u32[]{:S(2)}) collective-permute-start(bf16[512,512]{1,0:T(8,128)(2,1)S(1)} %get-tuple-element.87), channel_id=1, source_target_pairs={{0,16},{16,0},{32,48},{48,32},{64,80},{80,64},{96,112},{112,96},{1... | collective-permute-start | bytes 1572872 | tf_op jit(solution)/shard_map/ppermute | solution.py:41
  50.8 10.4 %collective-permute-start.18 = (bf16[512,512]{1,0:T(8,128)(2,1)S(1)}, bf16[512,512]{1,0:T(8,128)(2,1)S(1)}, u32[]{:S(2)}, u32[]{:S(2)}) collective-permute-start(bf16[512,512]{1,0:T(8,128)(2,1)S(1)} %get-tuple-element.92), channel_id=1, source_target_pairs={{0,16},{16,0},{32,48},{48,32},{64,80},{80,64},{96,112},{112,96},{1... | collective-permute-start | bytes 1572872 | tf_op jit(solution)/shard_map/ppermute | solution.py:41
  56.9 11.0 %collective-permute-start.17 = (bf16[256,512]{1,0:T(8,128)(2,1)S(1)}, bf16[256,512]{1,0:T(8,128)(2,1)S(1)}, u32[]{:S(2)}, u32[]{:S(2)}) collective-permute-start(bf16[256,512]{1,0:T(8,128)(2,1)S(1)} %get-tuple-element.90), channel_id=1, source_target_pairs={{0,32},{16,48},{32,64},{48,80},{64,96},{80,112},{96,0},{112,16},{1... | collective-permute-start | bytes 786440 | tf_op jit(solution)/shard_map/ppermute | solution.py:36
  61.1 10.4 %collective-permute-start.14 = (bf16[512,512]{1,0:T(8,128)(2,1)S(1)}, bf16[512,512]{1,0:T(8,128)(2,1)S(1)}, u32[]{:S(2)}, u32[]{:S(2)}) collective-permute-start(bf16[512,512]{1,0:T(8,128)(2,1)S(1)} %get-tuple-element.85), channel_id=1, source_target_pairs={{0,16},{16,0},{32,48},{48,32},{64,80},{80,64},{96,112},{112,96},{1... | collective-permute-start | bytes 1572872 | tf_op jit(solution)/shard_map/ppermute | solution.py:41
  68.2 14.9 %collective-permute-start.20 = (bf16[512,512]{1,0:T(8,128)(2,1)S(1)}, bf16[512,512]{1,0:T(8,128)(2,1)S(1)}, u32[]{:S(2)}, u32[]{:S(2)}) collective-permute-start(bf16[512,512]{1,0:T(8,128)(2,1)S(1)} %get-tuple-element.94), channel_id=1, source_target_pairs={{0,32},{16,48},{32,64},{48,80},{64,96},{80,112},{96,0},{112,16},{1... | collective-permute-start | bytes 1572872 | tf_op jit(solution)/shard_map/ppermute | solution.py:36
  69.5 13.6 %collective-permute-start.21 = (bf16[512,512]{1,0:T(8,128)(2,1)S(1)}, bf16[512,512]{1,0:T(8,128)(2,1)S(1)}, u32[]{:S(2)}, u32[]{:S(2)}) collective-permute-start(bf16[512,512]{1,0:T(8,128)(2,1)S(1)} %get-tuple-element.95), channel_id=1, source_target_pairs={{0,96},{16,112},{32,0},{48,16},{64,32},{80,48},{96,64},{112,80},{1... | collective-permute-start | bytes 1572872 | tf_op jit(solution)/shard_map/ppermute | solution.py:36
  94.9 15.2 %collective-permute-start.25 = (bf16[512,512]{1,0:T(8,128)(2,1)S(1)}, bf16[512,512]{1,0:T(8,128)(2,1)S(1)}, u32[]{:S(2)}, u32[]{:S(2)}) collective-permute-start(bf16[512,512]{1,0:T(8,128)(2,1)S(1)} %shard_map.93.refs_0_), channel_id=1, source_target_pairs={{0,32},{16,48},{32,64},{48,80},{64,96},{80,112},{96,0},{112,16},{1... | collective-permute-start | bytes 1572872 | tf_op jit(solution)/shard_map/ppermute | solution.py:36
  96.0 14.3 %collective-permute-start.24 = (bf16[512,512]{1,0:T(8,128)(2,1)S(1)}, bf16[512,512]{1,0:T(8,128)(2,1)S(1)}, u32[]{:S(2)}, u32[]{:S(2)}) collective-permute-start(bf16[512,512]{1,0:T(8,128)(2,1)S(1)} %shard_map.93.refs_0_), channel_id=1, source_target_pairs={{0,96},{16,112},{32,0},{48,16},{64,32},{80,48},{96,64},{112,80},{1... | collective-permute-start | bytes 1572872 | tf_op jit(solution)/shard_map/ppermute | solution.py:36
  98.2 21.7 %collective-permute-start.28 = (bf16[512,512]{1,0:T(8,128)(2,1)S(1)}, bf16[512,512]{1,0:T(8,128)(2,1)S(1)}, u32[]{:S(2)}, u32[]{:S(2)}) collective-permute-start(bf16[512,512]{1,0:T(8,128)(2,1)S(1)} %shard_map.93.refs_0_), channel_id=1, source_target_pairs={{0,16},{16,0},{32,48},{48,32},{64,80},{80,64},{96,112},{112,96},{1... | collective-permute-start | bytes 1572872 | tf_op jit(solution)/shard_map/ppermute | solution.py:41
  110.3 9.6 %collective-permute-start.29 = (bf16[512,512]{1,0:T(8,128)(2,1)S(1)}, bf16[512,512]{1,0:T(8,128)(2,1)S(1)}, u32[]{:S(2)}, u32[]{:S(2)}) collective-permute-start(bf16[512,512]{1,0:T(8,128)(2,1)S(1)} %collective-permute-done.24.refs_1_), channel_id=1, source_target_pairs={{0,16},{16,0},{32,48},{48,32},{64,80},{80,64},{96,112},{112,96},{1... | collective-permute-start | bytes 1572872 | tf_op jit(solution)/shard_map/ppermute | solution.py:41
  110.4 9.5 %collective-permute-start.32 = (bf16[512,512]{1,0:T(8,128)(2,1)S(1)}, bf16[512,512]{1,0:T(8,128)(2,1)S(1)}, u32[]{:S(2)}, u32[]{:S(2)}) collective-permute-start(bf16[512,512]{1,0:T(8,128)(2,1)S(1)} %collective-permute-done.25.refs_4_.refs_3_), channel_id=1, source_target_pairs={{0,16},{16,0},{32,48},{48,32},{64,80},{80,64},{96,112},{112,96},{1... | collective-permute-start | bytes 1572872 | tf_op jit(solution)/shard_map/ppermute | solution.py:41
  121.9 9.6 %collective-permute-start.33 = (bf16[128,1024]{1,0:T(8,128)(2,1)S(1)}, bf16[128,1024]{1,0:T(8,128)(2,1)S(1)}, u32[]{:S(2)}, u32[]{:S(2)}) collective-permute-start(bf16[128,1024]{1,0:T(8,128)(2,1)S(1)} %get-tuple-element.102), channel_id=1, source_target_pairs={{0,4},{1,5},{2,6},{3,7},{4,8},{5,9},{6,10},{7,11},{8,12},{9,13},{1... | collective-permute-start | bytes 786440 | tf_op jit(solution)/shard_map/ppermute | solution.py:26
  122.7 9.5 %collective-permute-start.35 = (bf16[128,1024]{1,0:T(8,128)(2,1)S(1)}, bf16[128,1024]{1,0:T(8,128)(2,1)S(1)}, u32[]{:S(2)}, u32[]{:S(2)}) collective-permute-start(bf16[128,1024]{1,0:T(8,128)(2,1)S(1)} %get-tuple-element.103), channel_id=1, source_target_pairs={{0,12},{1,13},{2,14},{3,15},{4,0},{5,1},{6,2},{7,3},{8,4},{9,5},{1... | collective-permute-start | bytes 786440 | tf_op jit(solution)/shard_map/ppermute | solution.py:26
  126.2 9.6 %collective-permute-start.40 = (bf16[128,1024]{1,0:T(8,128)(2,1)S(1)}, bf16[128,1024]{1,0:T(8,128)(2,1)S(1)}, u32[]{:S(2)}, u32[]{:S(2)}) collective-permute-start(bf16[128,1024]{1,0:T(8,128)(2,1)S(1)} %get-tuple-element.108), channel_id=1, source_target_pairs={{0,1},{1,2},{2,3},{3,0},{4,5},{5,6},{6,7},{7,4},{8,9},{9,10},{10,1... | collective-permute-start | bytes 786440 | tf_op jit(solution)/shard_map/ppermute | solution.py:31
  129.6 10.9 %collective-permute-start.42 = (bf16[128,1024]{1,0:T(8,128)(2,1)S(1)}, bf16[128,1024]{1,0:T(8,128)(2,1)S(1)}, u32[]{:S(2)}, u32[]{:S(2)}) collective-permute-start(bf16[128,1024]{1,0:T(8,128)(2,1)S(1)} %get-tuple-element.109), channel_id=1, source_target_pairs={{0,3},{1,0},{2,1},{3,2},{4,7},{5,4},{6,5},{7,6},{8,11},{9,8},{10,9... | collective-permute-start | bytes 786440 | tf_op jit(solution)/shard_map/ppermute | solution.py:31
  132.0 14.4 %collective-permute-start.34 = (bf16[256,1024]{1,0:T(8,128)(2,1)S(1)}, bf16[256,1024]{1,0:T(8,128)(2,1)S(1)}, u32[]{:S(2)}, u32[]{:S(2)}) collective-permute-start(bf16[256,1024]{1,0:T(8,128)(2,1)S(1)} %shard_map.96), channel_id=1, source_target_pairs={{0,4},{1,5},{2,6},{3,7},{4,8},{5,9},{6,10},{7,11},{8,12},{9,13},{1... | collective-permute-start | bytes 1572872 | tf_op jit(solution)/shard_map/ppermute | solution.py:26
  132.6 13.8 %collective-permute-start.36 = (bf16[256,1024]{1,0:T(8,128)(2,1)S(1)}, bf16[256,1024]{1,0:T(8,128)(2,1)S(1)}, u32[]{:S(2)}, u32[]{:S(2)}) collective-permute-start(bf16[256,1024]{1,0:T(8,128)(2,1)S(1)} %shard_map.97), channel_id=1, source_target_pairs={{0,12},{1,13},{2,14},{3,15},{4,0},{5,1},{6,2},{7,3},{8,4},{9,5},{1... | collective-permute-start | bytes 1572872 | tf_op jit(solution)/shard_map/ppermute | solution.py:26
  136.9 18.2 %collective-permute-start.41 = (bf16[256,1024]{1,0:T(8,128)(2,1)S(1)}, bf16[256,1024]{1,0:T(8,128)(2,1)S(1)}, u32[]{:S(2)}, u32[]{:S(2)}) collective-permute-start(bf16[256,1024]{1,0:T(8,128)(2,1)S(1)} %shard_map.102), channel_id=1, source_target_pairs={{0,1},{1,2},{2,3},{3,0},{4,5},{5,6},{6,7},{7,4},{8,9},{9,10},{10,1... | collective-permute-start | bytes 1572872 | tf_op jit(solution)/shard_map/ppermute | solution.py:31
  141.5 17.6 %collective-permute-start.43 = (bf16[256,1024]{1,0:T(8,128)(2,1)S(1)}, bf16[256,1024]{1,0:T(8,128)(2,1)S(1)}, u32[]{:S(2)}, u32[]{:S(2)}) collective-permute-start(bf16[256,1024]{1,0:T(8,128)(2,1)S(1)} %shard_map.103), channel_id=1, source_target_pairs={{0,3},{1,0},{2,1},{3,2},{4,7},{5,4},{6,5},{7,6},{8,11},{9,8},{10,9... | collective-permute-start | bytes 1572872 | tf_op jit(solution)/shard_map/ppermute | solution.py:31
  146.6 13.1 %collective-permute-start.37 = (bf16[64,1024]{1,0:T(8,128)(2,1)S(1)}, bf16[64,1024]{1,0:T(8,128)(2,1)S(1)}, u32[]{:S(2)}, u32[]{:S(2)}) collective-permute-start(bf16[64,1024]{1,0:T(8,128)(2,1)S(1)} %get-tuple-element.105), channel_id=1, source_target_pairs={{0,2},{1,3},{2,0},{3,1},{4,6},{5,7},{6,4},{7,5},{8,10},{9,11},{10,... | collective-permute-start | bytes 393224 | tf_op jit(solution)/shard_map/ppermute | solution.py:31
  152.7 18.9 %collective-permute-start.38 = (bf16[64,1024]{1,0:T(8,128)(2,1)S(1)}, bf16[64,1024]{1,0:T(8,128)(2,1)S(1)}, u32[]{:S(2)}, u32[]{:S(2)}) collective-permute-start(bf16[64,1024]{1,0:T(8,128)(2,1)S(1)} %get-tuple-element.106), channel_id=1, source_target_pairs={{0,1},{1,2},{2,3},{3,0},{4,5},{5,6},{6,7},{7,4},{8,9},{9,10},{10,1... | collective-permute-start | bytes 393224 | tf_op jit(solution)/shard_map/ppermute | solution.py:31
  154.2 17.5 %collective-permute-start.39 = (bf16[64,1024]{1,0:T(8,128)(2,1)S(1)}, bf16[64,1024]{1,0:T(8,128)(2,1)S(1)}, u32[]{:S(2)}, u32[]{:S(2)}) collective-permute-start(bf16[64,1024]{1,0:T(8,128)(2,1)S(1)} %get-tuple-element.107), channel_id=1, source_target_pairs={{0,3},{1,0},{2,1},{3,2},{4,7},{5,4},{6,5},{7,6},{8,11},{9,8},{10,9... | collective-permute-start | bytes 393224 | tf_op jit(solution)/shard_map/ppermute | solution.py:31
  159.3 13.1 %collective-permute-start.44 = (bf16[64,1024]{1,0:T(8,128)(2,1)S(1)}, bf16[64,1024]{1,0:T(8,128)(2,1)S(1)}, u32[]{:S(2)}, u32[]{:S(2)}) collective-permute-start(bf16[64,1024]{1,0:T(8,128)(2,1)S(1)} %get-tuple-element.111), channel_id=1, source_target_pairs={{0,8},{1,9},{2,10},{3,11},{4,12},{5,13},{6,14},{7,15},{8,0},{9,1},... | collective-permute-start | bytes 393224 | tf_op jit(solution)/shard_map/ppermute | solution.py:26
  159.6 12.8 %collective-permute-start.45 = (bf16[64,1024]{1,0:T(8,128)(2,1)S(1)}, bf16[64,1024]{1,0:T(8,128)(2,1)S(1)}, u32[]{:S(2)}, u32[]{:S(2)}) collective-permute-start(bf16[64,1024]{1,0:T(8,128)(2,1)S(1)} %get-tuple-element.112), channel_id=1, source_target_pairs={{0,4},{1,5},{2,6},{3,7},{4,8},{5,9},{6,10},{7,11},{8,12},{9,13},{1... | collective-permute-start | bytes 393224 | tf_op jit(solution)/shard_map/ppermute | solution.py:26
  159.7 12.7 %collective-permute-start.46 = (bf16[64,1024]{1,0:T(8,128)(2,1)S(1)}, bf16[64,1024]{1,0:T(8,128)(2,1)S(1)}, u32[]{:S(2)}, u32[]{:S(2)}) collective-permute-start(bf16[64,1024]{1,0:T(8,128)(2,1)S(1)} %get-tuple-element.113), channel_id=1, source_target_pairs={{0,12},{1,13},{2,14},{3,15},{4,0},{5,1},{6,2},{7,3},{8,4},{9,5},{1... | collective-permute-start | bytes 393224 | tf_op jit(solution)/shard_map/ppermute | solution.py:26
  (31 other events, 165.0 us)
where the time goes:
time: 174 us; the launch traced here: 173 us
  waiting for transfers between devices  63.7 us (37%)
  starting transfers between devices  58 us (33%)
  Pallas kernels  40 us (23%)
  local copies, waits for them, and re-layouts  10.3 us (6%)
    pallas_call x25, Pallas kernels, call(): pl.pallas_call(kernel, grid_spec=pltpu.PrefetchScalarGridSpec(num_scalar_...  40 us
    ppermute x8, waiting for transfers between devices, to_z(): return lax.ppermute(value, 'row', pairs)  36 us
    ppermute x14, starting transfers between devices, to_x(): return lax.ppermute(value, 'col', pairs)  22.2 us
    ppermute x14, starting transfers between devices, to_y(): return lax.ppermute(value, 'col', pairs)  20.2 us
    ppermute x8, starting transfers between devices, to_z(): return lax.ppermute(value, 'row', pairs)  14.1 us
    ppermute x14, waiting for transfers between devices, to_x(): return lax.ppermute(value, 'col', pairs)  12.6 us
    ppermute x14, waiting for transfers between devices, to_y(): return lax.ppermute(value, 'col', pairs)  10.3 us
    unnamed x32, local copies, waits for them, and re-layouts  7.34 us
  transfers between devices with their start and end apart: 47, of which 19 were waited for; matrix products, arithmetic and copies ran while one was open for 2% of the time, Pallas kernels for 15%

commit v1 on v0

--- a/solution.py
+++ b/solution.py
@@ -70,9 +70,17 @@
     moved=0,
     scratch=(),
     limit=16,
+    after=(),
 ):
+    count = len(inputs)
+
+    def wrapped(scalar_ref, *refs):
+        kernel(scalar_ref, *refs[:count], *refs[count + len(after) :])
+
+    inputs = list(inputs) + list(after)
+    in_specs = list(in_specs) + [pl.BlockSpec(memory_space=pl.ANY)] * len(after)
     return pl.pallas_call(
-        kernel,
+        wrapped,
         grid_spec=pltpu.PrefetchScalarGridSpec(
             num_scalar_prefetch=1,
             grid=(grid,),
@@ -178,50 +186,50 @@
 
     def kernel(z_ref, *refs):
         x_refs, dy_refs, (w_ref, wo_ref) = refs[:RING], refs[RING : 2 * RING], refs[2 * RING : 2 * RING + 2]
-        out_refs, (x_all, dy_all) = refs[2 * RING + 2 : -2], refs[-2:]
-        step = pl.program_id(0)
-
-        @pl.when(step == 0)
-        def _():
-            x_all[...] = jnp.concatenate([ref[...] for ref in x_refs], axis=0)
-            dy_all[...] = by_place(dy_refs, part)
-
-        w = jnp.concatenate([w_ref[which] for which in range(count)], axis=1)
-        prod = mm(x_all[...], w).astype(dtype)
-        prod_out = lax.dot_general(
-            dy_all[...], wo_ref[...], NT, preferred_element_type=F32
-        ).astype(dtype)
-        for i, out_ref in enumerate(out_refs):
-
-            @pl.when(step == i)
-            def _():
-                out_ref[:, : count * HD] = prod
-                out_ref[:, count * HD :] = prod_out
+        out_refs = refs[2 * RING + 2 :]
+        x = jnp.concatenate([ref[...] for ref in x_refs], axis=0)
+        dy = by_place(dy_refs, part)
+        places = [
+            pl.ds(pl.multiple_of(lax.rem(z_ref[0] + step, RING) * HD, HD), HD) for step in range(RING)
+        ]
+        for pair in ((2, 1), (3, 0)):
+            w = jnp.concatenate(
+                [w_ref[which, :, places[step]] for step in pair for which in range(count)], axis=1
+            )
+            wo = jnp.concatenate([wo_ref[places[step], :] for step in pair], axis=0)
+            prod = mm(x, w)
+            prod_out = lax.dot_general(dy, wo, NT, preferred_element_type=F32)
+            for i, step in enumerate(pair):
+                out_refs[step][:, : count * HD] = prod[
+                    :, i * count * HD : (i + 1) * count * HD
+                ].astype(dtype)
+                out_refs[step][:, count * HD :] = prod_out[:, i * HD : (i + 1) * HD].astype(dtype)
 
     outs = [shape_of((tokens, width), dtype) for _ in range(RING)]
     return call(
         kernel,
         z_arg,
         x_arrays + dy_arrays + [w_qkv, w_out],
-        x_specs
-        + dy_specs
-        + [
-            pl.BlockSpec((count, depth, HD), lambda i, z: (0, 0, (z[0] + i) % RING)),
-            pl.BlockSpec((HD, depth), lambda i, z: ((z[0] + i) % RING, 0)),
-        ],
+        x_specs + dy_specs + [whole(w_qkv), whole(w_out)],
         outs,
         [whole(o) for o in outs],
-        grid=RING,
         flops=2 * tokens * depth * width * RING,
         moved=8 * MIB,
-        scratch=[pltpu.VMEM((tokens, depth), BF16), pltpu.VMEM((tokens, depth), BF16)],
-    )
-
-
-def small(kernel, scalar, inputs, outs):
+        limit=24,
+    )
+
+
+def small(kernel, scalar, inputs, outs, after=()):
     moved = sum(a.size * a.dtype.itemsize for a in list(inputs) + list(outs))
     return call(
-        kernel, scalar, inputs, [whole(a) for a in inputs], outs, [whole(o) for o in outs], moved=moved
+        kernel,
+        scalar,
+        inputs,
+        [whole(a) for a in inputs],
+        outs,
+        [whole(o) for o in outs],
+        moved=moved,
+        after=after,
     )
 
 
@@ -251,7 +259,7 @@
     return small(kernel, scalar, inputs, [shape_of(one.shape, BF16)] * 2)
 
 
-def own_piece(scalar, own, got, one, three):
+def own_piece(scalar, own, got, one, three, after):
     def kernel(s_ref, own_ref, got_ref, one_ref, three_ref, out_ref, kv_ref):
         total = own_ref[...] + got_ref[...].astype(F32)
         total = total + one_ref[...].astype(F32) + three_ref[...].astype(F32)
@@ -260,20 +268,18 @@
         kv_ref[...] = total[:, HD : 3 * HD]
 
     outs = [shape_of(own.shape, BF16), shape_of((own.shape[0], 2 * HD), BF16)]
-    return small(kernel, scalar, [own, got, one, three], outs)
-
-
-def project(z_arg, x_parts, dy_parts, w_qkv, w_out):
+    return small(kernel, scalar, [own, got, one, three], outs, after)
+
+
+def project(z_arg, x_parts, dy_parts, w_qkv, w_out, meanwhile):
     sent = head_products(z_arg, x_parts, dy_parts, w_qkv, w_out, 1, BF16)
     got = {step: swap_cores(sent[step]) for step in (2, 1, 3, 0)}
     own = head_products(z_arg, x_parts, dy_parts, w_qkv, w_out, 0, F32)
     top, low = first_pieces(z_arg, own[2], got[2])
     top, low = to_z(top, 1), to_z(low, -1)
     one, three = second_pieces(z_arg, own[1], got[1], top, own[3], got[3], low)
-    x_late = tied(flat(x_parts) + flat(dy_parts), [one, three])
     one, three = to_z(one, 1), to_z(three, -1)
-    both, kv = own_piece(z_arg, own[0], got[0], one, three)
-    return both, kv, x_late
+    return own_piece(z_arg, own[0], got[0], one, three, meanwhile)
 
 
 def arrange(scalar, x_parts, dy_parts):
@@ -394,7 +400,7 @@
     return out
 
 
-def piece_y(scalar, mine, other, weights, step, received, dtype, cut):
+def piece_y(scalar, mine, other, weights, step, received, dtype, cut, after):
     rows = mine[0].shape[0] // RING
     width = QKV * HD
     depth, features = weights.shape
@@ -424,6 +430,7 @@
         received,
         dtype,
         cut,
+        after,
     )
 
 
@@ -444,7 +451,7 @@
         outs[0][half:, :] = low.astype(dtype)
 
 
-def piece_call(kernel, scalar, inputs, specs, shape, depth, received, dtype, cut):
+def piece_call(kernel, scalar, inputs, specs, shape, depth, received, dtype, cut, after):
     rows, features = shape
     outs = [shape_of((rows // 2, features), dtype)] * 2 if cut else [shape_of(shape, dtype)]
     return call(
@@ -456,10 +463,11 @@
         [whole(o) for o in outs],
         flops=2 * rows * depth * features,
         moved=2 * depth * (rows + features),
-    )
-
-
-def piece_x(z_arg, mine, other, w_out, step, received, dtype, cut):
+        after=after,
+    )
+
+
+def piece_x(z_arg, mine, other, w_out, step, received, dtype, cut, after):
     rows = mine[0].shape[0] // (RING * RING)
     depth, features = w_out.shape
 
@@ -502,6 +510,7 @@
         received,
         dtype,
         cut,
+        after,
     )
 
 
@@ -552,9 +561,9 @@
     )
 
 
-def scatter_sum_col(z_arg, core_arg, mine, other, weights, piece, first, second):
-    def product(step, received, dtype, cut=False):
-        return piece(z_arg, mine, other, weights, step, received, dtype, cut)
+def scatter_sum_col(z_arg, core_arg, mine, other, weights, piece, first, second, after=()):
+    def product(step, received, dtype, cut=False, after=()):
+        return piece(z_arg, mine, other, weights, step, received, dtype, cut, after)
 
     top, low = product(2, [], BF16, cut=True)
     top, low = first(top, 1), first(low, -1)
@@ -562,7 +571,7 @@
     one = first(one, 1)
     (three,) = product(3, [low], BF16)
     three = first(three, -1)
-    (own,) = product(0, [], F32)
+    (own,) = product(0, [], F32, after=after)
     own, *parts = split_sum(z_arg, own, [one, three])
     return last_sum(core_arg, own, [second(parts[step - 1], step) for step in (2, 1, 3)])
 
@@ -663,8 +672,8 @@
         return [[a[0], a[1], (a[2], a[3]), a[4]] for a in (arrays[:count], arrays[count:])]
 
     x_parts, dy_parts = parts_of(flat_parts)
-    both, kv_mine, late = project(z_arg, x_parts, dy_parts, w_qkv, w_out)
-    x_t, dy_all = arrange(z_arg, *parts_of(late))
+    x_t, dy_all = arrange(z_arg, x_parts, dy_parts)
+    both, kv_mine = project(z_arg, x_parts, dy_parts, w_qkv, w_out, [x_t])
 
     grad_query, attention, grad_kv, grad_kv_other = attend(
         place_arg, both, swap_cores(kv_mine), normed.shape[0]
@@ -676,10 +685,12 @@
         for part in g_mine
     ]
 
-    layer_out = scatter_sum_col(z_arg, core_arg, g_mine, g_other, w_out, piece_x, to_x, to_y)
+    grad_out = grad_out_product(z_arg, g_mine, g_other, dy_all)
+    layer_out = scatter_sum_col(
+        z_arg, core_arg, g_mine, g_other, w_out, piece_x, to_x, to_y, [grad_out]
+    )
     grad_x = scatter_sum_col(z_arg, core_arg, g_mine, g_other, w_rel_t, piece_y, to_y, to_x)
     grad_qkv = grad_qkv_product(z_arg, x_t, g_mine, g_other)
-    grad_out = grad_out_product(z_arg, g_mine, g_other, dy_all)
     return (layer_out, grad_x, grad_qkv, grad_out)
 
 

time: 174 us -> 167 us (0.960)
  Pallas kernels: 40 us -> 33.9 us
  waiting for transfers between devices: 63.7 us -> 57.8 us
  local copies, waits for them, and re-layouts: 10.3 us -> 14.9 us
    pallas_call x25, Pallas kernels: 40 us -> 33.9 us  [call(): pl.pallas_call(wrapped, grid_spec=pltpu.PrefetchScalarGridSpec(num_scalar...]
    ppermute x8, waiting for transfers between devices: 36 us -> 31.6 us  [to_z(): return lax.ppermute(value, 'row', pairs)]
    unnamed x32 -> x50, local copies, waits for them, and re-layouts: 7.34 us -> 11.8 us
    ppermute x14, waiting for transfers between devices: 12.6 us -> 8.26 us  [to_x(): return lax.ppermute(value, 'col', pairs)]
    ppermute x14, waiting for transfers between devices: 10.3 us -> 13.3 us  [to_y(): return lax.ppermute(value, 'col', pairs)]
  transfers between devices with their start and end apart: 47 -> 47, of which waited for: 19 -> 20; matrix products, arithmetic and copies ran while one was open for 2% -> 2% of each run, Pallas kernels for 15% -> 14%
where the time goes in v1:
time: 167 us; the launch traced here: 166 us
  starting transfers between devices  58.7 us (35%)
  waiting for transfers between devices  57.8 us (35%)
  Pallas kernels  33.9 us (20%)
  local copies, waits for them, and re-layouts  14.9 us (9%)
    pallas_call x25, Pallas kernels, call(): pl.pallas_call(wrapped, grid_spec=pltpu.PrefetchScalarGridSpec(num_scalar...  33.9 us
    ppermute x8, waiting for transfers between devices, to_z(): return lax.ppermute(value, 'row', pairs)  31.6 us
    ppermute x14, starting transfers between devices, to_x(): return lax.ppermute(value, 'col', pairs)  22.9 us
    ppermute x14, starting transfers between devices, to_y(): return lax.ppermute(value, 'col', pairs)  19.9 us
    ppermute x8, starting transfers between devices, to_z(): return lax.ppermute(value, 'row', pairs)  14.3 us
    ppermute x14, waiting for transfers between devices, to_y(): return lax.ppermute(value, 'col', pairs)  13.3 us
    unnamed x50, local copies, waits for them, and re-layouts  11.8 us
    ppermute x14, waiting for transfers between devices, to_x(): return lax.ppermute(value, 'col', pairs)  8.26 us
  transfers between devices with their start and end apart: 47, of which 20 were waited for; matrix products, arithmetic and copies ran while one was open for 2% of the time, Pallas kernels for 14%

profile of v1, /device:TPU:24, one launch (start us, length us, event | category | flops | bytes accessed | tf_op | source)
XLA Modules:
  0.0 166.4 jit_solution(16428397132092064704)
XLA Ops:
  0.6 2.8 %collective-permute-start = (bf16[64,1024]{1,0:T(8,128)(2,1)}, bf16[64,1024]{1,0:T(8,128)(2,1)S(1)}, u32[]{:S(2)}, u32[]{:S(2)}) collective-permute-start(bf16[64,1024]{1,0:T(8,128)(2,1)} %refs_0_), channel_id=1, source_target_pairs={{0,12},{1,13},{2,14},{3,15},{4,0},{5,1},{6,2},{7,3},{8,4},{9,5},{1... | collective-permute-start | bytes 393224 | tf_op jit(solution)/shard_map/ppermute | solution.py:26
  6.8 2.5 %collective-permute-done.refs_1_ = bf16[64,1024]{1,0:T(8,128)(2,1)S(1)} collective-permute-done((bf16[64,1024]{1,0:T(8,128)(2,1)}, bf16[64,1024]{1,0:T(8,128)(2,1)S(1)}, u32[]{:S(2)}, u32[]{:S(2)}) %collective-permute-start) | collective-permute-done | bytes 131104 | tf_op jit(solution)/shard_map/ppermute | solution.py:26
  9.6 2.0 %collective-permute-done.1.refs_2_ = bf16[64,1024]{1,0:T(8,128)(2,1)S(1)} collective-permute-done((bf16[64,1024]{1,0:T(8,128)(2,1)}, bf16[64,1024]{1,0:T(8,128)(2,1)S(1)}, u32[]{:S(2)}, u32[]{:S(2)}) %collective-permute-start.1) | collective-permute-done | bytes 131104 | tf_op jit(solution)/shard_map/ppermute | solution.py:26
  16.3 2.5 %collective-permute-start.7 = (bf16[256,1024]{1,0:T(8,128)(2,1)S(1)}, bf16[256,1024]{1,0:T(8,128)(2,1)S(1)}, u32[]{:S(2)}, u32[]{:S(2)}) collective-permute-start(bf16[256,1024]{1,0:T(8,128)(2,1)S(1)} %shard_map.84.refs_0_.refs_4_), channel_id=1, source_target_pairs={{0,1},{1,2},{2,3},{3,0},{4,5},{5,6},{6,7},{7,4},{8,9},{9,10},{10,1... | collective-permute-start | bytes 1572872 | tf_op jit(solution)/shard_map/ppermute | solution.py:31
  21.4 2.0 %collective-permute-start.10 = (bf16[256,1024]{1,0:T(8,128)(2,1)S(1)}, bf16[256,1024]{1,0:T(8,128)(2,1)S(1)}, u32[]{:S(2)}, u32[]{:S(2)}) collective-permute-start(bf16[256,1024]{1,0:T(8,128)(2,1)S(1)} %shard_map.85.refs_4_.refs_8_.refs_12_), channel_id=1, source_target_pairs={{0,12},{1,13},{2,14},{3,15},{4,0},{5,1},{6,2},{7,3},{8,4},{9,5},{1... | collective-permute-start | bytes 1572872 | tf_op jit(solution)/shard_map/ppermute | solution.py:26
  23.5 4.6 %collective-permute-done.7.refs_3_.refs_7_ = bf16[256,1024]{1,0:T(8,128)(2,1)S(1)} collective-permute-done((bf16[256,1024]{1,0:T(8,128)(2,1)S(1)}, bf16[256,1024]{1,0:T(8,128)(2,1)S(1)}, u32[]{:S(2)}, u32[]{:S(2)}) %collective-permute-start.7) | collective-permute-done | bytes 524320 | tf_op jit(solution)/shard_map/ppermute | solution.py:31
  28.9 3.7 %collective-permute-start.8 = (bf16[128,1024]{1,0:T(8,128)(2,1)}, bf16[128,1024]{1,0:T(8,128)(2,1)S(1)}, u32[]{:S(2)}, u32[]{:S(2)}) collective-permute-start(bf16[128,1024]{1,0:T(8,128)(2,1)} %slice.24), channel_id=1, source_target_pairs={{0,1},{1,2},{2,3},{3,0},{4,5},{5,6},{6,7},{7,4},{8,9},{9,10},{10,1... | collective-permute-start | bytes 786440 | tf_op jit(solution)/shard_map/ppermute | solution.py:31
  35.0 2.1 %collective-permute-start.12 = (bf16[128,1024]{1,0:T(8,128)(2,1)}, bf16[128,1024]{1,0:T(8,128)(2,1)}, u32[]{:S(2)}, u32[]{:S(2)}) collective-permute-start(bf16[128,1024]{1,0:T(8,128)(2,1)} %slice.26), channel_id=1, source_target_pairs={{0,4},{1,5},{2,6},{3,7},{4,8},{5,9},{6,10},{7,11},{8,12},{9,13},{1... | collective-permute-start | bytes 786440 | tf_op jit(solution)/shard_map/ppermute | solution.py:26
  45.7 3.4 %shard_map.88 = (bf16[512,512]{1,0:T(8,128)(2,1)S(1)}, bf16[512,512]{1,0:T(8,128)(2,1)S(1)}, bf16[512,512]{1,0:T(8,128)(2,1)S(1)}, bf16[512,512]{1,0:T(8,128)(2,1)S(1)}) custom-call(s32[1]{0:T(128)} %bitcast.1.scalar_ref, bf16[256,1024]{1,0:T(8,128)(2,1)S(1)} %shard_map.84.refs_0_.refs_4_, bf16[256,1024]{1,0:T(8,128)(2,1)S(1)} %collective-permute-done.6.refs_1_.refs_5_, ...), custom_call_target="tpu_custom_call" | custom-call | flops 2147483648 | bytes 8388608 | tf_op jit(solution)/shard_map/pallas_call | solution.py:82
  49.8 3.3 %shard_map.87 = (f32[512,512]{1,0:T(8,128)S(1)}, f32[512,512]{1,0:T(8,128)S(1)}, f32[512,512]{1,0:T(8,128)S(1)}, f32[512,512]{1,0:T(8,128)S(1)}) custom-call(s32[1]{0:T(128)} %bitcast.1.scalar_ref, bf16[256,1024]{1,0:T(8,128)(2,1)S(1)} %shard_map.84.refs_0_.refs_4_, bf16[256,1024]{1,0:T(8,128)(2,1)S(1)} %collective-permute-done.6.refs_1_.refs_5_, ...), custom_call_target="tpu_custom_call" | custom-call | flops 2147483648 | bytes 8388608 | tf_op jit(solution)/shard_map/pallas_call | solution.py:82
  53.3 2.0 %collective-permute-start.17 = (bf16[256,512]{1,0:T(8,128)(2,1)S(1)}, bf16[256,512]{1,0:T(8,128)(2,1)S(1)}, u32[]{:S(2)}, u32[]{:S(2)}) collective-permute-start(bf16[256,512]{1,0:T(8,128)(2,1)S(1)} %get-tuple-element.80), channel_id=1, source_target_pairs={{0,32},{16,48},{32,64},{48,80},{64,96},{80,112},{96,0},{112,16},{1... | collective-permute-start | bytes 786440 | tf_op jit(solution)/shard_map/ppermute | solution.py:36
  55.3 2.2 %collective-permute-start.19 = (bf16[256,512]{1,0:T(8,128)(2,1)S(1)}, bf16[256,512]{1,0:T(8,128)(2,1)S(1)}, u32[]{:S(2)}, u32[]{:S(2)}) collective-permute-start(bf16[256,512]{1,0:T(8,128)(2,1)S(1)} %get-tuple-element.83), channel_id=1, source_target_pairs={{0,96},{16,112},{32,0},{48,16},{64,32},{80,48},{96,64},{112,80},{1... | collective-permute-start | bytes 786440 | tf_op jit(solution)/shard_map/ppermute | solution.py:36
  57.7 6.6 %collective-permute-done.17.refs_2_ = bf16[256,512]{1,0:T(8,128)(2,1)S(1)} collective-permute-done((bf16[256,512]{1,0:T(8,128)(2,1)S(1)}, bf16[256,512]{1,0:T(8,128)(2,1)S(1)}, u32[]{:S(2)}, u32[]{:S(2)}) %collective-permute-start.17) | collective-permute-done | bytes 262176 | tf_op jit(solution)/shard_map/ppermute | solution.py:36
  66.1 2.0 %collective-permute-start.21 = (bf16[512,512]{1,0:T(8,128)(2,1)S(1)}, bf16[512,512]{1,0:T(8,128)(2,1)S(1)}, u32[]{:S(2)}, u32[]{:S(2)}) collective-permute-start(bf16[512,512]{1,0:T(8,128)(2,1)S(1)} %get-tuple-element.85), channel_id=1, source_target_pairs={{0,96},{16,112},{32,0},{48,16},{64,32},{80,48},{96,64},{112,80},{1... | collective-permute-start | bytes 1572872 | tf_op jit(solution)/shard_map/ppermute | solution.py:36
  68.1 3.1 %shard_map.91 = (bf16[1024,1024]{1,0:T(8,128)(2,1)S(1)}, bf16[1024,1024]{1,0:T(8,128)(2,1)S(1)}) custom-call(s32[1]{0:T(128)} %bitcast.1.scalar_ref, bf16[256,1024]{1,0:T(8,128)(2,1)S(1)} %copy-done.5, bf16[256,1024]{1,0:T(8,128)(2,1)S(1)} %copy-done.9, bf16[128,1024]{1,0:T(8,128)(2,1)S(1)} %collective-permute-done.8.refs_2_, ...), custom_call_target="tpu_custom_call" | custom-call | bytes 8388608 | tf_op jit(solution)/shard_map/pallas_call | solution.py:82
  72.5 7.2 %collective-permute-done.20.refs_2_ = bf16[512,512]{1,0:T(8,128)(2,1)S(1)} collective-permute-done((bf16[512,512]{1,0:T(8,128)(2,1)S(1)}, bf16[512,512]{1,0:T(8,128)(2,1)S(1)}, u32[]{:S(2)}, u32[]{:S(2)}) %collective-permute-start.20) | collective-permute-done | bytes 524320 | tf_op jit(solution)/shard_map/ppermute | solution.py:36
  84.2 4.5 %shard_map.93 = (bf16[512,128]{1,0:T(8,128)(2,1)S(1)}, bf16[512,128]{1,0:T(8,128)(2,1)S(1)}, f32[512,256]{1,0:T(8,128)S(1)}, bf16[512,256]{1,0:T(8,128)(2,1)S(1)}) custom-call(s32[11]{0:T(128)S(1)} %pad_add_fusion.scalar_ref, bf16[512,512]{1,0:T(8,128)(2,1)S(1)} %copy-done.23, bf16[512,256]{1,0:T(8,128)(2,1)S(1)} %collective-permute-done.22.refs_1_), custom_call_target="tpu_custom_call" | custom-call | flops 939524096 | bytes 4194304 | tf_op jit(solution)/shard_map/pallas_call | solution.py:82
  91.5 2.2 %collective-permute-start.24 = (bf16[512,512]{1,0:T(8,128)(2,1)S(1)}, bf16[512,512]{1,0:T(8,128)(2,1)S(1)}, u32[]{:S(2)}, u32[]{:S(2)}) collective-permute-start(bf16[512,512]{1,0:T(8,128)(2,1)S(1)} %shard_map.94.refs_0_.refs_1_), channel_id=1, source_target_pairs={{0,96},{16,112},{32,0},{48,16},{64,32},{80,48},{96,64},{112,80},{1... | collective-permute-start | bytes 1572872 | tf_op jit(solution)/shard_map/ppermute | solution.py:36
  93.7 11.9 %collective-permute-done.25.refs_4_.refs_3_.refs_5_ = bf16[512,512]{1,0:T(8,128)(2,1)S(1)} collective-permute-done((bf16[512,512]{1,0:T(8,128)(2,1)S(1)}, bf16[512,512]{1,0:T(8,128)(2,1)S(1)}, u32[]{:S(2)}, u32[]{:S(2)}) %collective-permute-start.25) | collective-permute-done | bytes 524320 | tf_op jit(solution)/shard_map/ppermute | solution.py:36
  106.4 3.2 %collective-permute-start.27 = (bf16[256,512]{1,0:T(8,128)(2,1)S(1)}, bf16[256,512]{1,0:T(8,128)(2,1)S(1)}, u32[]{:S(2)}, u32[]{:S(2)}) collective-permute-start(bf16[256,512]{1,0:T(8,128)(2,1)S(1)} %slice.29), channel_id=1, source_target_pairs={{0,96},{16,112},{32,0},{48,16},{64,32},{80,48},{96,64},{112,80},{1... | collective-permute-start | bytes 786440 | tf_op jit(solution)/shard_map/ppermute | solution.py:36
  109.6 4.9 %collective-permute-done.26.refs_2_.refs_3_ = bf16[256,512]{1,0:T(8,128)(2,1)S(1)} collective-permute-done((bf16[256,512]{1,0:T(8,128)(2,1)S(1)}, bf16[256,512]{1,0:T(8,128)(2,1)S(1)}, u32[]{:S(2)}, u32[]{:S(2)}) %collective-permute-start.26) | collective-permute-done | bytes 262176 | tf_op jit(solution)/shard_map/ppermute | solution.py:36
  118.3 2.5 %collective-permute-start.35 = (bf16[128,1024]{1,0:T(8,128)(2,1)S(1)}, bf16[128,1024]{1,0:T(8,128)(2,1)S(1)}, u32[]{:S(2)}, u32[]{:S(2)}) collective-permute-start(bf16[128,1024]{1,0:T(8,128)(2,1)S(1)} %get-tuple-element.95), channel_id=1, source_target_pairs={{0,12},{1,13},{2,14},{3,15},{4,0},{5,1},{6,2},{7,3},{8,4},{9,5},{1... | collective-permute-start | bytes 786440 | tf_op jit(solution)/shard_map/ppermute | solution.py:26
  121.7 3.3 %collective-permute-start.40 = (bf16[128,1024]{1,0:T(8,128)(2,1)S(1)}, bf16[128,1024]{1,0:T(8,128)(2,1)S(1)}, u32[]{:S(2)}, u32[]{:S(2)}) collective-permute-start(bf16[128,1024]{1,0:T(8,128)(2,1)S(1)} %get-tuple-element.100), channel_id=1, source_target_pairs={{0,1},{1,2},{2,3},{3,0},{4,5},{5,6},{6,7},{7,4},{8,9},{9,10},{10,1... | collective-permute-start | bytes 786440 | tf_op jit(solution)/shard_map/ppermute | solution.py:31
  125.1 2.0 %collective-permute-done.33.refs_14_ = bf16[128,1024]{1,0:T(8,128)(2,1)S(1)} collective-permute-done((bf16[128,1024]{1,0:T(8,128)(2,1)S(1)}, bf16[128,1024]{1,0:T(8,128)(2,1)S(1)}, u32[]{:S(2)}, u32[]{:S(2)}) %collective-permute-start.33) | collective-permute-done | bytes 262176 | tf_op jit(solution)/shard_map/ppermute | solution.py:26
  128.3 3.3 %collective-permute-start.36 = (bf16[256,1024]{1,0:T(8,128)(2,1)S(1)}, bf16[256,1024]{1,0:T(8,128)(2,1)S(1)}, u32[]{:S(2)}, u32[]{:S(2)}) collective-permute-start(bf16[256,1024]{1,0:T(8,128)(2,1)S(1)} %shard_map.99), channel_id=1, source_target_pairs={{0,12},{1,13},{2,14},{3,15},{4,0},{5,1},{6,2},{7,3},{8,4},{9,5},{1... | collective-permute-start | bytes 1572872 | tf_op jit(solution)/shard_map/ppermute | solution.py:26
  132.6 3.3 %collective-permute-start.41 = (bf16[256,1024]{1,0:T(8,128)(2,1)S(1)}, bf16[256,1024]{1,0:T(8,128)(2,1)S(1)}, u32[]{:S(2)}, u32[]{:S(2)}) collective-permute-start(bf16[256,1024]{1,0:T(8,128)(2,1)S(1)} %shard_map.104), channel_id=1, source_target_pairs={{0,1},{1,2},{2,3},{3,0},{4,5},{5,6},{6,7},{7,4},{8,9},{9,10},{10,1... | collective-permute-start | bytes 1572872 | tf_op jit(solution)/shard_map/ppermute | solution.py:31
  137.0 2.9 %shard_map.95.refs_14_ = f32[512,1024]{1,0:T(8,128)} custom-call(s32[1]{0:T(128)} %bitcast.1.scalar_ref, bf16[512,512]{1,0:T(8,128)(2,1)S(1)} %shard_map.94.refs_0_.refs_1_, bf16[512,512]{1,0:T(8,128)(2,1)S(1)} %collective-permute-done.24.refs_1_.refs_2_, bf16[256,512]{1,0:T(8,128)(2,1)S(1)} %collective-permute-done.26.refs_2_.refs_3_, ...), custom_call_target="tpu_custom_call" | custom-call | flops 1073741824 | bytes 5242880 | tf_op jit(solution)/shard_map/pallas_call | solution.py:82
  142.3 2.0 %collective-permute-start.37 = (bf16[64,1024]{1,0:T(8,128)(2,1)S(1)}, bf16[64,1024]{1,0:T(8,128)(2,1)S(1)}, u32[]{:S(2)}, u32[]{:S(2)}) collective-permute-start(bf16[64,1024]{1,0:T(8,128)(2,1)S(1)} %get-tuple-element.97), channel_id=1, source_target_pairs={{0,2},{1,3},{2,0},{3,1},{4,6},{5,7},{6,4},{7,5},{8,10},{9,11},{10,... | collective-permute-start | bytes 393224 | tf_op jit(solution)/shard_map/ppermute | solution.py:31
  147.6 2.6 %collective-permute-done.41.refs_1_ = bf16[256,1024]{1,0:T(8,128)(2,1)S(1)} collective-permute-done((bf16[256,1024]{1,0:T(8,128)(2,1)S(1)}, bf16[256,1024]{1,0:T(8,128)(2,1)S(1)}, u32[]{:S(2)}, u32[]{:S(2)}) %collective-permute-start.41) | collective-permute-done | bytes 524320 | tf_op jit(solution)/shard_map/ppermute | solution.py:31
  150.3 4.5 %collective-permute-done.43.refs_2_ = bf16[256,1024]{1,0:T(8,128)(2,1)S(1)} collective-permute-done((bf16[256,1024]{1,0:T(8,128)(2,1)S(1)}, bf16[256,1024]{1,0:T(8,128)(2,1)S(1)}, u32[]{:S(2)}, u32[]{:S(2)}) %collective-permute-start.43) | collective-permute-done | bytes 524320 | tf_op jit(solution)/shard_map/ppermute | solution.py:31
  156.0 2.9 %collective-permute-start.46 = (bf16[64,1024]{1,0:T(8,128)(2,1)S(1)}, bf16[64,1024]{1,0:T(8,128)(2,1)S(1)}, u32[]{:S(2)}, u32[]{:S(2)}) collective-permute-start(bf16[64,1024]{1,0:T(8,128)(2,1)S(1)} %get-tuple-element.105), channel_id=1, source_target_pairs={{0,12},{1,13},{2,14},{3,15},{4,0},{5,1},{6,2},{7,3},{8,4},{9,5},{1... | collective-permute-start | bytes 393224 | tf_op jit(solution)/shard_map/ppermute | solution.py:26
  158.9 6.0 %shard_map.108 = f32[3,1024,512]{2,1,0:T(8,128)} custom-call(s32[1]{0:T(128)} %bitcast.1.scalar_ref, bf16[1024,1024]{1,0:T(8,128)(2,1)S(1)} %get-tuple-element.86.refs_4_.refs_0_, bf16[512,512]{1,0:T(8,128)(2,1)S(1)} %shard_map.94.refs_0_.refs_1_, bf16[512,512]{1,0:T(8,128)(2,1)S(1)} %collective-permute-done.24.refs_1_.refs_2_, ...), custom_call_target="tpu_custom_call" | custom-call | flops 3221225472 | bytes 12582912 | tf_op jit(solution)/shard_map/pallas_call | solution.py:82
  (144 shorter events, 51.3 us)
Async XLA Ops:
  15.5 17.1 %collective-permute-start.6 = (bf16[256,1024]{1,0:T(8,128)(2,1)S(1)}, bf16[256,1024]{1,0:T(8,128)(2,1)S(1)}, u32[]{:S(2)}, u32[]{:S(2)}) collective-permute-start(bf16[256,1024]{1,0:T(8,128)(2,1)S(1)} %shard_map.84.refs_0_.refs_4_), channel_id=1, source_target_pairs={{0,3},{1,0},{2,1},{3,2},{4,7},{5,4},{6,5},{7,6},{8,11},{9,8},{10,9... | collective-permute-start | bytes 1572872 | tf_op jit(solution)/shard_map/ppermute | solution.py:31
  16.3 11.8 %collective-permute-start.7 = (bf16[256,1024]{1,0:T(8,128)(2,1)S(1)}, bf16[256,1024]{1,0:T(8,128)(2,1)S(1)}, u32[]{:S(2)}, u32[]{:S(2)}) collective-permute-start(bf16[256,1024]{1,0:T(8,128)(2,1)S(1)} %shard_map.84.refs_0_.refs_4_), channel_id=1, source_target_pairs={{0,1},{1,2},{2,3},{3,0},{4,5},{5,6},{6,7},{7,4},{8,9},{9,10},{10,1... | collective-permute-start | bytes 1572872 | tf_op jit(solution)/shard_map/ppermute | solution.py:31
  19.8 13.7 %collective-permute-start.11 = (bf16[256,1024]{1,0:T(8,128)(2,1)S(1)}, bf16[256,1024]{1,0:T(8,128)(2,1)S(1)}, u32[]{:S(2)}, u32[]{:S(2)}) collective-permute-start(bf16[256,1024]{1,0:T(8,128)(2,1)S(1)} %shard_map.85.refs_4_.refs_8_.refs_12_), channel_id=1, source_target_pairs={{0,4},{1,5},{2,6},{3,7},{4,8},{5,9},{6,10},{7,11},{8,12},{9,13},{1... | collective-permute-start | bytes 1572872 | tf_op jit(solution)/shard_map/ppermute | solution.py:26
  21.4 15.6 %collective-permute-start.10 = (bf16[256,1024]{1,0:T(8,128)(2,1)S(1)}, bf16[256,1024]{1,0:T(8,128)(2,1)S(1)}, u32[]{:S(2)}, u32[]{:S(2)}) collective-permute-start(bf16[256,1024]{1,0:T(8,128)(2,1)S(1)} %shard_map.85.refs_4_.refs_8_.refs_12_), channel_id=1, source_target_pairs={{0,12},{1,13},{2,14},{3,15},{4,0},{5,1},{6,2},{7,3},{8,4},{9,5},{1... | collective-permute-start | bytes 1572872 | tf_op jit(solution)/shard_map/ppermute | solution.py:26
  28.9 16.8 %collective-permute-start.8 = (bf16[128,1024]{1,0:T(8,128)(2,1)}, bf16[128,1024]{1,0:T(8,128)(2,1)S(1)}, u32[]{:S(2)}, u32[]{:S(2)}) collective-permute-start(bf16[128,1024]{1,0:T(8,128)(2,1)} %slice.24), channel_id=1, source_target_pairs={{0,1},{1,2},{2,3},{3,0},{4,5},{5,6},{6,7},{7,4},{8,9},{9,10},{10,1... | collective-permute-start | bytes 786440 | tf_op jit(solution)/shard_map/ppermute | solution.py:31
  33.4 12.3 %collective-permute-start.9 = (bf16[128,1024]{1,0:T(8,128)(2,1)}, bf16[128,1024]{1,0:T(8,128)(2,1)}, u32[]{:S(2)}, u32[]{:S(2)}) collective-permute-start(bf16[128,1024]{1,0:T(8,128)(2,1)} %slice.25), channel_id=1, source_target_pairs={{0,3},{1,0},{2,1},{3,2},{4,7},{5,4},{6,5},{7,6},{8,11},{9,8},{10,9... | collective-permute-start | bytes 786440 | tf_op jit(solution)/shard_map/ppermute | solution.py:31
  35.0 10.6 %collective-permute-start.12 = (bf16[128,1024]{1,0:T(8,128)(2,1)}, bf16[128,1024]{1,0:T(8,128)(2,1)}, u32[]{:S(2)}, u32[]{:S(2)}) collective-permute-start(bf16[128,1024]{1,0:T(8,128)(2,1)} %slice.26), channel_id=1, source_target_pairs={{0,4},{1,5},{2,6},{3,7},{4,8},{5,9},{6,10},{7,11},{8,12},{9,13},{1... | collective-permute-start | bytes 786440 | tf_op jit(solution)/shard_map/ppermute | solution.py:26
  53.3 11.0 %collective-permute-start.17 = (bf16[256,512]{1,0:T(8,128)(2,1)S(1)}, bf16[256,512]{1,0:T(8,128)(2,1)S(1)}, u32[]{:S(2)}, u32[]{:S(2)}) collective-permute-start(bf16[256,512]{1,0:T(8,128)(2,1)S(1)} %get-tuple-element.80), channel_id=1, source_target_pairs={{0,32},{16,48},{32,64},{48,80},{64,96},{80,112},{96,0},{112,16},{1... | collective-permute-start | bytes 786440 | tf_op jit(solution)/shard_map/ppermute | solution.py:36
  55.3 9.0 %collective-permute-start.19 = (bf16[256,512]{1,0:T(8,128)(2,1)S(1)}, bf16[256,512]{1,0:T(8,128)(2,1)S(1)}, u32[]{:S(2)}, u32[]{:S(2)}) collective-permute-start(bf16[256,512]{1,0:T(8,128)(2,1)S(1)} %get-tuple-element.83), channel_id=1, source_target_pairs={{0,96},{16,112},{32,0},{48,16},{64,32},{80,48},{96,64},{112,80},{1... | collective-permute-start | bytes 786440 | tf_op jit(solution)/shard_map/ppermute | solution.py:36
  57.5 15.0 %collective-permute-start.14 = (bf16[512,512]{1,0:T(8,128)(2,1)S(1)}, bf16[512,512]{1,0:T(8,128)(2,1)S(1)}, u32[]{:S(2)}, u32[]{:S(2)}) collective-permute-start(bf16[512,512]{1,0:T(8,128)(2,1)S(1)} %get-tuple-element.75), channel_id=1, source_target_pairs={{0,16},{16,0},{32,48},{48,32},{64,80},{80,64},{96,112},{112,96},{1... | collective-permute-start | bytes 1572872 | tf_op jit(solution)/shard_map/ppermute | solution.py:41
  64.6 15.1 %collective-permute-start.20 = (bf16[512,512]{1,0:T(8,128)(2,1)S(1)}, bf16[512,512]{1,0:T(8,128)(2,1)S(1)}, u32[]{:S(2)}, u32[]{:S(2)}) collective-permute-start(bf16[512,512]{1,0:T(8,128)(2,1)S(1)} %get-tuple-element.84), channel_id=1, source_target_pairs={{0,32},{16,48},{32,64},{48,80},{64,96},{80,112},{96,0},{112,16},{1... | collective-permute-start | bytes 1572872 | tf_op jit(solution)/shard_map/ppermute | solution.py:36
  66.1 13.6 %collective-permute-start.21 = (bf16[512,512]{1,0:T(8,128)(2,1)S(1)}, bf16[512,512]{1,0:T(8,128)(2,1)S(1)}, u32[]{:S(2)}, u32[]{:S(2)}) collective-permute-start(bf16[512,512]{1,0:T(8,128)(2,1)S(1)} %get-tuple-element.85), channel_id=1, source_target_pairs={{0,96},{16,112},{32,0},{48,16},{64,32},{80,48},{96,64},{112,80},{1... | collective-permute-start | bytes 1572872 | tf_op jit(solution)/shard_map/ppermute | solution.py:36
  90.4 15.2 %collective-permute-start.25 = (bf16[512,512]{1,0:T(8,128)(2,1)S(1)}, bf16[512,512]{1,0:T(8,128)(2,1)S(1)}, u32[]{:S(2)}, u32[]{:S(2)}) collective-permute-start(bf16[512,512]{1,0:T(8,128)(2,1)S(1)} %shard_map.94.refs_0_.refs_1_), channel_id=1, source_target_pairs={{0,32},{16,48},{32,64},{48,80},{64,96},{80,112},{96,0},{112,16},{1... | collective-permute-start | bytes 1572872 | tf_op jit(solution)/shard_map/ppermute | solution.py:36
  91.5 14.3 %collective-permute-start.24 = (bf16[512,512]{1,0:T(8,128)(2,1)S(1)}, bf16[512,512]{1,0:T(8,128)(2,1)S(1)}, u32[]{:S(2)}, u32[]{:S(2)}) collective-permute-start(bf16[512,512]{1,0:T(8,128)(2,1)S(1)} %shard_map.94.refs_0_.refs_1_), channel_id=1, source_target_pairs={{0,96},{16,112},{32,0},{48,16},{64,32},{80,48},{96,64},{112,80},{1... | collective-permute-start | bytes 1572872 | tf_op jit(solution)/shard_map/ppermute | solution.py:36
  93.7 21.7 %collective-permute-start.28 = (bf16[512,512]{1,0:T(8,128)(2,1)S(1)}, bf16[512,512]{1,0:T(8,128)(2,1)S(1)}, u32[]{:S(2)}, u32[]{:S(2)}) collective-permute-start(bf16[512,512]{1,0:T(8,128)(2,1)S(1)} %shard_map.94.refs_0_.refs_1_), channel_id=1, source_target_pairs={{0,16},{16,0},{32,48},{48,32},{64,80},{80,64},{96,112},{112,96},{1... | collective-permute-start | bytes 1572872 | tf_op jit(solution)/shard_map/ppermute | solution.py:41
  105.8 9.6 %collective-permute-start.29 = (bf16[512,512]{1,0:T(8,128)(2,1)S(1)}, bf16[512,512]{1,0:T(8,128)(2,1)S(1)}, u32[]{:S(2)}, u32[]{:S(2)}) collective-permute-start(bf16[512,512]{1,0:T(8,128)(2,1)S(1)} %collective-permute-done.24.refs_1_.refs_2_), channel_id=1, source_target_pairs={{0,16},{16,0},{32,48},{48,32},{64,80},{80,64},{96,112},{112,96},{1... | collective-permute-start | bytes 1572872 | tf_op jit(solution)/shard_map/ppermute | solution.py:41
  105.9 9.5 %collective-permute-start.32 = (bf16[512,512]{1,0:T(8,128)(2,1)S(1)}, bf16[512,512]{1,0:T(8,128)(2,1)S(1)}, u32[]{:S(2)}, u32[]{:S(2)}) collective-permute-start(bf16[512,512]{1,0:T(8,128)(2,1)S(1)} %collective-permute-done.25.refs_4_.refs_3_.refs_5_), channel_id=1, source_target_pairs={{0,16},{16,0},{32,48},{48,32},{64,80},{80,64},{96,112},{112,96},{1... | collective-permute-start | bytes 1572872 | tf_op jit(solution)/shard_map/ppermute | solution.py:41
  106.4 9.0 %collective-permute-start.27 = (bf16[256,512]{1,0:T(8,128)(2,1)S(1)}, bf16[256,512]{1,0:T(8,128)(2,1)S(1)}, u32[]{:S(2)}, u32[]{:S(2)}) collective-permute-start(bf16[256,512]{1,0:T(8,128)(2,1)S(1)} %slice.29), channel_id=1, source_target_pairs={{0,96},{16,112},{32,0},{48,16},{64,32},{80,48},{96,64},{112,80},{1... | collective-permute-start | bytes 786440 | tf_op jit(solution)/shard_map/ppermute | solution.py:36
  117.4 9.6 %collective-permute-start.33 = (bf16[128,1024]{1,0:T(8,128)(2,1)S(1)}, bf16[128,1024]{1,0:T(8,128)(2,1)S(1)}, u32[]{:S(2)}, u32[]{:S(2)}) collective-permute-start(bf16[128,1024]{1,0:T(8,128)(2,1)S(1)} %get-tuple-element.94), channel_id=1, source_target_pairs={{0,4},{1,5},{2,6},{3,7},{4,8},{5,9},{6,10},{7,11},{8,12},{9,13},{1... | collective-permute-start | bytes 786440 | tf_op jit(solution)/shard_map/ppermute | solution.py:26
  118.3 9.6 %collective-permute-start.35 = (bf16[128,1024]{1,0:T(8,128)(2,1)S(1)}, bf16[128,1024]{1,0:T(8,128)(2,1)S(1)}, u32[]{:S(2)}, u32[]{:S(2)}) collective-permute-start(bf16[128,1024]{1,0:T(8,128)(2,1)S(1)} %get-tuple-element.95), channel_id=1, source_target_pairs={{0,12},{1,13},{2,14},{3,15},{4,0},{5,1},{6,2},{7,3},{8,4},{9,5},{1... | collective-permute-start | bytes 786440 | tf_op jit(solution)/shard_map/ppermute | solution.py:26
  121.7 9.9 %collective-permute-start.40 = (bf16[128,1024]{1,0:T(8,128)(2,1)S(1)}, bf16[128,1024]{1,0:T(8,128)(2,1)S(1)}, u32[]{:S(2)}, u32[]{:S(2)}) collective-permute-start(bf16[128,1024]{1,0:T(8,128)(2,1)S(1)} %get-tuple-element.100), channel_id=1, source_target_pairs={{0,1},{1,2},{2,3},{3,0},{4,5},{5,6},{6,7},{7,4},{8,9},{9,10},{10,1... | collective-permute-start | bytes 786440 | tf_op jit(solution)/shard_map/ppermute | solution.py:31
  125.1 10.9 %collective-permute-start.42 = (bf16[128,1024]{1,0:T(8,128)(2,1)S(1)}, bf16[128,1024]{1,0:T(8,128)(2,1)S(1)}, u32[]{:S(2)}, u32[]{:S(2)}) collective-permute-start(bf16[128,1024]{1,0:T(8,128)(2,1)S(1)} %get-tuple-element.101), channel_id=1, source_target_pairs={{0,3},{1,0},{2,1},{3,2},{4,7},{5,4},{6,5},{7,6},{8,11},{9,8},{10,9... | collective-permute-start | bytes 786440 | tf_op jit(solution)/shard_map/ppermute | solution.py:31
  127.5 14.6 %collective-permute-start.34 = (bf16[256,1024]{1,0:T(8,128)(2,1)S(1)}, bf16[256,1024]{1,0:T(8,128)(2,1)S(1)}, u32[]{:S(2)}, u32[]{:S(2)}) collective-permute-start(bf16[256,1024]{1,0:T(8,128)(2,1)S(1)} %shard_map.98), channel_id=1, source_target_pairs={{0,4},{1,5},{2,6},{3,7},{4,8},{5,9},{6,10},{7,11},{8,12},{9,13},{1... | collective-permute-start | bytes 1572872 | tf_op jit(solution)/shard_map/ppermute | solution.py:26
  128.3 13.8 %collective-permute-start.36 = (bf16[256,1024]{1,0:T(8,128)(2,1)S(1)}, bf16[256,1024]{1,0:T(8,128)(2,1)S(1)}, u32[]{:S(2)}, u32[]{:S(2)}) collective-permute-start(bf16[256,1024]{1,0:T(8,128)(2,1)S(1)} %shard_map.99), channel_id=1, source_target_pairs={{0,12},{1,13},{2,14},{3,15},{4,0},{5,1},{6,2},{7,3},{8,4},{9,5},{1... | collective-permute-start | bytes 1572872 | tf_op jit(solution)/shard_map/ppermute | solution.py:26
  132.6 17.6 %collective-permute-start.41 = (bf16[256,1024]{1,0:T(8,128)(2,1)S(1)}, bf16[256,1024]{1,0:T(8,128)(2,1)S(1)}, u32[]{:S(2)}, u32[]{:S(2)}) collective-permute-start(bf16[256,1024]{1,0:T(8,128)(2,1)S(1)} %shard_map.104), channel_id=1, source_target_pairs={{0,1},{1,2},{2,3},{3,0},{4,5},{5,6},{6,7},{7,4},{8,9},{9,10},{10,1... | collective-permute-start | bytes 1572872 | tf_op jit(solution)/shard_map/ppermute | solution.py:31
  136.9 17.8 %collective-permute-start.43 = (bf16[256,1024]{1,0:T(8,128)(2,1)S(1)}, bf16[256,1024]{1,0:T(8,128)(2,1)S(1)}, u32[]{:S(2)}, u32[]{:S(2)}) collective-permute-start(bf16[256,1024]{1,0:T(8,128)(2,1)S(1)} %shard_map.105), channel_id=1, source_target_pairs={{0,3},{1,0},{2,1},{3,2},{4,7},{5,4},{6,5},{7,6},{8,11},{9,8},{10,9... | collective-permute-start | bytes 1572872 | tf_op jit(solution)/shard_map/ppermute | solution.py:31
  142.3 13.7 %collective-permute-start.37 = (bf16[64,1024]{1,0:T(8,128)(2,1)S(1)}, bf16[64,1024]{1,0:T(8,128)(2,1)S(1)}, u32[]{:S(2)}, u32[]{:S(2)}) collective-permute-start(bf16[64,1024]{1,0:T(8,128)(2,1)S(1)} %get-tuple-element.97), channel_id=1, source_target_pairs={{0,2},{1,3},{2,0},{3,1},{4,6},{5,7},{6,4},{7,5},{8,10},{9,11},{10,... | collective-permute-start | bytes 393224 | tf_op jit(solution)/shard_map/ppermute | solution.py:31
  145.3 19.6 %collective-permute-start.38 = (bf16[64,1024]{1,0:T(8,128)(2,1)S(1)}, bf16[64,1024]{1,0:T(8,128)(2,1)S(1)}, u32[]{:S(2)}, u32[]{:S(2)}) collective-permute-start(bf16[64,1024]{1,0:T(8,128)(2,1)S(1)} %get-tuple-element.98), channel_id=1, source_target_pairs={{0,1},{1,2},{2,3},{3,0},{4,5},{5,6},{6,7},{7,4},{8,9},{9,10},{10,1... | collective-permute-start | bytes 393224 | tf_op jit(solution)/shard_map/ppermute | solution.py:31
  146.7 18.2 %collective-permute-start.39 = (bf16[64,1024]{1,0:T(8,128)(2,1)S(1)}, bf16[64,1024]{1,0:T(8,128)(2,1)S(1)}, u32[]{:S(2)}, u32[]{:S(2)}) collective-permute-start(bf16[64,1024]{1,0:T(8,128)(2,1)S(1)} %get-tuple-element.99), channel_id=1, source_target_pairs={{0,3},{1,0},{2,1},{3,2},{4,7},{5,4},{6,5},{7,6},{8,11},{9,8},{10,9... | collective-permute-start | bytes 393224 | tf_op jit(solution)/shard_map/ppermute | solution.py:31
  154.9 10.8 %collective-permute-start.44 = (bf16[64,1024]{1,0:T(8,128)(2,1)S(1)}, bf16[64,1024]{1,0:T(8,128)(2,1)S(1)}, u32[]{:S(2)}, u32[]{:S(2)}) collective-permute-start(bf16[64,1024]{1,0:T(8,128)(2,1)S(1)} %get-tuple-element.103), channel_id=1, source_target_pairs={{0,8},{1,9},{2,10},{3,11},{4,12},{5,13},{6,14},{7,15},{8,0},{9,1},... | collective-permute-start | bytes 393224 | tf_op jit(solution)/shard_map/ppermute | solution.py:26
  155.7 10.0 %collective-permute-start.45 = (bf16[64,1024]{1,0:T(8,128)(2,1)S(1)}, bf16[64,1024]{1,0:T(8,128)(2,1)S(1)}, u32[]{:S(2)}, u32[]{:S(2)}) collective-permute-start(bf16[64,1024]{1,0:T(8,128)(2,1)S(1)} %get-tuple-element.104), channel_id=1, source_target_pairs={{0,4},{1,5},{2,6},{3,7},{4,8},{5,9},{6,10},{7,11},{8,12},{9,13},{1... | collective-permute-start | bytes 393224 | tf_op jit(solution)/shard_map/ppermute | solution.py:26
  156.0 9.6 %collective-permute-start.46 = (bf16[64,1024]{1,0:T(8,128)(2,1)S(1)}, bf16[64,1024]{1,0:T(8,128)(2,1)S(1)}, u32[]{:S(2)}, u32[]{:S(2)}) collective-permute-start(bf16[64,1024]{1,0:T(8,128)(2,1)S(1)} %get-tuple-element.105), channel_id=1, source_target_pairs={{0,12},{1,13},{2,14},{3,15},{4,0},{5,1},{6,2},{7,3},{8,4},{9,5},{1... | collective-permute-start | bytes 393224 | tf_op jit(solution)/shard_map/ppermute | solution.py:26
  (40 other events, 306.4 us)

commit v2 on v1

--- a/solution.py
+++ b/solution.py
@@ -274,7 +274,7 @@
 def project(z_arg, x_parts, dy_parts, w_qkv, w_out, meanwhile):
     sent = head_products(z_arg, x_parts, dy_parts, w_qkv, w_out, 1, BF16)
     got = {step: swap_cores(sent[step]) for step in (2, 1, 3, 0)}
-    own = head_products(z_arg, x_parts, dy_parts, w_qkv, w_out, 0, F32)
+    own = head_products(z_arg, x_parts, dy_parts, w_qkv, w_out, 0, BF16)
     top, low = first_pieces(z_arg, own[2], got[2])
     top, low = to_z(top, 1), to_z(low, -1)
     one, three = second_pieces(z_arg, own[1], got[1], top, own[3], got[3], low)

time: 167 us -> 167 us (level)
  no operation moved by 1% of the time
where the time goes in v2:
time: 167 us; the launch traced here: 166 us
  starting transfers between devices  58.5 us (35%)
  waiting for transfers between devices  57.8 us (35%)
  Pallas kernels  34 us (20%)
  local copies, waits for them, and re-layouts  14.9 us (9%)
    pallas_call x25, Pallas kernels, call(): pl.pallas_call(wrapped, grid_spec=pltpu.PrefetchScalarGridSpec(num_scalar...  34 us
    ppermute x8, waiting for transfers between devices, to_z(): return lax.ppermute(value, 'row', pairs)  31.6 us
    ppermute x14, starting transfers between devices, to_x(): return lax.ppermute(value, 'col', pairs)  22.9 us
    ppermute x14, starting transfers between devices, to_y(): return lax.ppermute(value, 'col', pairs)  19.9 us
    ppermute x8, starting transfers between devices, to_z(): return lax.ppermute(value, 'row', pairs)  14.1 us
    ppermute x14, waiting for transfers between devices, to_y(): return lax.ppermute(value, 'col', pairs)  13.3 us
    unnamed x50, local copies, waits for them, and re-layouts  11.8 us
    ppermute x14, waiting for transfers between devices, to_x(): return lax.ppermute(value, 'col', pairs)  8.27 us
  transfers between devices with their start and end apart: 47, of which 20 were waited for; matrix products, arithmetic and copies ran while one was open for 2% of the time, Pallas kernels for 14%

profile of v2, /device:TPU:24, one launch (start us, length us, event | category | flops | bytes accessed | tf_op | source)
XLA Modules:
  0.0 166.3 jit_solution(15434941470899487215)
XLA Ops:
  0.6 2.8 %collective-permute-start = (bf16[64,1024]{1,0:T(8,128)(2,1)}, bf16[64,1024]{1,0:T(8,128)(2,1)S(1)}, u32[]{:S(2)}, u32[]{:S(2)}) collective-permute-start(bf16[64,1024]{1,0:T(8,128)(2,1)} %refs_0_), channel_id=1, source_target_pairs={{0,12},{1,13},{2,14},{3,15},{4,0},{5,1},{6,2},{7,3},{8,4},{9,5},{1... | collective-permute-start | bytes 393224 | tf_op jit(solution)/shard_map/ppermute | solution.py:26
  6.8 2.5 %collective-permute-done.refs_1_ = bf16[64,1024]{1,0:T(8,128)(2,1)S(1)} collective-permute-done((bf16[64,1024]{1,0:T(8,128)(2,1)}, bf16[64,1024]{1,0:T(8,128)(2,1)S(1)}, u32[]{:S(2)}, u32[]{:S(2)}) %collective-permute-start) | collective-permute-done | bytes 131104 | tf_op jit(solution)/shard_map/ppermute | solution.py:26
  9.6 2.0 %collective-permute-done.1.refs_2_ = bf16[64,1024]{1,0:T(8,128)(2,1)S(1)} collective-permute-done((bf16[64,1024]{1,0:T(8,128)(2,1)}, bf16[64,1024]{1,0:T(8,128)(2,1)S(1)}, u32[]{:S(2)}, u32[]{:S(2)}) %collective-permute-start.1) | collective-permute-done | bytes 131104 | tf_op jit(solution)/shard_map/ppermute | solution.py:26
  16.3 2.5 %collective-permute-start.7 = (bf16[256,1024]{1,0:T(8,128)(2,1)S(1)}, bf16[256,1024]{1,0:T(8,128)(2,1)S(1)}, u32[]{:S(2)}, u32[]{:S(2)}) collective-permute-start(bf16[256,1024]{1,0:T(8,128)(2,1)S(1)} %shard_map.84.refs_0_.refs_4_), channel_id=1, source_target_pairs={{0,1},{1,2},{2,3},{3,0},{4,5},{5,6},{6,7},{7,4},{8,9},{9,10},{10,1... | collective-permute-start | bytes 1572872 | tf_op jit(solution)/shard_map/ppermute | solution.py:31
  21.4 2.0 %collective-permute-start.10 = (bf16[256,1024]{1,0:T(8,128)(2,1)S(1)}, bf16[256,1024]{1,0:T(8,128)(2,1)S(1)}, u32[]{:S(2)}, u32[]{:S(2)}) collective-permute-start(bf16[256,1024]{1,0:T(8,128)(2,1)S(1)} %shard_map.85.refs_4_.refs_8_.refs_12_), channel_id=1, source_target_pairs={{0,12},{1,13},{2,14},{3,15},{4,0},{5,1},{6,2},{7,3},{8,4},{9,5},{1... | collective-permute-start | bytes 1572872 | tf_op jit(solution)/shard_map/ppermute | solution.py:26
  23.5 4.6 %collective-permute-done.7.refs_3_.refs_7_ = bf16[256,1024]{1,0:T(8,128)(2,1)S(1)} collective-permute-done((bf16[256,1024]{1,0:T(8,128)(2,1)S(1)}, bf16[256,1024]{1,0:T(8,128)(2,1)S(1)}, u32[]{:S(2)}, u32[]{:S(2)}) %collective-permute-start.7) | collective-permute-done | bytes 524320 | tf_op jit(solution)/shard_map/ppermute | solution.py:31
  28.9 3.7 %collective-permute-start.8 = (bf16[128,1024]{1,0:T(8,128)(2,1)}, bf16[128,1024]{1,0:T(8,128)(2,1)S(1)}, u32[]{:S(2)}, u32[]{:S(2)}) collective-permute-start(bf16[128,1024]{1,0:T(8,128)(2,1)} %slice.24), channel_id=1, source_target_pairs={{0,1},{1,2},{2,3},{3,0},{4,5},{5,6},{6,7},{7,4},{8,9},{9,10},{10,1... | collective-permute-start | bytes 786440 | tf_op jit(solution)/shard_map/ppermute | solution.py:31
  35.0 2.1 %collective-permute-start.12 = (bf16[128,1024]{1,0:T(8,128)(2,1)}, bf16[128,1024]{1,0:T(8,128)(2,1)}, u32[]{:S(2)}, u32[]{:S(2)}) collective-permute-start(bf16[128,1024]{1,0:T(8,128)(2,1)} %slice.26), channel_id=1, source_target_pairs={{0,4},{1,5},{2,6},{3,7},{4,8},{5,9},{6,10},{7,11},{8,12},{9,13},{1... | collective-permute-start | bytes 786440 | tf_op jit(solution)/shard_map/ppermute | solution.py:26
  45.7 3.4 %shard_map.88 = (bf16[512,512]{1,0:T(8,128)(2,1)S(1)}, bf16[512,512]{1,0:T(8,128)(2,1)S(1)}, bf16[512,512]{1,0:T(8,128)(2,1)S(1)}, bf16[512,512]{1,0:T(8,128)(2,1)S(1)}) custom-call(s32[1]{0:T(128)} %bitcast.1.scalar_ref, bf16[256,1024]{1,0:T(8,128)(2,1)S(1)} %shard_map.84.refs_0_.refs_4_, bf16[256,1024]{1,0:T(8,128)(2,1)S(1)} %collective-permute-done.6.refs_1_.refs_5_, ...), custom_call_target="tpu_custom_call" | custom-call | flops 2147483648 | bytes 8388608 | tf_op jit(solution)/shard_map/pallas_call | solution.py:82
  49.8 3.3 %shard_map.87 = (bf16[512,512]{1,0:T(8,128)(2,1)S(1)}, bf16[512,512]{1,0:T(8,128)(2,1)S(1)}, bf16[512,512]{1,0:T(8,128)(2,1)S(1)}, bf16[512,512]{1,0:T(8,128)(2,1)S(1)}) custom-call(s32[1]{0:T(128)} %bitcast.1.scalar_ref, bf16[256,1024]{1,0:T(8,128)(2,1)S(1)} %shard_map.84.refs_0_.refs_4_, bf16[256,1024]{1,0:T(8,128)(2,1)S(1)} %collective-permute-done.6.refs_1_.refs_5_, ...), custom_call_target="tpu_custom_call" | custom-call | flops 2147483648 | bytes 8388608 | tf_op jit(solution)/shard_map/pallas_call | solution.py:82
  53.4 2.0 %collective-permute-start.17 = (bf16[256,512]{1,0:T(8,128)(2,1)S(1)}, bf16[256,512]{1,0:T(8,128)(2,1)S(1)}, u32[]{:S(2)}, u32[]{:S(2)}) collective-permute-start(bf16[256,512]{1,0:T(8,128)(2,1)S(1)} %get-tuple-element.80), channel_id=1, source_target_pairs={{0,32},{16,48},{32,64},{48,80},{64,96},{80,112},{96,0},{112,16},{1... | collective-permute-start | bytes 786440 | tf_op jit(solution)/shard_map/ppermute | solution.py:36
  55.3 2.2 %collective-permute-start.19 = (bf16[256,512]{1,0:T(8,128)(2,1)S(1)}, bf16[256,512]{1,0:T(8,128)(2,1)S(1)}, u32[]{:S(2)}, u32[]{:S(2)}) collective-permute-start(bf16[256,512]{1,0:T(8,128)(2,1)S(1)} %get-tuple-element.83), channel_id=1, source_target_pairs={{0,96},{16,112},{32,0},{48,16},{64,32},{80,48},{96,64},{112,80},{1... | collective-permute-start | bytes 786440 | tf_op jit(solution)/shard_map/ppermute | solution.py:36
  57.7 6.6 %collective-permute-done.17.refs_2_ = bf16[256,512]{1,0:T(8,128)(2,1)S(1)} collective-permute-done((bf16[256,512]{1,0:T(8,128)(2,1)S(1)}, bf16[256,512]{1,0:T(8,128)(2,1)S(1)}, u32[]{:S(2)}, u32[]{:S(2)}) %collective-permute-start.17) | collective-permute-done | bytes 262176 | tf_op jit(solution)/shard_map/ppermute | solution.py:36
  66.0 2.0 %collective-permute-start.21 = (bf16[512,512]{1,0:T(8,128)(2,1)S(1)}, bf16[512,512]{1,0:T(8,128)(2,1)S(1)}, u32[]{:S(2)}, u32[]{:S(2)}) collective-permute-start(bf16[512,512]{1,0:T(8,128)(2,1)S(1)} %get-tuple-element.85), channel_id=1, source_target_pairs={{0,96},{16,112},{32,0},{48,16},{64,32},{80,48},{96,64},{112,80},{1... | collective-permute-start | bytes 1572872 | tf_op jit(solution)/shard_map/ppermute | solution.py:36
  68.0 3.1 %shard_map.91 = (bf16[1024,1024]{1,0:T(8,128)(2,1)S(1)}, bf16[1024,1024]{1,0:T(8,128)(2,1)S(1)}) custom-call(s32[1]{0:T(128)} %bitcast.1.scalar_ref, bf16[256,1024]{1,0:T(8,128)(2,1)S(1)} %copy-done.5, bf16[256,1024]{1,0:T(8,128)(2,1)S(1)} %copy-done.9, bf16[128,1024]{1,0:T(8,128)(2,1)S(1)} %collective-permute-done.8.refs_2_, ...), custom_call_target="tpu_custom_call" | custom-call | bytes 8388608 | tf_op jit(solution)/shard_map/pallas_call | solution.py:82
  72.4 7.2 %collective-permute-done.20.refs_2_ = bf16[512,512]{1,0:T(8,128)(2,1)S(1)} collective-permute-done((bf16[512,512]{1,0:T(8,128)(2,1)S(1)}, bf16[512,512]{1,0:T(8,128)(2,1)S(1)}, u32[]{:S(2)}, u32[]{:S(2)}) %collective-permute-start.20) | collective-permute-done | bytes 524320 | tf_op jit(solution)/shard_map/ppermute | solution.py:36
  84.1 4.5 %shard_map.93 = (bf16[512,128]{1,0:T(8,128)(2,1)S(1)}, bf16[512,128]{1,0:T(8,128)(2,1)S(1)}, f32[512,256]{1,0:T(8,128)S(1)}, bf16[512,256]{1,0:T(8,128)(2,1)S(1)}) custom-call(s32[11]{0:T(128)S(1)} %pad_add_fusion.scalar_ref, bf16[512,512]{1,0:T(8,128)(2,1)S(1)} %copy-done.23, bf16[512,256]{1,0:T(8,128)(2,1)S(1)} %collective-permute-done.22.refs_1_), custom_call_target="tpu_custom_call" | custom-call | flops 939524096 | bytes 4194304 | tf_op jit(solution)/shard_map/pallas_call | solution.py:82
  91.4 2.2 %collective-permute-start.24 = (bf16[512,512]{1,0:T(8,128)(2,1)S(1)}, bf16[512,512]{1,0:T(8,128)(2,1)S(1)}, u32[]{:S(2)}, u32[]{:S(2)}) collective-permute-start(bf16[512,512]{1,0:T(8,128)(2,1)S(1)} %shard_map.94.refs_0_.refs_1_), channel_id=1, source_target_pairs={{0,96},{16,112},{32,0},{48,16},{64,32},{80,48},{96,64},{112,80},{1... | collective-permute-start | bytes 1572872 | tf_op jit(solution)/shard_map/ppermute | solution.py:36
  93.6 11.9 %collective-permute-done.25.refs_4_.refs_3_.refs_5_ = bf16[512,512]{1,0:T(8,128)(2,1)S(1)} collective-permute-done((bf16[512,512]{1,0:T(8,128)(2,1)S(1)}, bf16[512,512]{1,0:T(8,128)(2,1)S(1)}, u32[]{:S(2)}, u32[]{:S(2)}) %collective-permute-start.25) | collective-permute-done | bytes 524320 | tf_op jit(solution)/shard_map/ppermute | solution.py:36
  106.3 3.2 %collective-permute-start.27 = (bf16[256,512]{1,0:T(8,128)(2,1)S(1)}, bf16[256,512]{1,0:T(8,128)(2,1)S(1)}, u32[]{:S(2)}, u32[]{:S(2)}) collective-permute-start(bf16[256,512]{1,0:T(8,128)(2,1)S(1)} %slice.29), channel_id=1, source_target_pairs={{0,96},{16,112},{32,0},{48,16},{64,32},{80,48},{96,64},{112,80},{1... | collective-permute-start | bytes 786440 | tf_op jit(solution)/shard_map/ppermute | solution.py:36
  109.5 4.9 %collective-permute-done.26.refs_2_.refs_3_ = bf16[256,512]{1,0:T(8,128)(2,1)S(1)} collective-permute-done((bf16[256,512]{1,0:T(8,128)(2,1)S(1)}, bf16[256,512]{1,0:T(8,128)(2,1)S(1)}, u32[]{:S(2)}, u32[]{:S(2)}) %collective-permute-start.26) | collective-permute-done | bytes 262176 | tf_op jit(solution)/shard_map/ppermute | solution.py:36
  118.2 2.5 %collective-permute-start.35 = (bf16[128,1024]{1,0:T(8,128)(2,1)S(1)}, bf16[128,1024]{1,0:T(8,128)(2,1)S(1)}, u32[]{:S(2)}, u32[]{:S(2)}) collective-permute-start(bf16[128,1024]{1,0:T(8,128)(2,1)S(1)} %get-tuple-element.95), channel_id=1, source_target_pairs={{0,12},{1,13},{2,14},{3,15},{4,0},{5,1},{6,2},{7,3},{8,4},{9,5},{1... | collective-permute-start | bytes 786440 | tf_op jit(solution)/shard_map/ppermute | solution.py:26
  121.7 3.3 %collective-permute-start.40 = (bf16[128,1024]{1,0:T(8,128)(2,1)S(1)}, bf16[128,1024]{1,0:T(8,128)(2,1)S(1)}, u32[]{:S(2)}, u32[]{:S(2)}) collective-permute-start(bf16[128,1024]{1,0:T(8,128)(2,1)S(1)} %get-tuple-element.100), channel_id=1, source_target_pairs={{0,1},{1,2},{2,3},{3,0},{4,5},{5,6},{6,7},{7,4},{8,9},{9,10},{10,1... | collective-permute-start | bytes 786440 | tf_op jit(solution)/shard_map/ppermute | solution.py:31
  125.0 2.0 %collective-permute-done.33.refs_14_ = bf16[128,1024]{1,0:T(8,128)(2,1)S(1)} collective-permute-done((bf16[128,1024]{1,0:T(8,128)(2,1)S(1)}, bf16[128,1024]{1,0:T(8,128)(2,1)S(1)}, u32[]{:S(2)}, u32[]{:S(2)}) %collective-permute-start.33) | collective-permute-done | bytes 262176 | tf_op jit(solution)/shard_map/ppermute | solution.py:26
  128.0 3.3 %collective-permute-start.36 = (bf16[256,1024]{1,0:T(8,128)(2,1)S(1)}, bf16[256,1024]{1,0:T(8,128)(2,1)S(1)}, u32[]{:S(2)}, u32[]{:S(2)}) collective-permute-start(bf16[256,1024]{1,0:T(8,128)(2,1)S(1)} %shard_map.99), channel_id=1, source_target_pairs={{0,12},{1,13},{2,14},{3,15},{4,0},{5,1},{6,2},{7,3},{8,4},{9,5},{1... | collective-permute-start | bytes 1572872 | tf_op jit(solution)/shard_map/ppermute | solution.py:26
  132.3 3.3 %collective-permute-start.41 = (bf16[256,1024]{1,0:T(8,128)(2,1)S(1)}, bf16[256,1024]{1,0:T(8,128)(2,1)S(1)}, u32[]{:S(2)}, u32[]{:S(2)}) collective-permute-start(bf16[256,1024]{1,0:T(8,128)(2,1)S(1)} %shard_map.104), channel_id=1, source_target_pairs={{0,1},{1,2},{2,3},{3,0},{4,5},{5,6},{6,7},{7,4},{8,9},{9,10},{10,1... | collective-permute-start | bytes 1572872 | tf_op jit(solution)/shard_map/ppermute | solution.py:31
  136.8 2.9 %shard_map.95.refs_14_ = f32[512,1024]{1,0:T(8,128)} custom-call(s32[1]{0:T(128)} %bitcast.1.scalar_ref, bf16[512,512]{1,0:T(8,128)(2,1)S(1)} %shard_map.94.refs_0_.refs_1_, bf16[512,512]{1,0:T(8,128)(2,1)S(1)} %collective-permute-done.24.refs_1_.refs_2_, bf16[256,512]{1,0:T(8,128)(2,1)S(1)} %collective-permute-done.26.refs_2_.refs_3_, ...), custom_call_target="tpu_custom_call" | custom-call | flops 1073741824 | bytes 5242880 | tf_op jit(solution)/shard_map/pallas_call | solution.py:82
  142.0 2.0 %collective-permute-start.37 = (bf16[64,1024]{1,0:T(8,128)(2,1)S(1)}, bf16[64,1024]{1,0:T(8,128)(2,1)S(1)}, u32[]{:S(2)}, u32[]{:S(2)}) collective-permute-start(bf16[64,1024]{1,0:T(8,128)(2,1)S(1)} %get-tuple-element.97), channel_id=1, source_target_pairs={{0,2},{1,3},{2,0},{3,1},{4,6},{5,7},{6,4},{7,5},{8,10},{9,11},{10,... | collective-permute-start | bytes 393224 | tf_op jit(solution)/shard_map/ppermute | solution.py:31
  147.4 2.6 %collective-permute-done.41.refs_1_ = bf16[256,1024]{1,0:T(8,128)(2,1)S(1)} collective-permute-done((bf16[256,1024]{1,0:T(8,128)(2,1)S(1)}, bf16[256,1024]{1,0:T(8,128)(2,1)S(1)}, u32[]{:S(2)}, u32[]{:S(2)}) %collective-permute-start.41) | collective-permute-done | bytes 524320 | tf_op jit(solution)/shard_map/ppermute | solution.py:31
  150.0 4.5 %collective-permute-done.43.refs_2_ = bf16[256,1024]{1,0:T(8,128)(2,1)S(1)} collective-permute-done((bf16[256,1024]{1,0:T(8,128)(2,1)S(1)}, bf16[256,1024]{1,0:T(8,128)(2,1)S(1)}, u32[]{:S(2)}, u32[]{:S(2)}) %collective-permute-start.43) | collective-permute-done | bytes 524320 | tf_op jit(solution)/shard_map/ppermute | solution.py:31
  156.1 2.8 %collective-permute-start.46 = (bf16[64,1024]{1,0:T(8,128)(2,1)S(1)}, bf16[64,1024]{1,0:T(8,128)(2,1)S(1)}, u32[]{:S(2)}, u32[]{:S(2)}) collective-permute-start(bf16[64,1024]{1,0:T(8,128)(2,1)S(1)} %get-tuple-element.105), channel_id=1, source_target_pairs={{0,12},{1,13},{2,14},{3,15},{4,0},{5,1},{6,2},{7,3},{8,4},{9,5},{1... | collective-permute-start | bytes 393224 | tf_op jit(solution)/shard_map/ppermute | solution.py:26
  158.9 6.0 %shard_map.108 = f32[3,1024,512]{2,1,0:T(8,128)} custom-call(s32[1]{0:T(128)} %bitcast.1.scalar_ref, bf16[1024,1024]{1,0:T(8,128)(2,1)S(1)} %get-tuple-element.86.refs_4_.refs_0_, bf16[512,512]{1,0:T(8,128)(2,1)S(1)} %shard_map.94.refs_0_.refs_1_, bf16[512,512]{1,0:T(8,128)(2,1)S(1)} %collective-permute-done.24.refs_1_.refs_2_, ...), custom_call_target="tpu_custom_call" | custom-call | flops 3221225472 | bytes 12582912 | tf_op jit(solution)/shard_map/pallas_call | solution.py:82
  (144 shorter events, 51.4 us)
Async XLA Ops:
  15.5 17.1 %collective-permute-start.6 = (bf16[256,1024]{1,0:T(8,128)(2,1)S(1)}, bf16[256,1024]{1,0:T(8,128)(2,1)S(1)}, u32[]{:S(2)}, u32[]{:S(2)}) collective-permute-start(bf16[256,1024]{1,0:T(8,128)(2,1)S(1)} %shard_map.84.refs_0_.refs_4_), channel_id=1, source_target_pairs={{0,3},{1,0},{2,1},{3,2},{4,7},{5,4},{6,5},{7,6},{8,11},{9,8},{10,9... | collective-permute-start | bytes 1572872 | tf_op jit(solution)/shard_map/ppermute | solution.py:31
  16.3 11.8 %collective-permute-start.7 = (bf16[256,1024]{1,0:T(8,128)(2,1)S(1)}, bf16[256,1024]{1,0:T(8,128)(2,1)S(1)}, u32[]{:S(2)}, u32[]{:S(2)}) collective-permute-start(bf16[256,1024]{1,0:T(8,128)(2,1)S(1)} %shard_map.84.refs_0_.refs_4_), channel_id=1, source_target_pairs={{0,1},{1,2},{2,3},{3,0},{4,5},{5,6},{6,7},{7,4},{8,9},{9,10},{10,1... | collective-permute-start | bytes 1572872 | tf_op jit(solution)/shard_map/ppermute | solution.py:31
  19.8 13.7 %collective-permute-start.11 = (bf16[256,1024]{1,0:T(8,128)(2,1)S(1)}, bf16[256,1024]{1,0:T(8,128)(2,1)S(1)}, u32[]{:S(2)}, u32[]{:S(2)}) collective-permute-start(bf16[256,1024]{1,0:T(8,128)(2,1)S(1)} %shard_map.85.refs_4_.refs_8_.refs_12_), channel_id=1, source_target_pairs={{0,4},{1,5},{2,6},{3,7},{4,8},{5,9},{6,10},{7,11},{8,12},{9,13},{1... | collective-permute-start | bytes 1572872 | tf_op jit(solution)/shard_map/ppermute | solution.py:26
  21.4 15.6 %collective-permute-start.10 = (bf16[256,1024]{1,0:T(8,128)(2,1)S(1)}, bf16[256,1024]{1,0:T(8,128)(2,1)S(1)}, u32[]{:S(2)}, u32[]{:S(2)}) collective-permute-start(bf16[256,1024]{1,0:T(8,128)(2,1)S(1)} %shard_map.85.refs_4_.refs_8_.refs_12_), channel_id=1, source_target_pairs={{0,12},{1,13},{2,14},{3,15},{4,0},{5,1},{6,2},{7,3},{8,4},{9,5},{1... | collective-permute-start | bytes 1572872 | tf_op jit(solution)/shard_map/ppermute | solution.py:26
  28.9 16.8 %collective-permute-start.8 = (bf16[128,1024]{1,0:T(8,128)(2,1)}, bf16[128,1024]{1,0:T(8,128)(2,1)S(1)}, u32[]{:S(2)}, u32[]{:S(2)}) collective-permute-start(bf16[128,1024]{1,0:T(8,128)(2,1)} %slice.24), channel_id=1, source_target_pairs={{0,1},{1,2},{2,3},{3,0},{4,5},{5,6},{6,7},{7,4},{8,9},{9,10},{10,1... | collective-permute-start | bytes 786440 | tf_op jit(solution)/shard_map/ppermute | solution.py:31
  33.4 12.3 %collective-permute-start.9 = (bf16[128,1024]{1,0:T(8,128)(2,1)}, bf16[128,1024]{1,0:T(8,128)(2,1)}, u32[]{:S(2)}, u32[]{:S(2)}) collective-permute-start(bf16[128,1024]{1,0:T(8,128)(2,1)} %slice.25), channel_id=1, source_target_pairs={{0,3},{1,0},{2,1},{3,2},{4,7},{5,4},{6,5},{7,6},{8,11},{9,8},{10,9... | collective-permute-start | bytes 786440 | tf_op jit(solution)/shard_map/ppermute | solution.py:31
  35.0 10.6 %collective-permute-start.12 = (bf16[128,1024]{1,0:T(8,128)(2,1)}, bf16[128,1024]{1,0:T(8,128)(2,1)}, u32[]{:S(2)}, u32[]{:S(2)}) collective-permute-start(bf16[128,1024]{1,0:T(8,128)(2,1)} %slice.26), channel_id=1, source_target_pairs={{0,4},{1,5},{2,6},{3,7},{4,8},{5,9},{6,10},{7,11},{8,12},{9,13},{1... | collective-permute-start | bytes 786440 | tf_op jit(solution)/shard_map/ppermute | solution.py:26
  53.4 11.0 %collective-permute-start.17 = (bf16[256,512]{1,0:T(8,128)(2,1)S(1)}, bf16[256,512]{1,0:T(8,128)(2,1)S(1)}, u32[]{:S(2)}, u32[]{:S(2)}) collective-permute-start(bf16[256,512]{1,0:T(8,128)(2,1)S(1)} %get-tuple-element.80), channel_id=1, source_target_pairs={{0,32},{16,48},{32,64},{48,80},{64,96},{80,112},{96,0},{112,16},{1... | collective-permute-start | bytes 786440 | tf_op jit(solution)/shard_map/ppermute | solution.py:36
  55.3 9.0 %collective-permute-start.19 = (bf16[256,512]{1,0:T(8,128)(2,1)S(1)}, bf16[256,512]{1,0:T(8,128)(2,1)S(1)}, u32[]{:S(2)}, u32[]{:S(2)}) collective-permute-start(bf16[256,512]{1,0:T(8,128)(2,1)S(1)} %get-tuple-element.83), channel_id=1, source_target_pairs={{0,96},{16,112},{32,0},{48,16},{64,32},{80,48},{96,64},{112,80},{1... | collective-permute-start | bytes 786440 | tf_op jit(solution)/shard_map/ppermute | solution.py:36
  57.5 14.9 %collective-permute-start.14 = (bf16[512,512]{1,0:T(8,128)(2,1)S(1)}, bf16[512,512]{1,0:T(8,128)(2,1)S(1)}, u32[]{:S(2)}, u32[]{:S(2)}) collective-permute-start(bf16[512,512]{1,0:T(8,128)(2,1)S(1)} %get-tuple-element.75), channel_id=1, source_target_pairs={{0,16},{16,0},{32,48},{48,32},{64,80},{80,64},{96,112},{112,96},{1... | collective-permute-start | bytes 1572872 | tf_op jit(solution)/shard_map/ppermute | solution.py:41
  64.6 14.9 %collective-permute-start.20 = (bf16[512,512]{1,0:T(8,128)(2,1)S(1)}, bf16[512,512]{1,0:T(8,128)(2,1)S(1)}, u32[]{:S(2)}, u32[]{:S(2)}) collective-permute-start(bf16[512,512]{1,0:T(8,128)(2,1)S(1)} %get-tuple-element.84), channel_id=1, source_target_pairs={{0,32},{16,48},{32,64},{48,80},{64,96},{80,112},{96,0},{112,16},{1... | collective-permute-start | bytes 1572872 | tf_op jit(solution)/shard_map/ppermute | solution.py:36
  66.0 13.6 %collective-permute-start.21 = (bf16[512,512]{1,0:T(8,128)(2,1)S(1)}, bf16[512,512]{1,0:T(8,128)(2,1)S(1)}, u32[]{:S(2)}, u32[]{:S(2)}) collective-permute-start(bf16[512,512]{1,0:T(8,128)(2,1)S(1)} %get-tuple-element.85), channel_id=1, source_target_pairs={{0,96},{16,112},{32,0},{48,16},{64,32},{80,48},{96,64},{112,80},{1... | collective-permute-start | bytes 1572872 | tf_op jit(solution)/shard_map/ppermute | solution.py:36
  90.3 15.3 %collective-permute-start.25 = (bf16[512,512]{1,0:T(8,128)(2,1)S(1)}, bf16[512,512]{1,0:T(8,128)(2,1)S(1)}, u32[]{:S(2)}, u32[]{:S(2)}) collective-permute-start(bf16[512,512]{1,0:T(8,128)(2,1)S(1)} %shard_map.94.refs_0_.refs_1_), channel_id=1, source_target_pairs={{0,32},{16,48},{32,64},{48,80},{64,96},{80,112},{96,0},{112,16},{1... | collective-permute-start | bytes 1572872 | tf_op jit(solution)/shard_map/ppermute | solution.py:36
  91.4 14.3 %collective-permute-start.24 = (bf16[512,512]{1,0:T(8,128)(2,1)S(1)}, bf16[512,512]{1,0:T(8,128)(2,1)S(1)}, u32[]{:S(2)}, u32[]{:S(2)}) collective-permute-start(bf16[512,512]{1,0:T(8,128)(2,1)S(1)} %shard_map.94.refs_0_.refs_1_), channel_id=1, source_target_pairs={{0,96},{16,112},{32,0},{48,16},{64,32},{80,48},{96,64},{112,80},{1... | collective-permute-start | bytes 1572872 | tf_op jit(solution)/shard_map/ppermute | solution.py:36
  93.6 21.7 %collective-permute-start.28 = (bf16[512,512]{1,0:T(8,128)(2,1)S(1)}, bf16[512,512]{1,0:T(8,128)(2,1)S(1)}, u32[]{:S(2)}, u32[]{:S(2)}) collective-permute-start(bf16[512,512]{1,0:T(8,128)(2,1)S(1)} %shard_map.94.refs_0_.refs_1_), channel_id=1, source_target_pairs={{0,16},{16,0},{32,48},{48,32},{64,80},{80,64},{96,112},{112,96},{1... | collective-permute-start | bytes 1572872 | tf_op jit(solution)/shard_map/ppermute | solution.py:41
  105.7 9.6 %collective-permute-start.29 = (bf16[512,512]{1,0:T(8,128)(2,1)S(1)}, bf16[512,512]{1,0:T(8,128)(2,1)S(1)}, u32[]{:S(2)}, u32[]{:S(2)}) collective-permute-start(bf16[512,512]{1,0:T(8,128)(2,1)S(1)} %collective-permute-done.24.refs_1_.refs_2_), channel_id=1, source_target_pairs={{0,16},{16,0},{32,48},{48,32},{64,80},{80,64},{96,112},{112,96},{1... | collective-permute-start | bytes 1572872 | tf_op jit(solution)/shard_map/ppermute | solution.py:41
  105.8 9.5 %collective-permute-start.32 = (bf16[512,512]{1,0:T(8,128)(2,1)S(1)}, bf16[512,512]{1,0:T(8,128)(2,1)S(1)}, u32[]{:S(2)}, u32[]{:S(2)}) collective-permute-start(bf16[512,512]{1,0:T(8,128)(2,1)S(1)} %collective-permute-done.25.refs_4_.refs_3_.refs_5_), channel_id=1, source_target_pairs={{0,16},{16,0},{32,48},{48,32},{64,80},{80,64},{96,112},{112,96},{1... | collective-permute-start | bytes 1572872 | tf_op jit(solution)/shard_map/ppermute | solution.py:41
  106.3 9.0 %collective-permute-start.27 = (bf16[256,512]{1,0:T(8,128)(2,1)S(1)}, bf16[256,512]{1,0:T(8,128)(2,1)S(1)}, u32[]{:S(2)}, u32[]{:S(2)}) collective-permute-start(bf16[256,512]{1,0:T(8,128)(2,1)S(1)} %slice.29), channel_id=1, source_target_pairs={{0,96},{16,112},{32,0},{48,16},{64,32},{80,48},{96,64},{112,80},{1... | collective-permute-start | bytes 786440 | tf_op jit(solution)/shard_map/ppermute | solution.py:36
  117.4 9.6 %collective-permute-start.33 = (bf16[128,1024]{1,0:T(8,128)(2,1)S(1)}, bf16[128,1024]{1,0:T(8,128)(2,1)S(1)}, u32[]{:S(2)}, u32[]{:S(2)}) collective-permute-start(bf16[128,1024]{1,0:T(8,128)(2,1)S(1)} %get-tuple-element.94), channel_id=1, source_target_pairs={{0,4},{1,5},{2,6},{3,7},{4,8},{5,9},{6,10},{7,11},{8,12},{9,13},{1... | collective-permute-start | bytes 786440 | tf_op jit(solution)/shard_map/ppermute | solution.py:26
  118.2 9.4 %collective-permute-start.35 = (bf16[128,1024]{1,0:T(8,128)(2,1)S(1)}, bf16[128,1024]{1,0:T(8,128)(2,1)S(1)}, u32[]{:S(2)}, u32[]{:S(2)}) collective-permute-start(bf16[128,1024]{1,0:T(8,128)(2,1)S(1)} %get-tuple-element.95), channel_id=1, source_target_pairs={{0,12},{1,13},{2,14},{3,15},{4,0},{5,1},{6,2},{7,3},{8,4},{9,5},{1... | collective-permute-start | bytes 786440 | tf_op jit(solution)/shard_map/ppermute | solution.py:26
  121.7 9.6 %collective-permute-start.40 = (bf16[128,1024]{1,0:T(8,128)(2,1)S(1)}, bf16[128,1024]{1,0:T(8,128)(2,1)S(1)}, u32[]{:S(2)}, u32[]{:S(2)}) collective-permute-start(bf16[128,1024]{1,0:T(8,128)(2,1)S(1)} %get-tuple-element.100), channel_id=1, source_target_pairs={{0,1},{1,2},{2,3},{3,0},{4,5},{5,6},{6,7},{7,4},{8,9},{9,10},{10,1... | collective-permute-start | bytes 786440 | tf_op jit(solution)/shard_map/ppermute | solution.py:31
  125.0 10.7 %collective-permute-start.42 = (bf16[128,1024]{1,0:T(8,128)(2,1)S(1)}, bf16[128,1024]{1,0:T(8,128)(2,1)S(1)}, u32[]{:S(2)}, u32[]{:S(2)}) collective-permute-start(bf16[128,1024]{1,0:T(8,128)(2,1)S(1)} %get-tuple-element.101), channel_id=1, source_target_pairs={{0,3},{1,0},{2,1},{3,2},{4,7},{5,4},{6,5},{7,6},{8,11},{9,8},{10,9... | collective-permute-start | bytes 786440 | tf_op jit(solution)/shard_map/ppermute | solution.py:31
  127.5 14.4 %collective-permute-start.34 = (bf16[256,1024]{1,0:T(8,128)(2,1)S(1)}, bf16[256,1024]{1,0:T(8,128)(2,1)S(1)}, u32[]{:S(2)}, u32[]{:S(2)}) collective-permute-start(bf16[256,1024]{1,0:T(8,128)(2,1)S(1)} %shard_map.98), channel_id=1, source_target_pairs={{0,4},{1,5},{2,6},{3,7},{4,8},{5,9},{6,10},{7,11},{8,12},{9,13},{1... | collective-permute-start | bytes 1572872 | tf_op jit(solution)/shard_map/ppermute | solution.py:26
  128.0 13.8 %collective-permute-start.36 = (bf16[256,1024]{1,0:T(8,128)(2,1)S(1)}, bf16[256,1024]{1,0:T(8,128)(2,1)S(1)}, u32[]{:S(2)}, u32[]{:S(2)}) collective-permute-start(bf16[256,1024]{1,0:T(8,128)(2,1)S(1)} %shard_map.99), channel_id=1, source_target_pairs={{0,12},{1,13},{2,14},{3,15},{4,0},{5,1},{6,2},{7,3},{8,4},{9,5},{1... | collective-permute-start | bytes 1572872 | tf_op jit(solution)/shard_map/ppermute | solution.py:26
  132.3 17.6 %collective-permute-start.41 = (bf16[256,1024]{1,0:T(8,128)(2,1)S(1)}, bf16[256,1024]{1,0:T(8,128)(2,1)S(1)}, u32[]{:S(2)}, u32[]{:S(2)}) collective-permute-start(bf16[256,1024]{1,0:T(8,128)(2,1)S(1)} %shard_map.104), channel_id=1, source_target_pairs={{0,1},{1,2},{2,3},{3,0},{4,5},{5,6},{6,7},{7,4},{8,9},{9,10},{10,1... | collective-permute-start | bytes 1572872 | tf_op jit(solution)/shard_map/ppermute | solution.py:31
  136.7 17.8 %collective-permute-start.43 = (bf16[256,1024]{1,0:T(8,128)(2,1)S(1)}, bf16[256,1024]{1,0:T(8,128)(2,1)S(1)}, u32[]{:S(2)}, u32[]{:S(2)}) collective-permute-start(bf16[256,1024]{1,0:T(8,128)(2,1)S(1)} %shard_map.105), channel_id=1, source_target_pairs={{0,3},{1,0},{2,1},{3,2},{4,7},{5,4},{6,5},{7,6},{8,11},{9,8},{10,9... | collective-permute-start | bytes 1572872 | tf_op jit(solution)/shard_map/ppermute | solution.py:31
  142.0 14.1 %collective-permute-start.37 = (bf16[64,1024]{1,0:T(8,128)(2,1)S(1)}, bf16[64,1024]{1,0:T(8,128)(2,1)S(1)}, u32[]{:S(2)}, u32[]{:S(2)}) collective-permute-start(bf16[64,1024]{1,0:T(8,128)(2,1)S(1)} %get-tuple-element.97), channel_id=1, source_target_pairs={{0,2},{1,3},{2,0},{3,1},{4,6},{5,7},{6,4},{7,5},{8,10},{9,11},{10,... | collective-permute-start | bytes 393224 | tf_op jit(solution)/shard_map/ppermute | solution.py:31
  145.0 19.8 %collective-permute-start.38 = (bf16[64,1024]{1,0:T(8,128)(2,1)S(1)}, bf16[64,1024]{1,0:T(8,128)(2,1)S(1)}, u32[]{:S(2)}, u32[]{:S(2)}) collective-permute-start(bf16[64,1024]{1,0:T(8,128)(2,1)S(1)} %get-tuple-element.98), channel_id=1, source_target_pairs={{0,1},{1,2},{2,3},{3,0},{4,5},{5,6},{6,7},{7,4},{8,9},{9,10},{10,1... | collective-permute-start | bytes 393224 | tf_op jit(solution)/shard_map/ppermute | solution.py:31
  146.4 18.4 %collective-permute-start.39 = (bf16[64,1024]{1,0:T(8,128)(2,1)S(1)}, bf16[64,1024]{1,0:T(8,128)(2,1)S(1)}, u32[]{:S(2)}, u32[]{:S(2)}) collective-permute-start(bf16[64,1024]{1,0:T(8,128)(2,1)S(1)} %get-tuple-element.99), channel_id=1, source_target_pairs={{0,3},{1,0},{2,1},{3,2},{4,7},{5,4},{6,5},{7,6},{8,11},{9,8},{10,9... | collective-permute-start | bytes 393224 | tf_op jit(solution)/shard_map/ppermute | solution.py:31
  154.6 11.0 %collective-permute-start.44 = (bf16[64,1024]{1,0:T(8,128)(2,1)S(1)}, bf16[64,1024]{1,0:T(8,128)(2,1)S(1)}, u32[]{:S(2)}, u32[]{:S(2)}) collective-permute-start(bf16[64,1024]{1,0:T(8,128)(2,1)S(1)} %get-tuple-element.103), channel_id=1, source_target_pairs={{0,8},{1,9},{2,10},{3,11},{4,12},{5,13},{6,14},{7,15},{8,0},{9,1},... | collective-permute-start | bytes 393224 | tf_op jit(solution)/shard_map/ppermute | solution.py:26
  155.6 10.0 %collective-permute-start.45 = (bf16[64,1024]{1,0:T(8,128)(2,1)S(1)}, bf16[64,1024]{1,0:T(8,128)(2,1)S(1)}, u32[]{:S(2)}, u32[]{:S(2)}) collective-permute-start(bf16[64,1024]{1,0:T(8,128)(2,1)S(1)} %get-tuple-element.104), channel_id=1, source_target_pairs={{0,4},{1,5},{2,6},{3,7},{4,8},{5,9},{6,10},{7,11},{8,12},{9,13},{1... | collective-permute-start | bytes 393224 | tf_op jit(solution)/shard_map/ppermute | solution.py:26
  156.1 9.5 %collective-permute-start.46 = (bf16[64,1024]{1,0:T(8,128)(2,1)S(1)}, bf16[64,1024]{1,0:T(8,128)(2,1)S(1)}, u32[]{:S(2)}, u32[]{:S(2)}) collective-permute-start(bf16[64,1024]{1,0:T(8,128)(2,1)S(1)} %get-tuple-element.105), channel_id=1, source_target_pairs={{0,12},{1,13},{2,14},{3,15},{4,0},{5,1},{6,2},{7,3},{8,4},{9,5},{1... | collective-permute-start | bytes 393224 | tf_op jit(solution)/shard_map/ppermute | solution.py:26
  (40 other events, 306.1 us)

commit v3 on v1

--- a/solution.py
+++ b/solution.py
@@ -215,7 +215,7 @@
         [whole(o) for o in outs],
         flops=2 * tokens * depth * width * RING,
         moved=8 * MIB,
-        limit=24,
+        limit=16,
     )
 
 

time: 167 us -> 167 us (level)
  no operation moved by 1% of the time
where the time goes in v3:
time: 167 us; the launch traced here: 166 us
  starting transfers between devices  58.7 us (35%)
  waiting for transfers between devices  57.8 us (35%)
  Pallas kernels  33.9 us (20%)
  local copies, waits for them, and re-layouts  14.9 us (9%)
    pallas_call x25, Pallas kernels, call(): pl.pallas_call(wrapped, grid_spec=pltpu.PrefetchScalarGridSpec(num_scalar...  33.9 us
    ppermute x8, waiting for transfers between devices, to_z(): return lax.ppermute(value, 'row', pairs)  31.6 us
    ppermute x14, starting transfers between devices, to_x(): return lax.ppermute(value, 'col', pairs)  22.9 us
    ppermute x14, starting transfers between devices, to_y(): return lax.ppermute(value, 'col', pairs)  19.9 us
    ppermute x8, starting transfers between devices, to_z(): return lax.ppermute(value, 'row', pairs)  14.3 us
    ppermute x14, waiting for transfers between devices, to_y(): return lax.ppermute(value, 'col', pairs)  13.3 us
    unnamed x50, local copies, waits for them, and re-layouts  11.8 us
    ppermute x14, waiting for transfers between devices, to_x(): return lax.ppermute(value, 'col', pairs)  8.26 us
  transfers between devices with their start and end apart: 47, of which 20 were waited for; matrix products, arithmetic and copies ran while one was open for 2% of the time, Pallas kernels for 14%

profile of v3, /device:TPU:24, one launch (start us, length us, event | category | flops | bytes accessed | tf_op | source)
XLA Modules:
  0.0 166.4 jit_solution(1543162828931299803)
XLA Ops:
  0.6 2.8 %collective-permute-start = (bf16[64,1024]{1,0:T(8,128)(2,1)}, bf16[64,1024]{1,0:T(8,128)(2,1)S(1)}, u32[]{:S(2)}, u32[]{:S(2)}) collective-permute-start(bf16[64,1024]{1,0:T(8,128)(2,1)} %refs_0_), channel_id=1, source_target_pairs={{0,12},{1,13},{2,14},{3,15},{4,0},{5,1},{6,2},{7,3},{8,4},{9,5},{1... | collective-permute-start | bytes 393224 | tf_op jit(solution)/shard_map/ppermute | solution.py:26
  6.8 2.5 %collective-permute-done.refs_1_ = bf16[64,1024]{1,0:T(8,128)(2,1)S(1)} collective-permute-done((bf16[64,1024]{1,0:T(8,128)(2,1)}, bf16[64,1024]{1,0:T(8,128)(2,1)S(1)}, u32[]{:S(2)}, u32[]{:S(2)}) %collective-permute-start) | collective-permute-done | bytes 131104 | tf_op jit(solution)/shard_map/ppermute | solution.py:26
  9.6 2.0 %collective-permute-done.1.refs_2_ = bf16[64,1024]{1,0:T(8,128)(2,1)S(1)} collective-permute-done((bf16[64,1024]{1,0:T(8,128)(2,1)}, bf16[64,1024]{1,0:T(8,128)(2,1)S(1)}, u32[]{:S(2)}, u32[]{:S(2)}) %collective-permute-start.1) | collective-permute-done | bytes 131104 | tf_op jit(solution)/shard_map/ppermute | solution.py:26
  16.3 2.5 %collective-permute-start.7 = (bf16[256,1024]{1,0:T(8,128)(2,1)S(1)}, bf16[256,1024]{1,0:T(8,128)(2,1)S(1)}, u32[]{:S(2)}, u32[]{:S(2)}) collective-permute-start(bf16[256,1024]{1,0:T(8,128)(2,1)S(1)} %shard_map.84.refs_0_.refs_4_), channel_id=1, source_target_pairs={{0,1},{1,2},{2,3},{3,0},{4,5},{5,6},{6,7},{7,4},{8,9},{9,10},{10,1... | collective-permute-start | bytes 1572872 | tf_op jit(solution)/shard_map/ppermute | solution.py:31
  21.4 2.0 %collective-permute-start.10 = (bf16[256,1024]{1,0:T(8,128)(2,1)S(1)}, bf16[256,1024]{1,0:T(8,128)(2,1)S(1)}, u32[]{:S(2)}, u32[]{:S(2)}) collective-permute-start(bf16[256,1024]{1,0:T(8,128)(2,1)S(1)} %shard_map.85.refs_4_.refs_8_.refs_12_), channel_id=1, source_target_pairs={{0,12},{1,13},{2,14},{3,15},{4,0},{5,1},{6,2},{7,3},{8,4},{9,5},{1... | collective-permute-start | bytes 1572872 | tf_op jit(solution)/shard_map/ppermute | solution.py:26
  23.5 4.6 %collective-permute-done.7.refs_3_.refs_7_ = bf16[256,1024]{1,0:T(8,128)(2,1)S(1)} collective-permute-done((bf16[256,1024]{1,0:T(8,128)(2,1)S(1)}, bf16[256,1024]{1,0:T(8,128)(2,1)S(1)}, u32[]{:S(2)}, u32[]{:S(2)}) %collective-permute-start.7) | collective-permute-done | bytes 524320 | tf_op jit(solution)/shard_map/ppermute | solution.py:31
  28.9 3.7 %collective-permute-start.8 = (bf16[128,1024]{1,0:T(8,128)(2,1)}, bf16[128,1024]{1,0:T(8,128)(2,1)S(1)}, u32[]{:S(2)}, u32[]{:S(2)}) collective-permute-start(bf16[128,1024]{1,0:T(8,128)(2,1)} %slice.24), channel_id=1, source_target_pairs={{0,1},{1,2},{2,3},{3,0},{4,5},{5,6},{6,7},{7,4},{8,9},{9,10},{10,1... | collective-permute-start | bytes 786440 | tf_op jit(solution)/shard_map/ppermute | solution.py:31
  35.0 2.1 %collective-permute-start.12 = (bf16[128,1024]{1,0:T(8,128)(2,1)}, bf16[128,1024]{1,0:T(8,128)(2,1)}, u32[]{:S(2)}, u32[]{:S(2)}) collective-permute-start(bf16[128,1024]{1,0:T(8,128)(2,1)} %slice.26), channel_id=1, source_target_pairs={{0,4},{1,5},{2,6},{3,7},{4,8},{5,9},{6,10},{7,11},{8,12},{9,13},{1... | collective-permute-start | bytes 786440 | tf_op jit(solution)/shard_map/ppermute | solution.py:26
  45.7 3.4 %shard_map.88 = (bf16[512,512]{1,0:T(8,128)(2,1)S(1)}, bf16[512,512]{1,0:T(8,128)(2,1)S(1)}, bf16[512,512]{1,0:T(8,128)(2,1)S(1)}, bf16[512,512]{1,0:T(8,128)(2,1)S(1)}) custom-call(s32[1]{0:T(128)} %bitcast.1.scalar_ref, bf16[256,1024]{1,0:T(8,128)(2,1)S(1)} %shard_map.84.refs_0_.refs_4_, bf16[256,1024]{1,0:T(8,128)(2,1)S(1)} %collective-permute-done.6.refs_1_.refs_5_, ...), custom_call_target="tpu_custom_call" | custom-call | flops 2147483648 | bytes 8388608 | tf_op jit(solution)/shard_map/pallas_call | solution.py:82
  49.8 3.3 %shard_map.87 = (f32[512,512]{1,0:T(8,128)S(1)}, f32[512,512]{1,0:T(8,128)S(1)}, f32[512,512]{1,0:T(8,128)S(1)}, f32[512,512]{1,0:T(8,128)S(1)}) custom-call(s32[1]{0:T(128)} %bitcast.1.scalar_ref, bf16[256,1024]{1,0:T(8,128)(2,1)S(1)} %shard_map.84.refs_0_.refs_4_, bf16[256,1024]{1,0:T(8,128)(2,1)S(1)} %collective-permute-done.6.refs_1_.refs_5_, ...), custom_call_target="tpu_custom_call" | custom-call | flops 2147483648 | bytes 8388608 | tf_op jit(solution)/shard_map/pallas_call | solution.py:82
  53.3 2.0 %collective-permute-start.17 = (bf16[256,512]{1,0:T(8,128)(2,1)S(1)}, bf16[256,512]{1,0:T(8,128)(2,1)S(1)}, u32[]{:S(2)}, u32[]{:S(2)}) collective-permute-start(bf16[256,512]{1,0:T(8,128)(2,1)S(1)} %get-tuple-element.80), channel_id=1, source_target_pairs={{0,32},{16,48},{32,64},{48,80},{64,96},{80,112},{96,0},{112,16},{1... | collective-permute-start | bytes 786440 | tf_op jit(solution)/shard_map/ppermute | solution.py:36
  55.3 2.2 %collective-permute-start.19 = (bf16[256,512]{1,0:T(8,128)(2,1)S(1)}, bf16[256,512]{1,0:T(8,128)(2,1)S(1)}, u32[]{:S(2)}, u32[]{:S(2)}) collective-permute-start(bf16[256,512]{1,0:T(8,128)(2,1)S(1)} %get-tuple-element.83), channel_id=1, source_target_pairs={{0,96},{16,112},{32,0},{48,16},{64,32},{80,48},{96,64},{112,80},{1... | collective-permute-start | bytes 786440 | tf_op jit(solution)/shard_map/ppermute | solution.py:36
  57.7 6.6 %collective-permute-done.17.refs_2_ = bf16[256,512]{1,0:T(8,128)(2,1)S(1)} collective-permute-done((bf16[256,512]{1,0:T(8,128)(2,1)S(1)}, bf16[256,512]{1,0:T(8,128)(2,1)S(1)}, u32[]{:S(2)}, u32[]{:S(2)}) %collective-permute-start.17) | collective-permute-done | bytes 262176 | tf_op jit(solution)/shard_map/ppermute | solution.py:36
  66.1 2.0 %collective-permute-start.21 = (bf16[512,512]{1,0:T(8,128)(2,1)S(1)}, bf16[512,512]{1,0:T(8,128)(2,1)S(1)}, u32[]{:S(2)}, u32[]{:S(2)}) collective-permute-start(bf16[512,512]{1,0:T(8,128)(2,1)S(1)} %get-tuple-element.85), channel_id=1, source_target_pairs={{0,96},{16,112},{32,0},{48,16},{64,32},{80,48},{96,64},{112,80},{1... | collective-permute-start | bytes 1572872 | tf_op jit(solution)/shard_map/ppermute | solution.py:36
  68.1 3.1 %shard_map.91 = (bf16[1024,1024]{1,0:T(8,128)(2,1)S(1)}, bf16[1024,1024]{1,0:T(8,128)(2,1)S(1)}) custom-call(s32[1]{0:T(128)} %bitcast.1.scalar_ref, bf16[256,1024]{1,0:T(8,128)(2,1)S(1)} %copy-done.5, bf16[256,1024]{1,0:T(8,128)(2,1)S(1)} %copy-done.9, bf16[128,1024]{1,0:T(8,128)(2,1)S(1)} %collective-permute-done.8.refs_2_, ...), custom_call_target="tpu_custom_call" | custom-call | bytes 8388608 | tf_op jit(solution)/shard_map/pallas_call | solution.py:82
  72.5 7.2 %collective-permute-done.20.refs_2_ = bf16[512,512]{1,0:T(8,128)(2,1)S(1)} collective-permute-done((bf16[512,512]{1,0:T(8,128)(2,1)S(1)}, bf16[512,512]{1,0:T(8,128)(2,1)S(1)}, u32[]{:S(2)}, u32[]{:S(2)}) %collective-permute-start.20) | collective-permute-done | bytes 524320 | tf_op jit(solution)/shard_map/ppermute | solution.py:36
  84.2 4.5 %shard_map.93 = (bf16[512,128]{1,0:T(8,128)(2,1)S(1)}, bf16[512,128]{1,0:T(8,128)(2,1)S(1)}, f32[512,256]{1,0:T(8,128)S(1)}, bf16[512,256]{1,0:T(8,128)(2,1)S(1)}) custom-call(s32[11]{0:T(128)S(1)} %pad_add_fusion.scalar_ref, bf16[512,512]{1,0:T(8,128)(2,1)S(1)} %copy-done.23, bf16[512,256]{1,0:T(8,128)(2,1)S(1)} %collective-permute-done.22.refs_1_), custom_call_target="tpu_custom_call" | custom-call | flops 939524096 | bytes 4194304 | tf_op jit(solution)/shard_map/pallas_call | solution.py:82
  91.5 2.2 %collective-permute-start.24 = (bf16[512,512]{1,0:T(8,128)(2,1)S(1)}, bf16[512,512]{1,0:T(8,128)(2,1)S(1)}, u32[]{:S(2)}, u32[]{:S(2)}) collective-permute-start(bf16[512,512]{1,0:T(8,128)(2,1)S(1)} %shard_map.94.refs_0_.refs_1_), channel_id=1, source_target_pairs={{0,96},{16,112},{32,0},{48,16},{64,32},{80,48},{96,64},{112,80},{1... | collective-permute-start | bytes 1572872 | tf_op jit(solution)/shard_map/ppermute | solution.py:36
  93.7 11.9 %collective-permute-done.25.refs_4_.refs_3_.refs_5_ = bf16[512,512]{1,0:T(8,128)(2,1)S(1)} collective-permute-done((bf16[512,512]{1,0:T(8,128)(2,1)S(1)}, bf16[512,512]{1,0:T(8,128)(2,1)S(1)}, u32[]{:S(2)}, u32[]{:S(2)}) %collective-permute-start.25) | collective-permute-done | bytes 524320 | tf_op jit(solution)/shard_map/ppermute | solution.py:36
  106.4 3.2 %collective-permute-start.27 = (bf16[256,512]{1,0:T(8,128)(2,1)S(1)}, bf16[256,512]{1,0:T(8,128)(2,1)S(1)}, u32[]{:S(2)}, u32[]{:S(2)}) collective-permute-start(bf16[256,512]{1,0:T(8,128)(2,1)S(1)} %slice.29), channel_id=1, source_target_pairs={{0,96},{16,112},{32,0},{48,16},{64,32},{80,48},{96,64},{112,80},{1... | collective-permute-start | bytes 786440 | tf_op jit(solution)/shard_map/ppermute | solution.py:36
  109.6 4.9 %collective-permute-done.26.refs_2_.refs_3_ = bf16[256,512]{1,0:T(8,128)(2,1)S(1)} collective-permute-done((bf16[256,512]{1,0:T(8,128)(2,1)S(1)}, bf16[256,512]{1,0:T(8,128)(2,1)S(1)}, u32[]{:S(2)}, u32[]{:S(2)}) %collective-permute-start.26) | collective-permute-done | bytes 262176 | tf_op jit(solution)/shard_map/ppermute | solution.py:36
  118.3 2.5 %collective-permute-start.35 = (bf16[128,1024]{1,0:T(8,128)(2,1)S(1)}, bf16[128,1024]{1,0:T(8,128)(2,1)S(1)}, u32[]{:S(2)}, u32[]{:S(2)}) collective-permute-start(bf16[128,1024]{1,0:T(8,128)(2,1)S(1)} %get-tuple-element.95), channel_id=1, source_target_pairs={{0,12},{1,13},{2,14},{3,15},{4,0},{5,1},{6,2},{7,3},{8,4},{9,5},{1... | collective-permute-start | bytes 786440 | tf_op jit(solution)/shard_map/ppermute | solution.py:26
  121.7 3.3 %collective-permute-start.40 = (bf16[128,1024]{1,0:T(8,128)(2,1)S(1)}, bf16[128,1024]{1,0:T(8,128)(2,1)S(1)}, u32[]{:S(2)}, u32[]{:S(2)}) collective-permute-start(bf16[128,1024]{1,0:T(8,128)(2,1)S(1)} %get-tuple-element.100), channel_id=1, source_target_pairs={{0,1},{1,2},{2,3},{3,0},{4,5},{5,6},{6,7},{7,4},{8,9},{9,10},{10,1... | collective-permute-start | bytes 786440 | tf_op jit(solution)/shard_map/ppermute | solution.py:31
  125.1 2.0 %collective-permute-done.33.refs_14_ = bf16[128,1024]{1,0:T(8,128)(2,1)S(1)} collective-permute-done((bf16[128,1024]{1,0:T(8,128)(2,1)S(1)}, bf16[128,1024]{1,0:T(8,128)(2,1)S(1)}, u32[]{:S(2)}, u32[]{:S(2)}) %collective-permute-start.33) | collective-permute-done | bytes 262176 | tf_op jit(solution)/shard_map/ppermute | solution.py:26
  128.3 3.3 %collective-permute-start.36 = (bf16[256,1024]{1,0:T(8,128)(2,1)S(1)}, bf16[256,1024]{1,0:T(8,128)(2,1)S(1)}, u32[]{:S(2)}, u32[]{:S(2)}) collective-permute-start(bf16[256,1024]{1,0:T(8,128)(2,1)S(1)} %shard_map.99), channel_id=1, source_target_pairs={{0,12},{1,13},{2,14},{3,15},{4,0},{5,1},{6,2},{7,3},{8,4},{9,5},{1... | collective-permute-start | bytes 1572872 | tf_op jit(solution)/shard_map/ppermute | solution.py:26
  132.6 3.3 %collective-permute-start.41 = (bf16[256,1024]{1,0:T(8,128)(2,1)S(1)}, bf16[256,1024]{1,0:T(8,128)(2,1)S(1)}, u32[]{:S(2)}, u32[]{:S(2)}) collective-permute-start(bf16[256,1024]{1,0:T(8,128)(2,1)S(1)} %shard_map.104), channel_id=1, source_target_pairs={{0,1},{1,2},{2,3},{3,0},{4,5},{5,6},{6,7},{7,4},{8,9},{9,10},{10,1... | collective-permute-start | bytes 1572872 | tf_op jit(solution)/shard_map/ppermute | solution.py:31
  137.0 2.9 %shard_map.95.refs_14_ = f32[512,1024]{1,0:T(8,128)} custom-call(s32[1]{0:T(128)} %bitcast.1.scalar_ref, bf16[512,512]{1,0:T(8,128)(2,1)S(1)} %shard_map.94.refs_0_.refs_1_, bf16[512,512]{1,0:T(8,128)(2,1)S(1)} %collective-permute-done.24.refs_1_.refs_2_, bf16[256,512]{1,0:T(8,128)(2,1)S(1)} %collective-permute-done.26.refs_2_.refs_3_, ...), custom_call_target="tpu_custom_call" | custom-call | flops 1073741824 | bytes 5242880 | tf_op jit(solution)/shard_map/pallas_call | solution.py:82
  142.3 2.0 %collective-permute-start.37 = (bf16[64,1024]{1,0:T(8,128)(2,1)S(1)}, bf16[64,1024]{1,0:T(8,128)(2,1)S(1)}, u32[]{:S(2)}, u32[]{:S(2)}) collective-permute-start(bf16[64,1024]{1,0:T(8,128)(2,1)S(1)} %get-tuple-element.97), channel_id=1, source_target_pairs={{0,2},{1,3},{2,0},{3,1},{4,6},{5,7},{6,4},{7,5},{8,10},{9,11},{10,... | collective-permute-start | bytes 393224 | tf_op jit(solution)/shard_map/ppermute | solution.py:31
  147.6 2.6 %collective-permute-done.41.refs_1_ = bf16[256,1024]{1,0:T(8,128)(2,1)S(1)} collective-permute-done((bf16[256,1024]{1,0:T(8,128)(2,1)S(1)}, bf16[256,1024]{1,0:T(8,128)(2,1)S(1)}, u32[]{:S(2)}, u32[]{:S(2)}) %collective-permute-start.41) | collective-permute-done | bytes 524320 | tf_op jit(solution)/shard_map/ppermute | solution.py:31
  150.3 4.5 %collective-permute-done.43.refs_2_ = bf16[256,1024]{1,0:T(8,128)(2,1)S(1)} collective-permute-done((bf16[256,1024]{1,0:T(8,128)(2,1)S(1)}, bf16[256,1024]{1,0:T(8,128)(2,1)S(1)}, u32[]{:S(2)}, u32[]{:S(2)}) %collective-permute-start.43) | collective-permute-done | bytes 524320 | tf_op jit(solution)/shard_map/ppermute | solution.py:31
  156.0 2.9 %collective-permute-start.46 = (bf16[64,1024]{1,0:T(8,128)(2,1)S(1)}, bf16[64,1024]{1,0:T(8,128)(2,1)S(1)}, u32[]{:S(2)}, u32[]{:S(2)}) collective-permute-start(bf16[64,1024]{1,0:T(8,128)(2,1)S(1)} %get-tuple-element.105), channel_id=1, source_target_pairs={{0,12},{1,13},{2,14},{3,15},{4,0},{5,1},{6,2},{7,3},{8,4},{9,5},{1... | collective-permute-start | bytes 393224 | tf_op jit(solution)/shard_map/ppermute | solution.py:26
  158.9 6.0 %shard_map.108 = f32[3,1024,512]{2,1,0:T(8,128)} custom-call(s32[1]{0:T(128)} %bitcast.1.scalar_ref, bf16[1024,1024]{1,0:T(8,128)(2,1)S(1)} %get-tuple-element.86.refs_4_.refs_0_, bf16[512,512]{1,0:T(8,128)(2,1)S(1)} %shard_map.94.refs_0_.refs_1_, bf16[512,512]{1,0:T(8,128)(2,1)S(1)} %collective-permute-done.24.refs_1_.refs_2_, ...), custom_call_target="tpu_custom_call" | custom-call | flops 3221225472 | bytes 12582912 | tf_op jit(solution)/shard_map/pallas_call | solution.py:82
  (144 shorter events, 51.3 us)
Async XLA Ops:
  15.5 17.1 %collective-permute-start.6 = (bf16[256,1024]{1,0:T(8,128)(2,1)S(1)}, bf16[256,1024]{1,0:T(8,128)(2,1)S(1)}, u32[]{:S(2)}, u32[]{:S(2)}) collective-permute-start(bf16[256,1024]{1,0:T(8,128)(2,1)S(1)} %shard_map.84.refs_0_.refs_4_), channel_id=1, source_target_pairs={{0,3},{1,0},{2,1},{3,2},{4,7},{5,4},{6,5},{7,6},{8,11},{9,8},{10,9... | collective-permute-start | bytes 1572872 | tf_op jit(solution)/shard_map/ppermute | solution.py:31
  16.3 11.8 %collective-permute-start.7 = (bf16[256,1024]{1,0:T(8,128)(2,1)S(1)}, bf16[256,1024]{1,0:T(8,128)(2,1)S(1)}, u32[]{:S(2)}, u32[]{:S(2)}) collective-permute-start(bf16[256,1024]{1,0:T(8,128)(2,1)S(1)} %shard_map.84.refs_0_.refs_4_), channel_id=1, source_target_pairs={{0,1},{1,2},{2,3},{3,0},{4,5},{5,6},{6,7},{7,4},{8,9},{9,10},{10,1... | collective-permute-start | bytes 1572872 | tf_op jit(solution)/shard_map/ppermute | solution.py:31
  19.8 13.7 %collective-permute-start.11 = (bf16[256,1024]{1,0:T(8,128)(2,1)S(1)}, bf16[256,1024]{1,0:T(8,128)(2,1)S(1)}, u32[]{:S(2)}, u32[]{:S(2)}) collective-permute-start(bf16[256,1024]{1,0:T(8,128)(2,1)S(1)} %shard_map.85.refs_4_.refs_8_.refs_12_), channel_id=1, source_target_pairs={{0,4},{1,5},{2,6},{3,7},{4,8},{5,9},{6,10},{7,11},{8,12},{9,13},{1... | collective-permute-start | bytes 1572872 | tf_op jit(solution)/shard_map/ppermute | solution.py:26
  21.4 15.6 %collective-permute-start.10 = (bf16[256,1024]{1,0:T(8,128)(2,1)S(1)}, bf16[256,1024]{1,0:T(8,128)(2,1)S(1)}, u32[]{:S(2)}, u32[]{:S(2)}) collective-permute-start(bf16[256,1024]{1,0:T(8,128)(2,1)S(1)} %shard_map.85.refs_4_.refs_8_.refs_12_), channel_id=1, source_target_pairs={{0,12},{1,13},{2,14},{3,15},{4,0},{5,1},{6,2},{7,3},{8,4},{9,5},{1... | collective-permute-start | bytes 1572872 | tf_op jit(solution)/shard_map/ppermute | solution.py:26
  28.9 16.8 %collective-permute-start.8 = (bf16[128,1024]{1,0:T(8,128)(2,1)}, bf16[128,1024]{1,0:T(8,128)(2,1)S(1)}, u32[]{:S(2)}, u32[]{:S(2)}) collective-permute-start(bf16[128,1024]{1,0:T(8,128)(2,1)} %slice.24), channel_id=1, source_target_pairs={{0,1},{1,2},{2,3},{3,0},{4,5},{5,6},{6,7},{7,4},{8,9},{9,10},{10,1... | collective-permute-start | bytes 786440 | tf_op jit(solution)/shard_map/ppermute | solution.py:31
  33.4 12.3 %collective-permute-start.9 = (bf16[128,1024]{1,0:T(8,128)(2,1)}, bf16[128,1024]{1,0:T(8,128)(2,1)}, u32[]{:S(2)}, u32[]{:S(2)}) collective-permute-start(bf16[128,1024]{1,0:T(8,128)(2,1)} %slice.25), channel_id=1, source_target_pairs={{0,3},{1,0},{2,1},{3,2},{4,7},{5,4},{6,5},{7,6},{8,11},{9,8},{10,9... | collective-permute-start | bytes 786440 | tf_op jit(solution)/shard_map/ppermute | solution.py:31
  35.0 10.6 %collective-permute-start.12 = (bf16[128,1024]{1,0:T(8,128)(2,1)}, bf16[128,1024]{1,0:T(8,128)(2,1)}, u32[]{:S(2)}, u32[]{:S(2)}) collective-permute-start(bf16[128,1024]{1,0:T(8,128)(2,1)} %slice.26), channel_id=1, source_target_pairs={{0,4},{1,5},{2,6},{3,7},{4,8},{5,9},{6,10},{7,11},{8,12},{9,13},{1... | collective-permute-start | bytes 786440 | tf_op jit(solution)/shard_map/ppermute | solution.py:26
  53.3 11.0 %collective-permute-start.17 = (bf16[256,512]{1,0:T(8,128)(2,1)S(1)}, bf16[256,512]{1,0:T(8,128)(2,1)S(1)}, u32[]{:S(2)}, u32[]{:S(2)}) collective-permute-start(bf16[256,512]{1,0:T(8,128)(2,1)S(1)} %get-tuple-element.80), channel_id=1, source_target_pairs={{0,32},{16,48},{32,64},{48,80},{64,96},{80,112},{96,0},{112,16},{1... | collective-permute-start | bytes 786440 | tf_op jit(solution)/shard_map/ppermute | solution.py:36
  55.3 9.0 %collective-permute-start.19 = (bf16[256,512]{1,0:T(8,128)(2,1)S(1)}, bf16[256,512]{1,0:T(8,128)(2,1)S(1)}, u32[]{:S(2)}, u32[]{:S(2)}) collective-permute-start(bf16[256,512]{1,0:T(8,128)(2,1)S(1)} %get-tuple-element.83), channel_id=1, source_target_pairs={{0,96},{16,112},{32,0},{48,16},{64,32},{80,48},{96,64},{112,80},{1... | collective-permute-start | bytes 786440 | tf_op jit(solution)/shard_map/ppermute | solution.py:36
  57.5 15.0 %collective-permute-start.14 = (bf16[512,512]{1,0:T(8,128)(2,1)S(1)}, bf16[512,512]{1,0:T(8,128)(2,1)S(1)}, u32[]{:S(2)}, u32[]{:S(2)}) collective-permute-start(bf16[512,512]{1,0:T(8,128)(2,1)S(1)} %get-tuple-element.75), channel_id=1, source_target_pairs={{0,16},{16,0},{32,48},{48,32},{64,80},{80,64},{96,112},{112,96},{1... | collective-permute-start | bytes 1572872 | tf_op jit(solution)/shard_map/ppermute | solution.py:41
  64.6 15.1 %collective-permute-start.20 = (bf16[512,512]{1,0:T(8,128)(2,1)S(1)}, bf16[512,512]{1,0:T(8,128)(2,1)S(1)}, u32[]{:S(2)}, u32[]{:S(2)}) collective-permute-start(bf16[512,512]{1,0:T(8,128)(2,1)S(1)} %get-tuple-element.84), channel_id=1, source_target_pairs={{0,32},{16,48},{32,64},{48,80},{64,96},{80,112},{96,0},{112,16},{1... | collective-permute-start | bytes 1572872 | tf_op jit(solution)/shard_map/ppermute | solution.py:36
  66.1 13.6 %collective-permute-start.21 = (bf16[512,512]{1,0:T(8,128)(2,1)S(1)}, bf16[512,512]{1,0:T(8,128)(2,1)S(1)}, u32[]{:S(2)}, u32[]{:S(2)}) collective-permute-start(bf16[512,512]{1,0:T(8,128)(2,1)S(1)} %get-tuple-element.85), channel_id=1, source_target_pairs={{0,96},{16,112},{32,0},{48,16},{64,32},{80,48},{96,64},{112,80},{1... | collective-permute-start | bytes 1572872 | tf_op jit(solution)/shard_map/ppermute | solution.py:36
  90.4 15.2 %collective-permute-start.25 = (bf16[512,512]{1,0:T(8,128)(2,1)S(1)}, bf16[512,512]{1,0:T(8,128)(2,1)S(1)}, u32[]{:S(2)}, u32[]{:S(2)}) collective-permute-start(bf16[512,512]{1,0:T(8,128)(2,1)S(1)} %shard_map.94.refs_0_.refs_1_), channel_id=1, source_target_pairs={{0,32},{16,48},{32,64},{48,80},{64,96},{80,112},{96,0},{112,16},{1... | collective-permute-start | bytes 1572872 | tf_op jit(solution)/shard_map/ppermute | solution.py:36
  91.5 14.3 %collective-permute-start.24 = (bf16[512,512]{1,0:T(8,128)(2,1)S(1)}, bf16[512,512]{1,0:T(8,128)(2,1)S(1)}, u32[]{:S(2)}, u32[]{:S(2)}) collective-permute-start(bf16[512,512]{1,0:T(8,128)(2,1)S(1)} %shard_map.94.refs_0_.refs_1_), channel_id=1, source_target_pairs={{0,96},{16,112},{32,0},{48,16},{64,32},{80,48},{96,64},{112,80},{1... | collective-permute-start | bytes 1572872 | tf_op jit(solution)/shard_map/ppermute | solution.py:36
  93.7 21.7 %collective-permute-start.28 = (bf16[512,512]{1,0:T(8,128)(2,1)S(1)}, bf16[512,512]{1,0:T(8,128)(2,1)S(1)}, u32[]{:S(2)}, u32[]{:S(2)}) collective-permute-start(bf16[512,512]{1,0:T(8,128)(2,1)S(1)} %shard_map.94.refs_0_.refs_1_), channel_id=1, source_target_pairs={{0,16},{16,0},{32,48},{48,32},{64,80},{80,64},{96,112},{112,96},{1... | collective-permute-start | bytes 1572872 | tf_op jit(solution)/shard_map/ppermute | solution.py:41
  105.8 9.6 %collective-permute-start.29 = (bf16[512,512]{1,0:T(8,128)(2,1)S(1)}, bf16[512,512]{1,0:T(8,128)(2,1)S(1)}, u32[]{:S(2)}, u32[]{:S(2)}) collective-permute-start(bf16[512,512]{1,0:T(8,128)(2,1)S(1)} %collective-permute-done.24.refs_1_.refs_2_), channel_id=1, source_target_pairs={{0,16},{16,0},{32,48},{48,32},{64,80},{80,64},{96,112},{112,96},{1... | collective-permute-start | bytes 1572872 | tf_op jit(solution)/shard_map/ppermute | solution.py:41
  105.9 9.5 %collective-permute-start.32 = (bf16[512,512]{1,0:T(8,128)(2,1)S(1)}, bf16[512,512]{1,0:T(8,128)(2,1)S(1)}, u32[]{:S(2)}, u32[]{:S(2)}) collective-permute-start(bf16[512,512]{1,0:T(8,128)(2,1)S(1)} %collective-permute-done.25.refs_4_.refs_3_.refs_5_), channel_id=1, source_target_pairs={{0,16},{16,0},{32,48},{48,32},{64,80},{80,64},{96,112},{112,96},{1... | collective-permute-start | bytes 1572872 | tf_op jit(solution)/shard_map/ppermute | solution.py:41
  106.4 9.0 %collective-permute-start.27 = (bf16[256,512]{1,0:T(8,128)(2,1)S(1)}, bf16[256,512]{1,0:T(8,128)(2,1)S(1)}, u32[]{:S(2)}, u32[]{:S(2)}) collective-permute-start(bf16[256,512]{1,0:T(8,128)(2,1)S(1)} %slice.29), channel_id=1, source_target_pairs={{0,96},{16,112},{32,0},{48,16},{64,32},{80,48},{96,64},{112,80},{1... | collective-permute-start | bytes 786440 | tf_op jit(solution)/shard_map/ppermute | solution.py:36
  117.4 9.6 %collective-permute-start.33 = (bf16[128,1024]{1,0:T(8,128)(2,1)S(1)}, bf16[128,1024]{1,0:T(8,128)(2,1)S(1)}, u32[]{:S(2)}, u32[]{:S(2)}) collective-permute-start(bf16[128,1024]{1,0:T(8,128)(2,1)S(1)} %get-tuple-element.94), channel_id=1, source_target_pairs={{0,4},{1,5},{2,6},{3,7},{4,8},{5,9},{6,10},{7,11},{8,12},{9,13},{1... | collective-permute-start | bytes 786440 | tf_op jit(solution)/shard_map/ppermute | solution.py:26
  118.3 9.6 %collective-permute-start.35 = (bf16[128,1024]{1,0:T(8,128)(2,1)S(1)}, bf16[128,1024]{1,0:T(8,128)(2,1)S(1)}, u32[]{:S(2)}, u32[]{:S(2)}) collective-permute-start(bf16[128,1024]{1,0:T(8,128)(2,1)S(1)} %get-tuple-element.95), channel_id=1, source_target_pairs={{0,12},{1,13},{2,14},{3,15},{4,0},{5,1},{6,2},{7,3},{8,4},{9,5},{1... | collective-permute-start | bytes 786440 | tf_op jit(solution)/shard_map/ppermute | solution.py:26
  121.7 9.9 %collective-permute-start.40 = (bf16[128,1024]{1,0:T(8,128)(2,1)S(1)}, bf16[128,1024]{1,0:T(8,128)(2,1)S(1)}, u32[]{:S(2)}, u32[]{:S(2)}) collective-permute-start(bf16[128,1024]{1,0:T(8,128)(2,1)S(1)} %get-tuple-element.100), channel_id=1, source_target_pairs={{0,1},{1,2},{2,3},{3,0},{4,5},{5,6},{6,7},{7,4},{8,9},{9,10},{10,1... | collective-permute-start | bytes 786440 | tf_op jit(solution)/shard_map/ppermute | solution.py:31
  125.1 10.9 %collective-permute-start.42 = (bf16[128,1024]{1,0:T(8,128)(2,1)S(1)}, bf16[128,1024]{1,0:T(8,128)(2,1)S(1)}, u32[]{:S(2)}, u32[]{:S(2)}) collective-permute-start(bf16[128,1024]{1,0:T(8,128)(2,1)S(1)} %get-tuple-element.101), channel_id=1, source_target_pairs={{0,3},{1,0},{2,1},{3,2},{4,7},{5,4},{6,5},{7,6},{8,11},{9,8},{10,9... | collective-permute-start | bytes 786440 | tf_op jit(solution)/shard_map/ppermute | solution.py:31
  127.5 14.6 %collective-permute-start.34 = (bf16[256,1024]{1,0:T(8,128)(2,1)S(1)}, bf16[256,1024]{1,0:T(8,128)(2,1)S(1)}, u32[]{:S(2)}, u32[]{:S(2)}) collective-permute-start(bf16[256,1024]{1,0:T(8,128)(2,1)S(1)} %shard_map.98), channel_id=1, source_target_pairs={{0,4},{1,5},{2,6},{3,7},{4,8},{5,9},{6,10},{7,11},{8,12},{9,13},{1... | collective-permute-start | bytes 1572872 | tf_op jit(solution)/shard_map/ppermute | solution.py:26
  128.3 13.8 %collective-permute-start.36 = (bf16[256,1024]{1,0:T(8,128)(2,1)S(1)}, bf16[256,1024]{1,0:T(8,128)(2,1)S(1)}, u32[]{:S(2)}, u32[]{:S(2)}) collective-permute-start(bf16[256,1024]{1,0:T(8,128)(2,1)S(1)} %shard_map.99), channel_id=1, source_target_pairs={{0,12},{1,13},{2,14},{3,15},{4,0},{5,1},{6,2},{7,3},{8,4},{9,5},{1... | collective-permute-start | bytes 1572872 | tf_op jit(solution)/shard_map/ppermute | solution.py:26
  132.6 17.6 %collective-permute-start.41 = (bf16[256,1024]{1,0:T(8,128)(2,1)S(1)}, bf16[256,1024]{1,0:T(8,128)(2,1)S(1)}, u32[]{:S(2)}, u32[]{:S(2)}) collective-permute-start(bf16[256,1024]{1,0:T(8,128)(2,1)S(1)} %shard_map.104), channel_id=1, source_target_pairs={{0,1},{1,2},{2,3},{3,0},{4,5},{5,6},{6,7},{7,4},{8,9},{9,10},{10,1... | collective-permute-start | bytes 1572872 | tf_op jit(solution)/shard_map/ppermute | solution.py:31
  136.9 17.8 %collective-permute-start.43 = (bf16[256,1024]{1,0:T(8,128)(2,1)S(1)}, bf16[256,1024]{1,0:T(8,128)(2,1)S(1)}, u32[]{:S(2)}, u32[]{:S(2)}) collective-permute-start(bf16[256,1024]{1,0:T(8,128)(2,1)S(1)} %shard_map.105), channel_id=1, source_target_pairs={{0,3},{1,0},{2,1},{3,2},{4,7},{5,4},{6,5},{7,6},{8,11},{9,8},{10,9... | collective-permute-start | bytes 1572872 | tf_op jit(solution)/shard_map/ppermute | solution.py:31
  142.3 13.7 %collective-permute-start.37 = (bf16[64,1024]{1,0:T(8,128)(2,1)S(1)}, bf16[64,1024]{1,0:T(8,128)(2,1)S(1)}, u32[]{:S(2)}, u32[]{:S(2)}) collective-permute-start(bf16[64,1024]{1,0:T(8,128)(2,1)S(1)} %get-tuple-element.97), channel_id=1, source_target_pairs={{0,2},{1,3},{2,0},{3,1},{4,6},{5,7},{6,4},{7,5},{8,10},{9,11},{10,... | collective-permute-start | bytes 393224 | tf_op jit(solution)/shard_map/ppermute | solution.py:31
  145.3 19.6 %collective-permute-start.38 = (bf16[64,1024]{1,0:T(8,128)(2,1)S(1)}, bf16[64,1024]{1,0:T(8,128)(2,1)S(1)}, u32[]{:S(2)}, u32[]{:S(2)}) collective-permute-start(bf16[64,1024]{1,0:T(8,128)(2,1)S(1)} %get-tuple-element.98), channel_id=1, source_target_pairs={{0,1},{1,2},{2,3},{3,0},{4,5},{5,6},{6,7},{7,4},{8,9},{9,10},{10,1... | collective-permute-start | bytes 393224 | tf_op jit(solution)/shard_map/ppermute | solution.py:31
  146.7 18.2 %collective-permute-start.39 = (bf16[64,1024]{1,0:T(8,128)(2,1)S(1)}, bf16[64,1024]{1,0:T(8,128)(2,1)S(1)}, u32[]{:S(2)}, u32[]{:S(2)}) collective-permute-start(bf16[64,1024]{1,0:T(8,128)(2,1)S(1)} %get-tuple-element.99), channel_id=1, source_target_pairs={{0,3},{1,0},{2,1},{3,2},{4,7},{5,4},{6,5},{7,6},{8,11},{9,8},{10,9... | collective-permute-start | bytes 393224 | tf_op jit(solution)/shard_map/ppermute | solution.py:31
  154.9 10.8 %collective-permute-start.44 = (bf16[64,1024]{1,0:T(8,128)(2,1)S(1)}, bf16[64,1024]{1,0:T(8,128)(2,1)S(1)}, u32[]{:S(2)}, u32[]{:S(2)}) collective-permute-start(bf16[64,1024]{1,0:T(8,128)(2,1)S(1)} %get-tuple-element.103), channel_id=1, source_target_pairs={{0,8},{1,9},{2,10},{3,11},{4,12},{5,13},{6,14},{7,15},{8,0},{9,1},... | collective-permute-start | bytes 393224 | tf_op jit(solution)/shard_map/ppermute | solution.py:26
  155.7 10.0 %collective-permute-start.45 = (bf16[64,1024]{1,0:T(8,128)(2,1)S(1)}, bf16[64,1024]{1,0:T(8,128)(2,1)S(1)}, u32[]{:S(2)}, u32[]{:S(2)}) collective-permute-start(bf16[64,1024]{1,0:T(8,128)(2,1)S(1)} %get-tuple-element.104), channel_id=1, source_target_pairs={{0,4},{1,5},{2,6},{3,7},{4,8},{5,9},{6,10},{7,11},{8,12},{9,13},{1... | collective-permute-start | bytes 393224 | tf_op jit(solution)/shard_map/ppermute | solution.py:26
  156.0 9.6 %collective-permute-start.46 = (bf16[64,1024]{1,0:T(8,128)(2,1)S(1)}, bf16[64,1024]{1,0:T(8,128)(2,1)S(1)}, u32[]{:S(2)}, u32[]{:S(2)}) collective-permute-start(bf16[64,1024]{1,0:T(8,128)(2,1)S(1)} %get-tuple-element.105), channel_id=1, source_target_pairs={{0,12},{1,13},{2,14},{3,15},{4,0},{5,1},{6,2},{7,3},{8,4},{9,5},{1... | collective-permute-start | bytes 393224 | tf_op jit(solution)/shard_map/ppermute | solution.py:26
  (40 other events, 306.4 us)
